TPU v7x, 32 devices: a whole 2x2x4 slice. The times are simulated.
32 devices in a mesh: rows: 8 (over y, x, core), cols: 4 (over z).
Axes of the slice: x: 2, y: 2, z: 4, core: 2. Of those that a mesh axis runs over, the one named last changes fastest.
Arguments:
- features: bfloat16 [5120, 1152], P('rows', 'cols'), may hold values from -6 to 6
- weight: bfloat16 [1152, 1152], replicated, may hold values from -0.1875 to 0.1875
- bias: float32 [1152], P('cols'), may hold values from -3 to 3
- tile_values: bfloat16 [40, 48, 128, 128], P('rows'), may hold values from -0.078125 to 0.078125
- tile_coords: int32 [40, 48], P('rows'), may hold values from 0 to 39, as said below
- tile_counts: int32 [40], P('rows'), may hold values from 1 to 48, as said below
- cotangent: bfloat16 [5120, 1152], P('rows', 'cols'), may hold values from -6 to 6
Outputs:
- activations: bfloat16 [5120, 1152], P('rows', 'cols')
- input_grad: bfloat16 [5120, 1152], P('rows', 'cols')
- weight_grad: float32 [1152, 1152], P('rows', 'cols')
Inputs may be any that keep to these rules, and one draw needn't show every extreme that they name: `tile_counts`: each row block has between 1 and 48 live slots, and some row block has exactly 48; slots at or beyond the count are ignored. `tile_coords`: source row block of each tile slot; a block may appear in several slots.
All inputs are finite; a program needn't handle non-finite values.
Results may differ from a plain program's by a relative error of at most 0.006.
Values may be sent and summed in bfloat16 or wider, within the bound.
No kernel may reach another device: no remote copies, remote signals or barrier semaphores. Data moves between devices by JAX's collectives and lax.ppermute only.
A program may use at most 128 MiB of HBM per device.

v0:
```python
import math

import jax
import jax.numpy as jnp
from jax import lax
from jax.sharding import PartitionSpec as P


def silu_slope(v):
    s = jax.nn.sigmoid(v)
    return s * (1.0 + v * (1.0 - s))


def local(features, weight, bias, tile_values, tile_coords, tile_counts, cotangent):
    rows_dev, col_width = features.shape
    block_count, slots, tile, unused_side = tile_values.shape
    col_start = lax.axis_index("cols") * col_width
    blocks_all = lax.axis_size("rows") * block_count
    x_full = lax.all_gather(features, "cols", axis=1, tiled=True)
    w_cols = lax.dynamic_slice_in_dim(weight, col_start, col_width, 1)
    hidden = jnp.dot(x_full, w_cols, preferred_element_type=jnp.float32).astype(jnp.bfloat16)
    live = jnp.arange(slots, dtype=jnp.int32)[None, :] < tile_counts[:, None]
    index = jnp.where(live, tile_coords, blocks_all).reshape(-1)
    all_hidden = lax.all_gather(hidden, "rows", axis=0, tiled=True).reshape(
        blocks_all, tile, col_width
    )
    panels = all_hidden.at[index].get(mode="fill", fill_value=0)
    panels = panels.reshape(block_count, slots, tile, col_width)
    aggregated = jnp.einsum(
        "bkij,bkjf->bif", tile_values, panels, preferred_element_type=jnp.float32
    )
    pre = aggregated.reshape(rows_dev, col_width) + bias[None, :]
    activations = jax.nn.silu(pre).astype(jnp.bfloat16)
    grad_pre = (cotangent.astype(jnp.float32) * silu_slope(pre)).astype(jnp.bfloat16)
    contrib = jnp.einsum(
        "bkij,bif->bkjf",
        tile_values,
        grad_pre.reshape(block_count, tile, col_width),
        preferred_element_type=jnp.float32,
    )
    contrib = contrib.reshape(-1, tile, col_width)
    buffer = (
        jnp.zeros((blocks_all, tile, col_width), jnp.float32).at[index].add(contrib, mode="drop")
    )
    buffer = buffer.reshape(blocks_all * tile, col_width)
    grad_hidden = lax.psum_scatter(buffer, "rows", scatter_dimension=0, tiled=True).astype(
        jnp.bfloat16
    )
    w_rows = lax.dynamic_slice_in_dim(weight, col_start, col_width, 0)
    input_grad = lax.dot_general(
        lax.all_gather(grad_hidden, "cols", axis=1, tiled=True),
        w_rows,
        (((1,), (1,)), ((), ())),
        preferred_element_type=jnp.float32,
    ).astype(jnp.bfloat16)
    scale_factor = 1.0 / math.sqrt(rows_dev * lax.axis_size("rows"))
    weight_part = (
        lax.dot_general(
            x_full, grad_hidden, (((0,), (0,)), ((), ())), preferred_element_type=jnp.float32
        )
        * scale_factor
    )
    weight_grad = lax.psum_scatter(weight_part, "rows", scatter_dimension=0, tiled=True)
    return (activations, input_grad, weight_grad)


def solution(mesh):
    return jax.shard_map(
        local,
        mesh=mesh,
        in_specs=(
            P("rows", "cols"),
            P(),
            P("cols"),
            P("rows", None, None, None),
            P("rows", None),
            P("rows"),
            P("rows", "cols"),
        ),
        out_specs=(P("rows", "cols"), P("rows", "cols"), P("rows", "cols")),
        check_vma=False,
    )
```

profile of v0, /device:TPU:0, one launch (start us, length us, event | category | flops | bytes accessed | tf_op | source)
XLA Modules:
  0.0 360.9 jit_solution(8286425955652804677)
XLA Ops:
  7.2 0.0 copy-start
  7.2 0.0 copy-start.1
  7.2 0.0 all-gather.4.cloned.1.call-start
  7.2 0.7 all-gather.4.cloned.1.call-update
  7.9 0.0 all-gather.6.cloned.1.call-start
  8.0 39.8 %all-gather.4.cloned.1.call-done = bf16[640,1152]{0,1:T(8,128)(2,1)} async-done(((bf16[640,288]{0,1:T(8,128)(2,1)}), bf16[640,1152]{0,1:T(8,128)(2,1)}) %all-gather.4.cloned.1.call-update) | async-done | bytes 1474576 | tf_op jit(solution)/shard_map/all_gather | solution.py:19
  47.8 0.0 copy-done
  47.8 3.2 fusion.8
  51.0 0.0 all-gather.6.cloned.1.call-update
  51.0 0.0 reduce-scatter.5.cloned.1.call-start
  51.1 0.8 compare_and_fusion
  51.8 0.1 reshape.64
  51.9 0.0 copy-done.1
  51.9 1.0 copy.22
  52.9 28.6 %all-gather.6.cloned.1.call-done = bf16[5120,288]{0,1:T(8,128)(2,1)} async-done(((bf16[640,288]{0,1:T(8,128)(2,1)}), bf16[5120,288]{0,1:T(8,128)(2,1)}) %all-gather.6.cloned.1.call-update) | async-done | bytes 2949136 | tf_op jit(solution)/shard_map/all_gather | solution.py:24
  81.5 3.9 %copy_bitcast_fusion.1 = bf16[40,128,288]{1,2,0:T(8,128)(2,1)} fusion(bf16[5120,288]{0,1:T(8,128)(2,1)} %all-gather.6.cloned.1.call-done), kind=kLoop, calls=%fused_computation.7 | loop fusion | bytes 5898240 | tf_op jit(solution)/shard_map/reshape | solution.py:24
  85.4 11.8 %gather_fusion = bf16[240,128,288]{1,2,0:T(8,128)(2,1)} fusion(bf16[40,128,288]{1,2,0:T(8,128)(2,1)} %copy_bitcast_fusion.1, s32[1024]{0:T(1024)S(1)} %pad_clamp_fusion), kind=kCustom, calls=%fused_computation | custom fusion | bytes 35390400 | tf_op jit(solution)/shard_map/gather | solution.py:27
  97.2 0.0 copy-start.2
  97.2 10.8 %fusion.5 = f32[5,128,288]{1,2,0:T(8,128)S(1)} fusion(bf16[5,48,128,128]{3,2,1,0:T(8,128)(2,1)} %param.10, bf16[5,48,128,288]{2,3,1,0:T(8,128)(2,1)} %bitcast.44, pred[5,48]{1,0:T(8,128)(4,1)S(1)} %get-tuple-element.12), kind=kOutput, calls=%fused_computation.10 | convolution fusion | flops 2273771520 | bytes 26296560 | tf_op jit(solution)/shard_map/bkij,bkjf->bif/dot_general | solution.py:29
  108.1 1.3 copy.21
  109.3 0.0 copy-done.2
  109.4 1.8 multiply_convert_fusion
  111.2 19.7 %fusion.16 = f32[5,288,48,128]{3,1,2,0:T(8,128)} fusion(bf16[5,128,288,1]{2,1,3,0:T(8,128)(2,1)S(1)} %bitcast.45, bf16[5,48,128,128]{3,2,1,0:T(8,128)(2,1)} %param.10), kind=kOutput, calls=%fused_computation.29 | convolution fusion | flops 2264924160 | bytes 43622400 | tf_op jit(solution)/shard_map/bkij,bif->bkjf/dot_general | solution.py:35
  130.9 3.2 broadcast_in_dim.21
  134.0 74.9 %scatter_fusion = f32[40,128,288]{1,2,0:T(8,128)} fusion(f32[40,128,288]{1,2,0:T(8,128)} %broadcast_in_dim.21, s32[240]{0:T(256)S(1)} %bitcast.47, f32[240,128,288]{1,2,0:T(8,128)} %bitcast.43), kind=kCustom, calls=%fused_computation.1 | custom fusion | flops 8847360 | bytes 106169280 | tf_op jit(solution)/shard_map/scatter-add | solution.py:43
  208.9 6.0 %copy_bitcast_fusion = f32[5120,288]{0,1:T(8,128)} fusion(f32[40,128,288]{1,2,0:T(8,128)} %scatter_fusion), kind=kLoop, calls=%fused_computation.6 | loop fusion | bytes 11796480 | tf_op jit(solution)/shard_map/reshape | solution.py:45
  214.9 0.0 reduce-scatter.5.cloned.1.call-update
  214.9 0.0 all-gather.8.cloned.1.call-start
  214.9 59.8 %reduce-scatter.5.cloned.1.call-done = f32[640,288]{0,1:T(8,128)} async-done(((f32[5120,288]{0,1:T(8,128)}), f32[640,288]{0,1:T(8,128)}) %reduce-scatter.5.cloned.1.call-update) | async-done | bytes 737296 | tf_op jit(solution)/shard_map/reduce_scatter | solution.py:46
  274.8 1.9 convert_element_type.26
  276.7 0.0 all-gather.8.cloned.1.call-update
  276.7 0.0 reduce-scatter.7.cloned.1.call-start
  276.8 3.3 fusion.4
  280.1 3.1 copy.31
  283.1 0.0 reduce-scatter.7.cloned.1.call-update
  283.2 0.9 copy.25
  284.1 28.2 %all-gather.8.cloned.1.call-done = bf16[640,1152]{0,1:T(8,128)(2,1)} async-done(((bf16[640,288]{0,1:T(8,128)(2,1)}), bf16[640,1152]{0,1:T(8,128)(2,1)}) %all-gather.8.cloned.1.call-update) | async-done | bytes 1474576 | tf_op jit(solution)/shard_map/all_gather | solution.py:51
  312.3 2.8 convolution_convert_fusion
  315.2 39.2 %reduce-scatter.7.cloned.1.call-done = f32[144,288]{1,0:T(8,128)} async-done(((f32[1152,288]{1,0:T(8,128)}), f32[144,288]{1,0:T(8,128)}) %reduce-scatter.7.cloned.1.call-update) | async-done | bytes 165904
  (2 shorter events, 0.0 us)
Async XLA Ops:
  7.2 40.6 %copy-start = (bf16[1152,1152]{1,0:T(8,128)(2,1)S(1)}, bf16[1152,1152]{1,0:T(8,128)(2,1)}, u32[]{:S(2)}) copy-start(bf16[1152,1152]{1,0:T(8,128)(2,1)} %param.8) | copy-start | bytes 7962628
  7.2 44.7 %copy-start.1 = (bf16[640,288]{0,1:T(8,128)(2,1)S(1)}, bf16[640,288]{0,1:T(8,128)(2,1)}, u32[]{:S(2)}) copy-start(bf16[640,288]{0,1:T(8,128)(2,1)} %param.13) | copy-start | bytes 1105924
  7.2 40.6 %all-gather.4.cloned.1.call-start = ((), (), s32[]{:S(2)}) async-start(), calls=%async_computation.2 | async-start | bytes 1843200 | tf_op jit(solution)/shard_map/all_gather | solution.py:19
  7.9 73.6 %all-gather.6.cloned.1.call-start = ((), (), s32[]{:S(2)}) async-start(), calls=%async_computation.3 | async-start | bytes 3317760 | tf_op jit(solution)/shard_map/all_gather | solution.py:24
  51.0 223.8 %reduce-scatter.5.cloned.1.call-start = ((), (), s32[]{:S(2)}) async-start(), calls=%async_computation.4 | async-start | bytes 6635520 | tf_op jit(solution)/shard_map/reduce_scatter | solution.py:46
  97.2 12.1 %copy-start.2 = (f32[288]{0:T(512)S(1)}, f32[288]{0:T(512)}, u32[]{:S(2)}) copy-start(f32[288]{0:T(512)} %param.9) | copy-start | bytes 3460
  214.9 97.4 %all-gather.8.cloned.1.call-start = ((), (), s32[]{:S(2)}) async-start(), calls=%async_computation.5 | async-start | bytes 1843200 | tf_op jit(solution)/shard_map/all_gather | solution.py:51
  276.7 77.7 %reduce-scatter.7.cloned.1.call-start = ((), (), s32[]{:S(2)}) async-start(), calls=%async_computation.6 | async-start | bytes 1990656
Sparse Core Ops, SparseCore 0:
  9.6 38.1 all-gather.3
  51.1 30.3 all-gather.5
  215.0 59.7 reduce-scatter.4
  276.8 35.4 all-gather.7
  316.1 38.2 reduce-scatter.6
where the time goes:
time: 362 us; the launch traced here: 361 us
  waiting for transfers between devices  197 us (54%)
  other arithmetic  79.4 us (22%)
  matrix products  39.8 us (11%)
  local copies, waits for them, and re-layouts  31.2 us (9%)
  between operations  13.8 us (4%)
    scatter-add x1, other arithmetic, local(): jnp.zeros((blocks_all, tile, col_width), jnp.float32).at[index]  74.9 us
    reduce_scatter x1, waiting for transfers between devices, local(): lax.psum_scatter(buffer, 'rows', scatter_dimension=0, tiled=True)  59.8 us
    unnamed x6, waiting for transfers between devices  40 us
    all_gather x1, waiting for transfers between devices, local(): x_full = lax.all_gather(features, 'cols', axis=1, tiled=True)  39.8 us
    all_gather x1, waiting for transfers between devices, local(): lax.all_gather(hidden, 'rows', axis=0, tiled=True)  28.6 us
    all_gather x1, waiting for transfers between devices, local(): lax.all_gather(grad_hidden, 'cols', axis=1, tiled=True)  28.2 us
    dot_general x1, matrix products, local(): jnp.einsum('bkij,bif->bkjf', tile_values, grad_pre.reshape(block_count, t...  19.7 us
    gather x1, local copies, waits for them, and re-layouts, local(): panels = all_hidden.at[index].get(mode='fill', fill_value=0)  11.8 us
  transfers between devices with their start and end apart: 5, of which 5 were waited for; matrix products, arithmetic and copies ran while one was open for 3% of the time, Pallas kernels for 0%

commit v1 on v0

v1 whole, which is shorter than its diff:
```python
import functools
import math

import jax
import jax.numpy as jnp
from jax import lax
from jax.experimental import pallas as pl
from jax.experimental.pallas import tpu as pltpu
from jax.sharding import PartitionSpec as P

F32 = jnp.float32
BF16 = jnp.bfloat16


def largest_divisor(number, limit):
    return max(d for d in range(1, limit + 1) if number % d == 0)


def tile_kernel(
    block_count,
    slots,
    tile,
    group,
    shard_order,
    coords_ref,
    counts_ref,
    me_ref,
    bias_ref,
    cotangent_ref,
    tiles_ref,
    *rest,
):
    shards = len(shard_order)
    hidden_refs = rest[:shards]
    act_ref, part_ref, tiles, hidden, partial, tile_sems, hidden_sems = rest[shards:]
    groups = slots // group
    me = me_ref[0]

    def tile_copy(i, q):
        span = pl.ds(q * group, group)
        return pltpu.make_async_copy(
            tiles_ref.at[i, span], tiles.at[i, span], tile_sems.at[i, q]
        )

    def hidden_copy(s, b):
        owner = me ^ shard_order[s]
        return pltpu.make_async_copy(
            hidden_refs[s].at[:, pl.ds(b * tile, tile)],
            hidden.at[owner * block_count + b],
            hidden_sems.at[s, b],
        )

    for s in range(shards):
        for b in range(block_count):
            hidden_copy(s, b).start()
    for i in range(block_count):
        for q in range(groups):

            @pl.when(q * group < counts_ref[i])
            def _():
                tile_copy(i, q).start()

    partial[...] = jnp.zeros_like(partial)
    for s in range(shards):
        for b in range(block_count):
            hidden_copy(s, b).wait()

    def pair(i, p):
        first = 2 * p
        second = jnp.minimum(first + 1, slots - 1)
        left = tiles[i, first]
        right = tiles[i, second]
        right = jnp.where(first + 1 < counts_ref[i], right, jnp.zeros_like(right))
        both = jnp.concatenate([left, right], axis=1)
        return both, coords_ref[i * slots + first], coords_ref[i * slots + second]

    for i in range(block_count):
        for q in range(groups):

            @pl.when(q * group < counts_ref[i])
            def _():
                tile_copy(i, q).wait()

        pairs = (counts_ref[i] + 1) // 2
        lanes = pl.ds(i * tile, tile)

        def forward(p, total):
            both, c0, c1 = pair(i, p)
            panel = jnp.concatenate([hidden[c0], hidden[c1]], axis=1)
            return total + lax.dot_general(
                panel, both, (((1,), (1,)), ((), ())), preferred_element_type=F32
            )

        width = act_ref.shape[0]
        total = lax.fori_loop(0, pairs, forward, jnp.zeros((width, tile), F32))
        pre = total + bias_ref[...]
        s = jax.nn.sigmoid(pre)
        act_ref[:, lanes] = (pre * s).astype(BF16)
        slope = s * (1.0 + pre * (1.0 - s))
        grad = (cotangent_ref[:, lanes].astype(F32) * slope).astype(BF16)

        def backward(p, carry):
            both, c0, c1 = pair(i, p)
            out = jnp.dot(grad, both, preferred_element_type=F32)
            partial[c0] += out[:, :tile]
            partial[c1] += out[:, tile:]
            return carry

        lax.fori_loop(0, pairs, backward, 0)

    for s in range(shards):
        owner = me ^ shard_order[s]
        for b in range(block_count):
            part_ref[s, :, b * tile : (b + 1) * tile] = partial[owner * block_count + b].astype(BF16)


def tile_products(shard_order, hidden, coords, counts, me, bias, cotangent, tiles):
    block_count, slots, tile, unused_side = tiles.shape
    width, rows_dev = hidden[0].shape
    shards = len(shard_order)
    group = largest_divisor(slots, 8)
    smem = pl.BlockSpec(memory_space=pltpu.SMEM)
    vmem = pl.BlockSpec(memory_space=pltpu.VMEM)
    hbm = pl.BlockSpec(memory_space=pl.ANY)
    flops = 4 * block_count * slots * tile * tile * width
    return pl.pallas_call(
        functools.partial(tile_kernel, block_count, slots, tile, group, shard_order),
        out_shape=(
            jax.ShapeDtypeStruct((width, rows_dev), BF16),
            jax.ShapeDtypeStruct((shards, width, rows_dev), BF16),
        ),
        in_specs=[smem, smem, smem, vmem, vmem, hbm] + [hbm] * shards,
        out_specs=(vmem, vmem),
        scratch_shapes=[
            pltpu.VMEM(tiles.shape, BF16),
            pltpu.VMEM((shards * block_count, width, tile), BF16),
            pltpu.VMEM((shards * block_count, width, tile), F32),
            pltpu.SemaphoreType.DMA((block_count, slots // group)),
            pltpu.SemaphoreType.DMA((shards, block_count)),
        ],
        compiler_params=pltpu.CompilerParams(vmem_limit_bytes=48 * 1024 * 1024),
        cost_estimate=pl.CostEstimate(
            flops=flops, bytes_accessed=2 * tiles.size, transcendentals=width * rows_dev
        ),
    )(coords.reshape(-1), counts, me.reshape(1), bias[:, None], cotangent, tiles, *hidden)


def contract_first(a, b):
    return lax.dot_general(a, b, (((0,), (0,)), ((), ())), preferred_element_type=F32)


def local(features, weight, bias, tile_values, tile_coords, tile_counts, cotangent):
    rows_dev, col_width = features.shape
    n_rows = lax.axis_size("rows")
    me = lax.axis_index("rows")
    col_start = lax.axis_index("cols") * col_width
    x_full = lax.all_gather(features.T, "cols", axis=0, tiled=True)
    w_cols = lax.dynamic_slice_in_dim(weight, col_start, col_width, 1)
    hidden = contract_first(w_cols, x_full).astype(BF16)
    all_hidden = lax.all_gather(hidden, "rows", axis=0)
    order = tuple(range(n_rows))
    zero = jnp.zeros((), jnp.int32)
    act, part = tile_products(
        order,
        [all_hidden[s] for s in order],
        tile_coords,
        tile_counts,
        zero,
        bias,
        cotangent.T,
        tile_values,
    )
    grad_hidden = lax.psum_scatter(part, "rows", scatter_dimension=0, tiled=False)
    w_rows = lax.dynamic_slice_in_dim(weight, col_start, col_width, 0)
    grad_full = lax.all_gather(grad_hidden, "cols", axis=0, tiled=True)
    input_grad = jnp.dot(w_rows, grad_full, preferred_element_type=F32).astype(BF16)
    scale_factor = 1.0 / math.sqrt(rows_dev * n_rows)
    weight_part = lax.dot_general(
        x_full, grad_hidden, (((1,), (1,)), ((), ())), preferred_element_type=F32
    )
    weight_grad = lax.psum_scatter(
        weight_part * scale_factor, "rows", scatter_dimension=0, tiled=True
    )
    return (act.T, input_grad.T, weight_grad)


def solution(mesh):
    return jax.shard_map(
        local,
        mesh=mesh,
        in_specs=(
            P("rows", "cols"),
            P(),
            P("cols"),
            P("rows", None, None, None),
            P("rows", None),
            P("rows"),
            P("rows", "cols"),
        ),
        out_specs=(P("rows", "cols"), P("rows", "cols"), P("rows", "cols")),
        check_vma=False,
    )
```

time: 362 us -> 251 us (0.69); the launches traced: 361 us -> 246 us
  other arithmetic: 79.4 us -> 0 us
  matrix products: 39.8 us -> 9.33 us
  local copies, waits for them, and re-layouts: 31.2 us -> 5.31 us
  Pallas kernels: 0 us -> 24.6 us
  waiting for transfers between devices: 197 us -> 193 us
    scatter-add x1 -> x0, other arithmetic: 74.9 us -> none  [local(): jnp.zeros((blocks_all, tile, col_width), jnp.float32).at[index]]
    dot_general x5 -> x3, matrix products: 39.8 us -> 9.33 us  [the longest x1 3.33 us: local(): lax.dot_general(x_full, grad_hidden, (((1,), (1,)), ((), ())), preferred_...]
    pallas_call x0 -> x1, Pallas kernels: none -> 24.6 us  [tile_products(): pl.pallas_call(functools.partial(tile_kernel, block_count, slots, tile, g...]
    gather x1 -> x0, local copies, waits for them, and re-layouts: 11.8 us -> none  [local(): panels = all_hidden.at[index].get(mode='fill', fill_value=0)]
    reshape x3 -> x1, local copies, waits for them, and re-layouts: 9.94 us -> 0.08 us  [tile_products(): coords.reshape(-1)]
    reduce_scatter x1, waiting for transfers between devices: 59.8 us -> 52.3 us  [local(): lax.psum_scatter(part, 'rows', scatter_dimension=0, tiled=False)]
    all_gather x3, waiting for transfers between devices: 96.7 us -> 100 us  [the longest x1 39.8 us: local(): x_full = lax.all_gather(features.T, 'cols', axis=0, tiled=True)]
    convert_element_type x2 -> x0, other arithmetic: 3.72 us -> none  [the longest x1 1.89 us: local(): lax.psum_scatter(buffer, 'rows', scatter_dimension=0, tiled=True)]
  transfers between devices with their start and end apart: 5 -> 5, of which waited for: 5 -> 5; matrix products, arithmetic and copies ran while one was open for 3% -> 4% of each run, Pallas kernels for 0% -> 0%
where the time goes in v1:
time: 251 us; the launch traced here: 246 us
  waiting for transfers between devices  193 us (77%)
  Pallas kernels  24.6 us (10%)
  between operations  13.9 us (6%)
  matrix products  9.33 us (4%)
  local copies, waits for them, and re-layouts  5.31 us (2%)
    reduce_scatter x1, waiting for transfers between devices, local(): lax.psum_scatter(part, 'rows', scatter_dimension=0, tiled=False)  52.3 us
    unnamed x6, waiting for transfers between devices  40 us
    all_gather x1, waiting for transfers between devices, local(): x_full = lax.all_gather(features.T, 'cols', axis=0, tiled=True)  39.8 us
    all_gather x1, waiting for transfers between devices, local(): grad_full = lax.all_gather(grad_hidden, 'cols', axis=0, tiled=True)  30.4 us
    all_gather x1, waiting for transfers between devices, local(): all_hidden = lax.all_gather(hidden, 'rows', axis=0)  30.3 us
    pallas_call x1, Pallas kernels, tile_products(): pl.pallas_call(functools.partial(tile_kernel, block_count, slots, tile, g...  24.6 us
  transfers between devices with their start and end apart: 5, of which 5 were waited for; matrix products, arithmetic and copies ran while one was open for 4% of the time, Pallas kernels for 0%

profile of v1, /device:TPU:0, one launch (start us, length us, event | category | flops | bytes accessed | tf_op | source)
XLA Modules:
  0.0 246.1 jit_solution(16891275811880775178)
XLA Ops:
  7.2 0.0 copy-start
  7.2 0.0 all-gather.6.cloned.1.call-start
  7.2 0.7 all-gather.6.cloned.1.call-update
  7.9 0.0 all-gather.8.cloned.1.call-start
  8.0 0.0 copy-start.3
  8.0 0.0 copy-start.4
  8.0 39.8 %all-gather.6.cloned.1.call-done = bf16[1152,640]{1,0:T(8,128)(2,1)} async-done(((bf16[288,640]{1,0:T(8,128)(2,1)}), bf16[1152,640]{1,0:T(8,128)(2,1)}) %all-gather.6.cloned.1.call-update) | async-done | bytes 1474576 | tf_op jit(solution)/shard_map/all_gather | solution.py:157
  47.8 0.0 copy-done
  47.8 3.2 %convolution_convert_fusion = bf16[288,640]{1,0:T(8,128)(2,1)} fusion(bf16[1152,640]{1,0:T(8,128)(2,1)} %all-gather.6.cloned.1.call-done, bf16[1152,1152]{1,0:T(8,128)(2,1)S(1)} %copy-done, s32[]{:T(128)S(6)} %select_n.4), kind=kOutput, calls=%fused_computation.5 | convolution fusion | flops 424857600 | bytes 2727940 | tf_op jit(solution)/shard_map/dot_general | solution.py:149
  51.0 0.0 all-gather.8.cloned.1.call-update
  51.0 0.0 reduce-scatter.5.cloned.1.call-start
  51.0 0.0 copy-done.3
  51.1 0.1 reshape.9.coords_ref
  51.1 0.0 copy-done.4
  51.1 0.1 broadcast_in_dim.4.bias_ref
  51.2 0.0 copy-start.1
  51.2 0.0 copy-start.2
  51.3 30.3 %all-gather.8.cloned.1.call-done = bf16[2304,640]{1,0:T(8,128)(2,1)} async-done(((bf16[288,640]{1,0:T(8,128)(2,1)}), bf16[2304,640]{1,0:T(8,128)(2,1)}) %all-gather.8.cloned.1.call-update) | async-done | bytes 2949136 | tf_op jit(solution)/shard_map/all_gather | solution.py:160
  81.5 2.0 fusion.11
  83.5 0.0 copy-done.1
  83.6 0.0 copy-done.2
  83.6 24.6 %shard_map.94 = (bf16[288,640]{1,0:T(8,128)(2,1)}, bf16[8,288,640]{2,1,0:T(8,128)(2,1)}) custom-call(s32[240]{0:T(256)S(1)} %reshape.9.coords_ref, s32[5]{0:T(128)S(1)} %copy-done.2, s32[1]{0:T(128)} %constant.6.clone.1.me_ref, f32[288,1]{1,0:T(8,128)S(1)} %broadcast_in_dim.4.bias_ref, bf16[288,640]{1,0:T(8,128)(2,1)S(1)} %bitcast.16, ...), custom_call_target="tpu_custom_call" | custom-call | flops 4529848320 | bytes 7864320 | tf_op jit(solution)/shard_map/pallas_call | solution.py:126
  108.2 0.0 reduce-scatter.5.cloned.1.call-update
  108.2 0.0 all-gather.10.cloned.1.call-start
  108.2 52.3 %reduce-scatter.5.cloned.1.call-done = bf16[1,288,640]{2,1,0:T(8,128)(2,1)} async-done(((bf16[8,288,640]{2,1,0:T(8,128)(2,1)}), bf16[1,288,640]{2,1,0:T(8,128)(2,1)}) %reduce-scatter.5.cloned.1.call-update) | async-done | bytes 368656 | tf_op jit(solution)/shard_map/reduce_scatter | solution.py:173
  160.6 0.0 all-gather.10.cloned.1.call-update
  160.6 0.0 reduce-scatter.7.cloned.1.call-start
  160.7 3.3 %fusion = f32[1152,288]{0,1:T(8,128)} fusion(bf16[1152,640]{1,0:T(8,128)(2,1)} %all-gather.6.cloned.1.call-done, bf16[1,288,640]{2,1,0:T(8,128)(2,1)} %reduce-scatter.5.cloned.1.call-done), kind=kOutput, calls=%fused_computation.1 | convolution fusion | flops 425005056 | bytes 3170304 | tf_op jit(solution)/shard_map/dot_general | solution.py:178
  164.0 3.1 %copy.15 = f32[1152,288]{1,0:T(8,128)} copy(f32[1152,288]{0,1:T(8,128)} %fusion) | data formatting | bytes 2654208
  167.1 0.0 reduce-scatter.7.cloned.1.call-update
  167.1 30.4 %all-gather.10.cloned.1.call-done = bf16[1,1152,640]{2,1,0:T(8,128)(2,1)} async-done(((bf16[1,288,640]{2,1,0:T(8,128)(2,1)}), bf16[1,1152,640]{2,1,0:T(8,128)(2,1)}) %all-gather.10.cloned.1.call-update) | async-done | bytes 1474576 | tf_op jit(solution)/shard_map/all_gather | solution.py:175
  197.5 2.8 %fusion.3 = bf16[640,288]{0,1:T(8,128)(2,1)} fusion(bf16[1,1152,640]{2,1,0:T(8,128)(2,1)} %all-gather.10.cloned.1.call-done, bf16[1152,1152]{1,0:T(8,128)(2,1)S(1)} %copy-done, s32[]{:T(128)S(6)} %select_n.4), kind=kOutput, calls=%fused_computation.4 | convolution fusion | flops 424857600 | bytes 2506756 | tf_op jit(solution)/shard_map/dot_general | solution.py:176
  200.3 39.2 %reduce-scatter.7.cloned.1.call-done = f32[144,288]{1,0:T(8,128)} async-done(((f32[1152,288]{1,0:T(8,128)}), f32[144,288]{1,0:T(8,128)}) %reduce-scatter.7.cloned.1.call-update) | async-done | bytes 165904
Async XLA Ops:
  7.2 40.6 %copy-start = (bf16[1152,1152]{1,0:T(8,128)(2,1)S(1)}, bf16[1152,1152]{1,0:T(8,128)(2,1)}, u32[]{:S(2)}) copy-start(bf16[1152,1152]{1,0:T(8,128)(2,1)} %param.8) | copy-start | bytes 7962628
  7.2 40.6 %all-gather.6.cloned.1.call-start = ((), (), s32[]{:S(2)}) async-start(), calls=%async_computation.2 | async-start | bytes 1843200 | tf_op jit(solution)/shard_map/all_gather | solution.py:157
  7.9 73.6 %all-gather.8.cloned.1.call-start = ((), (), s32[]{:S(2)}) async-start(), calls=%async_computation.4 | async-start | bytes 3317760 | tf_op jit(solution)/shard_map/all_gather | solution.py:160
  8.0 43.1 %copy-start.3 = (s32[5,48]{1,0:T(8,128)S(1)}, s32[5,48]{1,0:T(8,128)}, u32[]{:S(2)}) copy-start(s32[5,48]{1,0:T(8,128)} %param.11) | copy-start | bytes 2884
  8.0 43.2 %copy-start.4 = (f32[288]{0:T(512)S(1)}, f32[288]{0:T(512)}, u32[]{:S(2)}) copy-start(f32[288]{0:T(512)} %param.9) | copy-start | bytes 3460
  51.0 109.6 %reduce-scatter.5.cloned.1.call-start = ((), (), s32[]{:S(2)}) async-start(), calls=%async_computation.3 | async-start | bytes 3317760 | tf_op jit(solution)/shard_map/reduce_scatter | solution.py:173
  51.2 32.3 %copy-start.1 = (bf16[640,288]{0,1:T(8,128)(2,1)S(1)}, bf16[640,288]{0,1:T(8,128)(2,1)}, u32[]{:S(2)}) copy-start(bf16[640,288]{0,1:T(8,128)(2,1)} %param.13) | copy-start | bytes 1105924
  51.2 32.3 %copy-start.2 = (s32[5]{0:T(128)S(1)}, s32[5]{0:T(128)}, u32[]{:S(2)}) copy-start(s32[5]{0:T(128)} %counts_ref.1) | copy-start | bytes 64
  108.2 89.3 %all-gather.10.cloned.1.call-start = ((), (), s32[]{:S(2)}) async-start(), calls=%async_computation.5 | async-start | bytes 1843200 | tf_op jit(solution)/shard_map/all_gather | solution.py:175
  160.6 79.0 %reduce-scatter.7.cloned.1.call-start = ((), (), s32[]{:S(2)}) async-start(), calls=%async_computation.6 | async-start | bytes 1990656
Sparse Core Ops, SparseCore 0:
  9.6 38.1 all-gather.5
  51.1 30.3 all-gather.7
  108.3 52.2 reduce-scatter.4
  162.0 35.4 all-gather.9
  201.3 38.2 reduce-scatter.6

commit v2 on v1

--- a/solution.py
+++ b/solution.py
@@ -10,6 +10,7 @@
 
 F32 = jnp.float32
 BF16 = jnp.bfloat16
+CHUNK = 16
 
 
 def largest_divisor(number, limit):
@@ -32,7 +33,7 @@
 ):
     shards = len(shard_order)
     hidden_refs = rest[:shards]
-    act_ref, part_ref, tiles, hidden, partial, tile_sems, hidden_sems = rest[shards:]
+    act_ref, keep_ref, send_ref, tiles, hidden, partial, tile_sems, hidden_sems = rest[shards:]
     groups = slots // group
     me = me_ref[0]
 
@@ -65,14 +66,18 @@
         for b in range(block_count):
             hidden_copy(s, b).wait()
 
-    def pair(i, p):
-        first = 2 * p
-        second = jnp.minimum(first + 1, slots - 1)
-        left = tiles[i, first]
-        right = tiles[i, second]
-        right = jnp.where(first + 1 < counts_ref[i], right, jnp.zeros_like(right))
-        both = jnp.concatenate([left, right], axis=1)
-        return both, coords_ref[i * slots + first], coords_ref[i * slots + second]
+    chunk = largest_divisor(slots, CHUNK)
+
+    def several(i, p):
+        parts, places = [], []
+        for t in range(chunk):
+            k = p * chunk + t
+            value = tiles[i, k]
+            if t:
+                value = jnp.where(k < counts_ref[i], value, jnp.zeros_like(value))
+            parts.append(value)
+            places.append(coords_ref[i * slots + k])
+        return jnp.concatenate(parts, axis=1), places
 
     for i in range(block_count):
         for q in range(groups):
@@ -81,18 +86,18 @@
             def _():
                 tile_copy(i, q).wait()
 
-        pairs = (counts_ref[i] + 1) // 2
+        steps = (counts_ref[i] + (chunk - 1)) // chunk
         lanes = pl.ds(i * tile, tile)
 
         def forward(p, total):
-            both, c0, c1 = pair(i, p)
-            panel = jnp.concatenate([hidden[c0], hidden[c1]], axis=1)
+            values, places = several(i, p)
+            panel = jnp.concatenate([hidden[c] for c in places], axis=1)
             return total + lax.dot_general(
-                panel, both, (((1,), (1,)), ((), ())), preferred_element_type=F32
+                panel, values, (((1,), (1,)), ((), ())), preferred_element_type=F32
             )
 
         width = act_ref.shape[0]
-        total = lax.fori_loop(0, pairs, forward, jnp.zeros((width, tile), F32))
+        total = lax.fori_loop(0, steps, forward, jnp.zeros((width, tile), F32))
         pre = total + bias_ref[...]
         s = jax.nn.sigmoid(pre)
         act_ref[:, lanes] = (pre * s).astype(BF16)
@@ -100,18 +105,21 @@
         grad = (cotangent_ref[:, lanes].astype(F32) * slope).astype(BF16)
 
         def backward(p, carry):
-            both, c0, c1 = pair(i, p)
-            out = jnp.dot(grad, both, preferred_element_type=F32)
-            partial[c0] += out[:, :tile]
-            partial[c1] += out[:, tile:]
+            values, places = several(i, p)
+            out = jnp.dot(grad, values, preferred_element_type=F32)
+            for t, c in enumerate(places):
+                partial[c] += out[:, t * tile : (t + 1) * tile]
             return carry
 
-        lax.fori_loop(0, pairs, backward, 0)
+        lax.fori_loop(0, steps, backward, 0)
 
     for s in range(shards):
         owner = me ^ shard_order[s]
+        half = shards // 2
+        out_ref = keep_ref.at[s] if s < half else send_ref.at[s - half]
         for b in range(block_count):
-            part_ref[s, :, b * tile : (b + 1) * tile] = partial[owner * block_count + b].astype(BF16)
+            value = partial[owner * block_count + b].astype(BF16)
+            out_ref[:, b * tile : (b + 1) * tile] = value
 
 
 def tile_products(shard_order, hidden, coords, counts, me, bias, cotangent, tiles):
@@ -127,10 +135,11 @@
         functools.partial(tile_kernel, block_count, slots, tile, group, shard_order),
         out_shape=(
             jax.ShapeDtypeStruct((width, rows_dev), BF16),
-            jax.ShapeDtypeStruct((shards, width, rows_dev), BF16),
+            jax.ShapeDtypeStruct((shards // 2, width, rows_dev), BF16),
+            jax.ShapeDtypeStruct((shards // 2, width, rows_dev), BF16),
         ),
         in_specs=[smem, smem, smem, vmem, vmem, hbm] + [hbm] * shards,
-        out_specs=(vmem, vmem),
+        out_specs=(vmem, vmem, vmem),
         scratch_shapes=[
             pltpu.VMEM(tiles.shape, BF16),
             pltpu.VMEM((shards * block_count, width, tile), BF16),
@@ -145,41 +154,151 @@
     )(coords.reshape(-1), counts, me.reshape(1), bias[:, None], cotangent, tiles, *hidden)
 
 
+def sum_dots_kernel(dims, lefts, *refs):
+    total = None
+    for left, right in zip(refs[:lefts], refs[lefts:-1]):
+        term = lax.dot_general(left[...], right[...], (dims, ((), ())), preferred_element_type=F32)
+        total = term if total is None else total + term
+    refs[-1][...] = total.astype(refs[-1].dtype)
+
+
+def sum_dots(lefts, rights, dims):
+    (left_dim,), (right_dim,) = dims
+    out = (lefts[0].shape[1 - left_dim], rights[0].shape[1 - right_dim])
+    vmem = pl.BlockSpec(memory_space=pltpu.VMEM)
+    depth = sum(v.shape[left_dim] for v in lefts)
+    return pl.pallas_call(
+        functools.partial(sum_dots_kernel, dims, len(lefts)),
+        out_shape=jax.ShapeDtypeStruct(out, BF16),
+        in_specs=[vmem] * (2 * len(lefts)),
+        out_specs=vmem,
+        compiler_params=pltpu.CompilerParams(vmem_limit_bytes=48 * 1024 * 1024),
+        cost_estimate=pl.CostEstimate(
+            flops=2 * out[0] * out[1] * depth,
+            bytes_accessed=2 * depth * (out[0] + out[1]),
+            transcendentals=0,
+        ),
+    )(*lefts, *rights)
+
+
+def weight_part_kernel(scale, order, col_ref, grad_ref, *refs):
+    grad = grad_ref[...]
+    out_ref = refs[-1]
+    for k, x_ref in zip(order, refs[:-1]):
+        width = x_ref.shape[0]
+        start = pl.multiple_of((col_ref[0] ^ k) * width, 16)
+        part = lax.dot_general(
+            x_ref[...], grad, (((1,), (1,)), ((), ())), preferred_element_type=F32
+        )
+        out_ref[pl.ds(start, width), :] = part * scale
+
+
+def weight_part(scale, order, col, grad, x_parts):
+    width = grad.shape[0]
+    vmem = pl.BlockSpec(memory_space=pltpu.VMEM)
+    smem = pl.BlockSpec(memory_space=pltpu.SMEM)
+    out = (width * len(x_parts), width)
+    return pl.pallas_call(
+        functools.partial(weight_part_kernel, scale, order),
+        out_shape=jax.ShapeDtypeStruct(out, F32),
+        in_specs=[smem, vmem] + [vmem] * len(x_parts),
+        out_specs=vmem,
+        compiler_params=pltpu.CompilerParams(vmem_limit_bytes=48 * 1024 * 1024),
+        cost_estimate=pl.CostEstimate(
+            flops=2 * out[0] * out[1] * grad.shape[1],
+            bytes_accessed=2 * grad.size * (len(x_parts) + 1) + 4 * out[0] * out[1],
+            transcendentals=0,
+        ),
+    )(col.reshape(1), grad, *x_parts)
+
+
+def swap(value, axis, k):
+    return lax.ppermute(value, axis, [(i, i ^ k) for i in range(lax.axis_size(axis))])
+
+
+def local(features, weight, bias, tile_values, tile_coords, tile_counts, cotangent):
+    rows_dev, width = features.shape
+    n_rows, n_cols = lax.axis_size("rows"), lax.axis_size("cols")
+    me, col = lax.axis_index("rows"), lax.axis_index("cols")
+    if not all(n & (n - 1) == 0 for n in (n_rows, n_cols)):
+        return local_any(features, weight, bias, tile_values, tile_coords, tile_counts, cotangent)
+    cols_order = tuple(range(n_cols))
+    chips = tuple(range(0, n_rows, 2))
+
+    x = features.T
+    x_parts = [x] + [swap(x, "cols", k) for k in cols_order[1:]]
+    weight_down = [
+        lax.dynamic_slice(weight, ((col ^ k) * width, col * width), (width, width))
+        for k in cols_order
+    ]
+    weight_across = [
+        lax.dynamic_slice(weight, (col * width, (col ^ k) * width), (width, width))
+        for k in cols_order
+    ]
+    hidden = sum_dots(weight_down, x_parts, ((0,), (0,)))
+
+    own = [hidden] + [swap(hidden, "rows", k) for k in chips[1:]]
+    other = [swap(h, "rows", 1) for h in own]
+    order = tuple(k + c for c in (0, 1) for k in chips)
+    act, keep, send = tile_products(
+        order, own + other, tile_coords, tile_counts, me, bias, cotangent.T, tile_values
+    )
+    got = swap(send, "rows", 1)
+    chip_sum = [keep[j].astype(F32) + got[j].astype(F32) for j in range(len(chips))]
+    total = chip_sum[0]
+    for j, k in enumerate(chips[1:], 1):
+        total = total + swap(chip_sum[j].astype(BF16), "rows", k).astype(F32)
+    grad_hidden = total.astype(BF16)
+
+    scale = 1.0 / math.sqrt(rows_dev * n_rows)
+    part = weight_part(scale, cols_order, col, grad_hidden, x_parts)
+    part = part.reshape(n_rows, -1, width)
+    part_send = jnp.stack([part[me ^ (k + 1)] for k in chips]).astype(BF16)
+    part_got = swap(part_send, "rows", 1)
+    weight_grad = part[me] + part_got[0].astype(F32)
+    for j, k in enumerate(chips[1:], 1):
+        both = (part[me ^ k] + part_got[j].astype(F32)).astype(BF16)
+        weight_grad = weight_grad + swap(both, "rows", k).astype(F32)
+
+    grads = [grad_hidden] + [swap(grad_hidden, "cols", k) for k in cols_order[1:]]
+    input_grad = sum_dots(weight_across, grads, ((1,), (0,)))
+    return (act.T, input_grad.T, weight_grad)
+
+
 def contract_first(a, b):
     return lax.dot_general(a, b, (((0,), (0,)), ((), ())), preferred_element_type=F32)
 
 
-def local(features, weight, bias, tile_values, tile_coords, tile_counts, cotangent):
+def local_any(features, weight, bias, tile_values, tile_coords, tile_counts, cotangent):
     rows_dev, col_width = features.shape
     n_rows = lax.axis_size("rows")
-    me = lax.axis_index("rows")
     col_start = lax.axis_index("cols") * col_width
     x_full = lax.all_gather(features.T, "cols", axis=0, tiled=True)
     w_cols = lax.dynamic_slice_in_dim(weight, col_start, col_width, 1)
     hidden = contract_first(w_cols, x_full).astype(BF16)
     all_hidden = lax.all_gather(hidden, "rows", axis=0)
     order = tuple(range(n_rows))
-    zero = jnp.zeros((), jnp.int32)
-    act, part = tile_products(
+    act, keep, send = tile_products(
         order,
         [all_hidden[s] for s in order],
         tile_coords,
         tile_counts,
-        zero,
+        jnp.zeros((), jnp.int32),
         bias,
         cotangent.T,
         tile_values,
     )
+    part = jnp.concatenate([keep, send], axis=0)
     grad_hidden = lax.psum_scatter(part, "rows", scatter_dimension=0, tiled=False)
     w_rows = lax.dynamic_slice_in_dim(weight, col_start, col_width, 0)
     grad_full = lax.all_gather(grad_hidden, "cols", axis=0, tiled=True)
     input_grad = jnp.dot(w_rows, grad_full, preferred_element_type=F32).astype(BF16)
     scale_factor = 1.0 / math.sqrt(rows_dev * n_rows)
-    weight_part = lax.dot_general(
+    weight_part_sum = lax.dot_general(
         x_full, grad_hidden, (((1,), (1,)), ((), ())), preferred_element_type=F32
     )
     weight_grad = lax.psum_scatter(
-        weight_part * scale_factor, "rows", scatter_dimension=0, tiled=True
+        weight_part_sum * scale_factor, "rows", scatter_dimension=0, tiled=True
     )
     return (act.T, input_grad.T, weight_grad)
 

time: 251 us -> 150 us (0.60)
  the two profiles are of different devices: /device:TPU:0 before, /device:TPU:8 now
where the time goes in v2:
time: 150 us; the launch traced here: 149 us
  waiting for transfers between devices  90.2 us (60%)
  Pallas kernels  20.7 us (14%)
  starting transfers between devices  18.3 us (12%)
  local copies, waits for them, and re-layouts  12 us (8%)
  other arithmetic  7.05 us (5%)
    ppermute x21, waiting for transfers between devices, swap(): lax.ppermute(value, axis, [(i, i ^ k) for i in range(lax.axis_size(axis))])  90.2 us
    ppermute x21, starting transfers between devices, swap(): lax.ppermute(value, axis, [(i, i ^ k) for i in range(lax.axis_size(axis))])  18.3 us
    pallas_call x1, Pallas kernels, tile_products(): pl.pallas_call(functools.partial(tile_kernel, block_count, slots, tile, g...  15.8 us
    unnamed x34, local copies, waits for them, and re-layouts  8.32 us
    pallas_call x2, Pallas kernels, sum_dots(): pl.pallas_call(functools.partial(sum_dots_kernel, dims, len(lefts)), out_...  3.89 us
    dynamic_slice x1, local copies, waits for them, and re-layouts, local(): lax.dynamic_slice(weight, (col * width, (col ^ k) * width), (width, width))  3.46 us
  transfers between devices with their start and end apart: 21, of which 12 were waited for; matrix products, arithmetic and copies ran while one was open for 4% of the time, Pallas kernels for 2%

profile of v2, /device:TPU:8, one launch (start us, length us, event | category | flops | bytes accessed | tf_op | source)
XLA Modules:
  0.0 149.0 jit_solution(13560098800826159492)
XLA Ops:
  0.6 0.1 collective-permute-start
  0.7 3.0 %collective-permute-start.1 = (bf16[288,640]{1,0:T(8,128)(2,1)}, bf16[288,640]{1,0:T(8,128)(2,1)S(1)}, u32[]{:S(2)}, u32[]{:S(2)}) collective-permute-start(bf16[288,640]{1,0:T(8,128)(2,1)} %bitcast.37), channel_id=1, source_target_pairs={{0,2},{1,3},{2,0},{3,1},{4,6},{5,7},{6,4},{7,5},{8,10},{9,11},{10,... | collective-permute-start | bytes 1105928 | tf_op jit(solution)/shard_map/ppermute | solution.py:216
  3.7 0.5 collective-permute-start.2
  4.2 3.5 %fusion.11 = (bf16[288,288]{1,0:T(8,128)(2,1)}, bf16[288,288]{1,0:T(8,128)(2,1)}, bf16[288,288]{1,0:T(8,128)(2,1)S(1)}, bf16[288,288]{1,0:T(8,128)(2,1)S(1)}, bf...) fusion(bf16[1152,1152]{1,0:T(8,128)(2,1)} %param.8, s32[]{:T(128)S(6)} %select_n.48, ...), kind=kLoop, calls=%fused_computation.24 | loop fusion | bytes 2322448 | tf_op jit(solution)/shard_map/dynamic_slice | solution.py:235
  7.7 8.6 %collective-permute-done.refs_5_.refs_1_ = bf16[288,640]{1,0:T(8,128)(2,1)S(1)} collective-permute-done((bf16[288,640]{1,0:T(8,128)(2,1)}, bf16[288,640]{1,0:T(8,128)(2,1)S(1)}, u32[]{:S(2)}, u32[]{:S(2)}) %collective-permute-start) | collective-permute-done | bytes 368672 | tf_op jit(solution)/shard_map/ppermute | solution.py:216
  16.3 12.6 %collective-permute-done.1.refs_6_.refs_2_ = bf16[288,640]{1,0:T(8,128)(2,1)S(1)} collective-permute-done((bf16[288,640]{1,0:T(8,128)(2,1)}, bf16[288,640]{1,0:T(8,128)(2,1)S(1)}, u32[]{:S(2)}, u32[]{:S(2)}) %collective-permute-start.1) | collective-permute-done | bytes 368672 | tf_op jit(solution)/shard_map/ppermute | solution.py:216
  28.9 7.3 %collective-permute-done.2.refs_7_.refs_3_ = bf16[288,640]{1,0:T(8,128)(2,1)S(1)} collective-permute-done((bf16[288,640]{1,0:T(8,128)(2,1)}, bf16[288,640]{1,0:T(8,128)(2,1)S(1)}, u32[]{:S(2)}, u32[]{:S(2)}) %collective-permute-start.2) | collective-permute-done | bytes 368672 | tf_op jit(solution)/shard_map/ppermute | solution.py:216
  36.2 1.0 shard_map.94.rest_0_
  37.2 1.6 %collective-permute-start.3 = (bf16[288,640]{1,0:T(8,128)(2,1)S(1)}, bf16[288,640]{1,0:T(8,128)(2,1)S(1)}, u32[]{:S(2)}, u32[]{:S(2)}) collective-permute-start(bf16[288,640]{1,0:T(8,128)(2,1)S(1)} %shard_map.94.rest_0_), channel_id=1, source_target_pairs={{0,8},{4,12},{8,0},{12,4},{16,24},{20,28},{24,16},{28,20},{1,9},{5... | collective-permute-start | bytes 1105928 | tf_op jit(solution)/shard_map/ppermute | solution.py:216
  38.8 1.5 %collective-permute-start.4 = (bf16[288,640]{1,0:T(8,128)(2,1)S(1)}, bf16[288,640]{1,0:T(8,128)(2,1)S(1)}, u32[]{:S(2)}, u32[]{:S(2)}) collective-permute-start(bf16[288,640]{1,0:T(8,128)(2,1)S(1)} %shard_map.94.rest_0_), channel_id=1, source_target_pairs={{0,16},{4,20},{8,24},{12,28},{16,0},{20,4},{24,8},{28,12},{1,17},{... | collective-permute-start | bytes 1105928 | tf_op jit(solution)/shard_map/ppermute | solution.py:216
  40.3 0.5 collective-permute-start.5
  40.8 8.0 %collective-permute-done.3.rest_1_ = bf16[288,640]{1,0:T(8,128)(2,1)S(1)} collective-permute-done((bf16[288,640]{1,0:T(8,128)(2,1)S(1)}, bf16[288,640]{1,0:T(8,128)(2,1)S(1)}, u32[]{:S(2)}, u32[]{:S(2)}) %collective-permute-start.3) | collective-permute-done | bytes 368672 | tf_op jit(solution)/shard_map/ppermute | solution.py:216
  48.8 0.7 copy-done.7
  49.6 6.0 %collective-permute-done.4.rest_2_ = bf16[288,640]{1,0:T(8,128)(2,1)S(1)} collective-permute-done((bf16[288,640]{1,0:T(8,128)(2,1)S(1)}, bf16[288,640]{1,0:T(8,128)(2,1)S(1)}, u32[]{:S(2)}, u32[]{:S(2)}) %collective-permute-start.4) | collective-permute-done | bytes 368672 | tf_op jit(solution)/shard_map/ppermute | solution.py:216
  55.6 0.7 copy-done.9
  56.4 0.5 collective-permute-start.9
  56.9 0.7 copy-done.11
  57.6 0.1 broadcast_in_dim.4.bias_ref
  57.7 0.1 reshape.44.coords_ref
  57.8 0.5 collective-permute-done.9.rest_7_
  58.3 1.0 copy-done.6
  59.3 1.0 copy-done.8
  60.3 1.0 copy-done.10
  61.3 1.0 copy-done.12
  62.3 15.8 %shard_map.95 = (bf16[288,640]{1,0:T(8,128)(2,1)}, bf16[4,288,640]{2,1,0:T(8,128)(2,1)S(1)}, bf16[4,288,640]{2,1,0:T(8,128)(2,1)}) custom-call(s32[240]{0:T(256)S(1)} %reshape.44.coords_ref, s32[5]{0:T(128)S(1)} %copy-done.13, s32[1]{0:T(128)} %bitcast.me_ref, f32[288,1]{1,0:T(8,128)S(1)} %broadcast_in_dim.4.bias_ref, bf16[288,640]{1,0:T(8,128)(2,1)S(1)} %bitcast.41, ...), custom_call_target="tpu_custom_call" | custom-call | flops 4529848320 | bytes 7864320 | tf_op jit(solution)/shard_map/pallas_call | solution.py:134
  78.1 0.1 collective-permute-start.10
  78.2 3.5 %collective-permute-done.10 = bf16[4,288,640]{2,1,0:T(8,128)(2,1)S(1)} collective-permute-done((bf16[4,288,640]{2,1,0:T(8,128)(2,1)}, bf16[4,288,640]{2,1,0:T(8,128)(2,1)S(1)}, u32[]{:S(2)}, u32[]{:S(2)}) %collective-permute-start.10) | collective-permute-done | bytes 1474592 | tf_op jit(solution)/shard_map/ppermute | solution.py:216
  81.6 1.1 copy-done.14
  82.8 1.0 fusion.3
  83.8 2.0 %collective-permute-start.12 = (bf16[288,640]{1,0:T(8,128)(2,1)S(1)}, bf16[288,640]{1,0:T(8,128)(2,1)}, u32[]{:S(2)}, u32[]{:S(2)}) collective-permute-start(bf16[288,640]{1,0:T(8,128)(2,1)S(1)} %get-tuple-element.11), channel_id=1, source_target_pairs={{0,16},{4,20},{8,24},{12,28},{16,0},{20,4},{24,8},{28,12},{1,17},{... | collective-permute-start | bytes 1105928 | tf_op jit(solution)/shard_map/ppermute | solution.py:216
  85.8 1.5 %collective-permute-start.13 = (bf16[288,640]{1,0:T(8,128)(2,1)S(1)}, bf16[288,640]{1,0:T(8,128)(2,1)}, u32[]{:S(2)}, u32[]{:S(2)}) collective-permute-start(bf16[288,640]{1,0:T(8,128)(2,1)S(1)} %get-tuple-element.10), channel_id=1, source_target_pairs={{0,24},{4,28},{8,16},{12,20},{16,8},{20,12},{24,0},{28,4},{1,25},{... | collective-permute-start | bytes 1105928 | tf_op jit(solution)/shard_map/ppermute | solution.py:216
  87.3 8.3 %collective-permute-done.11 = bf16[288,640]{1,0:T(8,128)(2,1)} collective-permute-done((bf16[288,640]{1,0:T(8,128)(2,1)}, bf16[288,640]{1,0:T(8,128)(2,1)}, u32[]{:S(2)}, u32[]{:S(2)}) %collective-permute-start.11) | collective-permute-done | bytes 368672 | tf_op jit(solution)/shard_map/ppermute | solution.py:216
  95.6 8.2 %collective-permute-done.13 = bf16[288,640]{1,0:T(8,128)(2,1)} collective-permute-done((bf16[288,640]{1,0:T(8,128)(2,1)S(1)}, bf16[288,640]{1,0:T(8,128)(2,1)}, u32[]{:S(2)}, u32[]{:S(2)}) %collective-permute-start.13) | collective-permute-done | bytes 368672 | tf_op jit(solution)/shard_map/ppermute | solution.py:216
  103.7 1.6 %fusion.2.refs_4_.grad_ref = bf16[288,640]{1,0:T(8,128)(2,1)S(1)} fusion(bf16[288,640]{1,0:T(8,128)(2,1)} %collective-permute-done.13, bf16[288,640]{1,0:T(8,128)(2,1)} %collective-permute-done.12, bf16[288,640]{1,0:T(8,128)(2,1)} %collective-permute-done.11, bf16[4,288,640]{2,1,0:T(8,128)(2,1)} %copy-done.14, bf16[4,288,640]{2,1,0:T(8,128)(2,1)S(1)} %get-tuple-element.7), kind=kLoop, calls=%fused_computation.3 | loop fusion | flops 1843200 | bytes 2211840 | tf_op jit(solution)/shard_map/convert_element_type | solution.py:251
  105.3 1.0 copy-done.2
  106.3 1.0 shard_map.97
  107.4 0.9 pad_maximum_fusion
  108.3 3.0 %collective-permute-start.15 = (bf16[288,640]{1,0:T(8,128)(2,1)S(1)}, bf16[288,640]{1,0:T(8,128)(2,1)}, u32[]{:S(2)}, u32[]{:S(2)}) collective-permute-start(bf16[288,640]{1,0:T(8,128)(2,1)S(1)} %fusion.2.refs_4_.grad_ref), channel_id=1, source_target_pairs={{0,2},{1,3},{2,0},{3,1},{4,6},{5,7},{6,4},{7,5},{8,10},{9,11},{10,... | collective-permute-start | bytes 1105928 | tf_op jit(solution)/shard_map/ppermute | solution.py:216
  111.3 0.5 collective-permute-start.16
  111.8 1.8 %fusion.8 = (bf16[144,288]{1,0:T(8,128)(2,1)}, bf16[144,288]{1,0:T(8,128)(2,1)}, bf16[144,288]{1,0:T(8,128)(2,1)}) fusion(f32[8,144,288]{2,1,0:T(8,128)S(1)} %bitcast.34, s32[]{:T(128)S(6)} %select_n.57, bf16[4,144,288]{2,1,0:T(8,128)(2,1)} %collective-permute-done.17, s32[]{:T(128)S(6)} %select_n.59, s32[]{:T(128)S(6)} %select_n.58), kind=kLoop, calls=%fused_computation.21 | loop fusion | flops 373248 | bytes 995340 | tf_op jit(solution)/shard_map/convert_element_type | solution.py:260
  113.6 0.6 collective-permute-start.18
  114.1 1.5 %collective-permute-start.19 = (bf16[144,288]{1,0:T(8,128)(2,1)}, bf16[144,288]{1,0:T(8,128)(2,1)}, u32[]{:S(2)}, u32[]{:S(2)}) collective-permute-start(bf16[144,288]{1,0:T(8,128)(2,1)} %get-tuple-element.21), channel_id=1, source_target_pairs={{0,16},{4,20},{8,24},{12,28},{16,0},{20,4},{24,8},{28,12},{1,17},{... | collective-permute-start | bytes 248840 | tf_op jit(solution)/shard_map/ppermute | solution.py:216
  115.7 8.9 %collective-permute-done.14.refs_5_ = bf16[288,640]{1,0:T(8,128)(2,1)S(1)} collective-permute-done((bf16[288,640]{1,0:T(8,128)(2,1)S(1)}, bf16[288,640]{1,0:T(8,128)(2,1)S(1)}, u32[]{:S(2)}, u32[]{:S(2)}) %collective-permute-start.14) | collective-permute-done | bytes 368672 | tf_op jit(solution)/shard_map/ppermute | solution.py:216
  124.6 1.5 %collective-permute-start.20 = (bf16[144,288]{1,0:T(8,128)(2,1)}, bf16[144,288]{1,0:T(8,128)(2,1)}, u32[]{:S(2)}, u32[]{:S(2)}) collective-permute-start(bf16[144,288]{1,0:T(8,128)(2,1)} %get-tuple-element.20), channel_id=1, source_target_pairs={{0,24},{4,28},{8,16},{12,20},{16,8},{20,12},{24,0},{28,4},{1,25},{... | collective-permute-start | bytes 248840 | tf_op jit(solution)/shard_map/ppermute | solution.py:216
  126.1 10.0 %collective-permute-done.15.refs_6_ = bf16[288,640]{1,0:T(8,128)(2,1)} collective-permute-done((bf16[288,640]{1,0:T(8,128)(2,1)S(1)}, bf16[288,640]{1,0:T(8,128)(2,1)}, u32[]{:S(2)}, u32[]{:S(2)}) %collective-permute-start.15) | collective-permute-done | bytes 368672 | tf_op jit(solution)/shard_map/ppermute | solution.py:216
  136.1 8.2 %collective-permute-done.16.refs_7_ = bf16[288,640]{1,0:T(8,128)(2,1)} collective-permute-done((bf16[288,640]{1,0:T(8,128)(2,1)S(1)}, bf16[288,640]{1,0:T(8,128)(2,1)}, u32[]{:S(2)}, u32[]{:S(2)}) %collective-permute-start.16) | collective-permute-done | bytes 368672 | tf_op jit(solution)/shard_map/ppermute | solution.py:216
  144.4 2.8 %shard_map.96 = bf16[288,640]{1,0:T(8,128)(2,1)} custom-call(bf16[288,288]{1,0:T(8,128)(2,1)S(1)} %get-tuple-element.17.refs_0_, bf16[288,288]{1,0:T(8,128)(2,1)S(1)} %copy-done.4, bf16[288,288]{1,0:T(8,128)(2,1)S(1)} %copy-done.5, bf16[288,288]{1,0:T(8,128)(2,1)S(1)} %copy-done.3, bf16[288,640]{1,0:T(8,128)(2,1)S(1)} %fusion.2.refs_4_.grad_ref, ...), custom_call_target="tpu_custom_call" | custom-call | flops 424673280 | bytes 2138112 | tf_op jit(solution)/shard_map/pallas_call | solution.py:170
  147.2 1.8 %fusion.7 = f32[144,288]{1,0:T(8,128)} fusion(bf16[144,288]{1,0:T(8,128)(2,1)} %collective-permute-done.20, bf16[144,288]{1,0:T(8,128)(2,1)} %collective-permute-done.19, bf16[144,288]{1,0:T(8,128)(2,1)} %collective-permute-done.18, f32[8,144,288]{2,1,0:T(8,128)S(1)} %bitcast.35, s32[]{:T(128)S(6)} %select_n.52, bf16[4,144,288]{2,1,0:T(8,128)(2,1)} %collective-permute-done.17), kind=kLoop, calls=%fused_computation.13 | loop fusion | flops 331776 | bytes 663556 | tf_op jit(solution)/shard_map/add | solution.py:261
  (41 shorter events, 0.2 us)
Async XLA Ops:
  0.6 35.6 %copy-start = (bf16[640,288]{0,1:T(8,128)(2,1)S(1)}, bf16[640,288]{0,1:T(8,128)(2,1)}, u32[]{:S(2)}) copy-start(bf16[640,288]{0,1:T(8,128)(2,1)} %param.7) | copy-start | bytes 1105924
  0.6 15.6 %collective-permute-start = (bf16[288,640]{1,0:T(8,128)(2,1)}, bf16[288,640]{1,0:T(8,128)(2,1)S(1)}, u32[]{:S(2)}, u32[]{:S(2)}) collective-permute-start(bf16[288,640]{1,0:T(8,128)(2,1)} %bitcast.36), channel_id=1, source_target_pairs={{0,1},{1,0},{2,3},{3,2},{4,5},{5,4},{6,7},{7,6},{8,9},{9,8},{10,11... | collective-permute-start | bytes 1105928 | tf_op jit(solution)/shard_map/ppermute | solution.py:216
  0.7 28.2 %collective-permute-start.1 = (bf16[288,640]{1,0:T(8,128)(2,1)}, bf16[288,640]{1,0:T(8,128)(2,1)S(1)}, u32[]{:S(2)}, u32[]{:S(2)}) collective-permute-start(bf16[288,640]{1,0:T(8,128)(2,1)} %bitcast.37), channel_id=1, source_target_pairs={{0,2},{1,3},{2,0},{3,1},{4,6},{5,7},{6,4},{7,5},{8,10},{9,11},{10,... | collective-permute-start | bytes 1105928 | tf_op jit(solution)/shard_map/ppermute | solution.py:216
  3.7 32.4 %collective-permute-start.2 = (bf16[288,640]{1,0:T(8,128)(2,1)}, bf16[288,640]{1,0:T(8,128)(2,1)S(1)}, u32[]{:S(2)}, u32[]{:S(2)}) collective-permute-start(bf16[288,640]{1,0:T(8,128)(2,1)} %bitcast.38), channel_id=1, source_target_pairs={{0,3},{1,2},{2,1},{3,0},{4,7},{5,6},{6,5},{7,4},{8,11},{9,10},{10,... | collective-permute-start | bytes 1105928 | tf_op jit(solution)/shard_map/ppermute | solution.py:216
  7.7 50.0 %copy-start.16 = (f32[288]{0:T(512)S(1)}, f32[288]{0:T(512)}, u32[]{:S(2)}) copy-start(f32[288]{0:T(512)} %param.9) | copy-start | bytes 3460
  7.7 50.1 %copy-start.15 = (s32[5,48]{1,0:T(8,128)S(1)}, s32[5,48]{1,0:T(8,128)}, u32[]{:S(2)}) copy-start(s32[5,48]{1,0:T(8,128)} %param.11) | copy-start | bytes 2884
  7.7 50.7 %copy-start.13 = (s32[5]{0:T(128)S(1)}, s32[5]{0:T(128)}, u32[]{:S(2)}) copy-start(s32[5]{0:T(128)} %counts_ref.1) | copy-start | bytes 64
  36.2 22.1 %copy-start.1 = (bf16[288,640]{1,0:T(8,128)(2,1)}, bf16[288,640]{1,0:T(8,128)(2,1)S(1)}, u32[]{:S(2)}) copy-start(bf16[288,640]{1,0:T(8,128)(2,1)S(1)} %collective-permute-done.2.refs_7_.refs_3_) | copy-start | bytes 1105924
  37.2 11.6 %collective-permute-start.3 = (bf16[288,640]{1,0:T(8,128)(2,1)S(1)}, bf16[288,640]{1,0:T(8,128)(2,1)S(1)}, u32[]{:S(2)}, u32[]{:S(2)}) collective-permute-start(bf16[288,640]{1,0:T(8,128)(2,1)S(1)} %shard_map.94.rest_0_), channel_id=1, source_target_pairs={{0,8},{4,12},{8,0},{12,4},{16,24},{20,28},{24,16},{28,20},{1,9},{5... | collective-permute-start | bytes 1105928 | tf_op jit(solution)/shard_map/ppermute | solution.py:216
  38.8 16.8 %collective-permute-start.4 = (bf16[288,640]{1,0:T(8,128)(2,1)S(1)}, bf16[288,640]{1,0:T(8,128)(2,1)S(1)}, u32[]{:S(2)}, u32[]{:S(2)}) collective-permute-start(bf16[288,640]{1,0:T(8,128)(2,1)S(1)} %shard_map.94.rest_0_), channel_id=1, source_target_pairs={{0,16},{4,20},{8,24},{12,28},{16,0},{20,4},{24,8},{28,12},{1,17},{... | collective-permute-start | bytes 1105928 | tf_op jit(solution)/shard_map/ppermute | solution.py:216
  40.3 16.0 %collective-permute-start.5 = (bf16[288,640]{1,0:T(8,128)(2,1)S(1)}, bf16[288,640]{1,0:T(8,128)(2,1)S(1)}, u32[]{:S(2)}, u32[]{:S(2)}) collective-permute-start(bf16[288,640]{1,0:T(8,128)(2,1)S(1)} %shard_map.94.rest_0_), channel_id=1, source_target_pairs={{0,24},{4,28},{8,16},{12,20},{16,8},{20,12},{24,0},{28,4},{1,25},{... | collective-permute-start | bytes 1105928 | tf_op jit(solution)/shard_map/ppermute | solution.py:216
  40.8 17.0 %collective-permute-start.6 = (bf16[288,640]{1,0:T(8,128)(2,1)S(1)}, bf16[288,640]{1,0:T(8,128)(2,1)}, u32[]{:S(2)}, u32[]{:S(2)}) collective-permute-start(bf16[288,640]{1,0:T(8,128)(2,1)S(1)} %shard_map.94.rest_0_), channel_id=1, source_target_pairs={{0,4},{4,0},{8,12},{12,8},{16,20},{20,16},{24,28},{28,24},{1,5},{5... | collective-permute-start | bytes 1105928 | tf_op jit(solution)/shard_map/ppermute | solution.py:216
  48.8 9.0 %collective-permute-start.7 = (bf16[288,640]{1,0:T(8,128)(2,1)S(1)}, bf16[288,640]{1,0:T(8,128)(2,1)}, u32[]{:S(2)}, u32[]{:S(2)}) collective-permute-start(bf16[288,640]{1,0:T(8,128)(2,1)S(1)} %collective-permute-done.3.rest_1_), channel_id=1, source_target_pairs={{0,4},{4,0},{8,12},{12,8},{16,20},{20,16},{24,28},{28,24},{1,5},{5... | collective-permute-start | bytes 1105928 | tf_op jit(solution)/shard_map/ppermute | solution.py:216
  48.8 0.7 copy-start.7
  55.6 2.2 %collective-permute-start.8 = (bf16[288,640]{1,0:T(8,128)(2,1)S(1)}, bf16[288,640]{1,0:T(8,128)(2,1)}, u32[]{:S(2)}, u32[]{:S(2)}) collective-permute-start(bf16[288,640]{1,0:T(8,128)(2,1)S(1)} %collective-permute-done.4.rest_2_), channel_id=1, source_target_pairs={{0,4},{4,0},{8,12},{12,8},{16,20},{20,16},{24,28},{28,24},{1,5},{5... | collective-permute-start | bytes 1105928 | tf_op jit(solution)/shard_map/ppermute | solution.py:216
  55.6 0.7 copy-start.9
  56.4 2.0 %collective-permute-start.9 = (bf16[288,640]{1,0:T(8,128)(2,1)S(1)}, bf16[288,640]{1,0:T(8,128)(2,1)}, u32[]{:S(2)}, u32[]{:S(2)}) collective-permute-start(bf16[288,640]{1,0:T(8,128)(2,1)S(1)} %collective-permute-done.5.rest_3_), channel_id=1, source_target_pairs={{0,4},{4,0},{8,12},{12,8},{16,20},{20,16},{24,28},{28,24},{1,5},{5... | collective-permute-start | bytes 1105928 | tf_op jit(solution)/shard_map/ppermute | solution.py:216
  56.9 0.7 copy-start.11
  58.3 1.0 copy-start.6
  59.3 1.0 copy-start.8
  60.3 1.0 copy-start.10
  61.3 1.0 copy-start.12
  78.1 3.5 %collective-permute-start.10 = (bf16[4,288,640]{2,1,0:T(8,128)(2,1)}, bf16[4,288,640]{2,1,0:T(8,128)(2,1)S(1)}, u32[]{:S(2)}, u32[]{:S(2)}) collective-permute-start(bf16[4,288,640]{2,1,0:T(8,128)(2,1)} %get-tuple-element.8), channel_id=1, source_target_pairs={{0,4},{4,0},{8,12},{12,8},{16,20},{20,16},{24,28},{28,24},{1,5},{5... | collective-permute-start | bytes 4423688 | tf_op jit(solution)/shard_map/ppermute | solution.py:216
  81.6 1.1 copy-start.14
  83.8 11.7 %collective-permute-start.11 = (bf16[288,640]{1,0:T(8,128)(2,1)}, bf16[288,640]{1,0:T(8,128)(2,1)}, u32[]{:S(2)}, u32[]{:S(2)}) collective-permute-start(bf16[288,640]{1,0:T(8,128)(2,1)} %get-tuple-element.9), channel_id=1, source_target_pairs={{0,8},{4,12},{8,0},{12,4},{16,24},{20,28},{24,16},{28,20},{1,9},{5... | collective-permute-start | bytes 1105928 | tf_op jit(solution)/shard_map/ppermute | solution.py:216
  83.8 11.7 %collective-permute-start.12 = (bf16[288,640]{1,0:T(8,128)(2,1)S(1)}, bf16[288,640]{1,0:T(8,128)(2,1)}, u32[]{:S(2)}, u32[]{:S(2)}) collective-permute-start(bf16[288,640]{1,0:T(8,128)(2,1)S(1)} %get-tuple-element.11), channel_id=1, source_target_pairs={{0,16},{4,20},{8,24},{12,28},{16,0},{20,4},{24,8},{28,12},{1,17},{... | collective-permute-start | bytes 1105928 | tf_op jit(solution)/shard_map/ppermute | solution.py:216
  85.8 17.9 %collective-permute-start.13 = (bf16[288,640]{1,0:T(8,128)(2,1)S(1)}, bf16[288,640]{1,0:T(8,128)(2,1)}, u32[]{:S(2)}, u32[]{:S(2)}) collective-permute-start(bf16[288,640]{1,0:T(8,128)(2,1)S(1)} %get-tuple-element.10), channel_id=1, source_target_pairs={{0,24},{4,28},{8,16},{12,20},{16,8},{20,12},{24,0},{28,4},{1,25},{... | collective-permute-start | bytes 1105928 | tf_op jit(solution)/shard_map/ppermute | solution.py:216
  105.3 1.0 copy-start.2
  107.3 37.0 %copy-start.3 = (bf16[288,288]{1,0:T(8,128)(2,1)S(1)}, bf16[288,288]{1,0:T(8,128)(2,1)}, u32[]{:S(2)}) copy-start(bf16[288,288]{1,0:T(8,128)(2,1)} %get-tuple-element.12.refs_3_) | copy-start | bytes 497668
  107.3 37.0 %copy-start.4 = (bf16[288,288]{1,0:T(8,128)(2,1)S(1)}, bf16[288,288]{1,0:T(8,128)(2,1)}, u32[]{:S(2)}) copy-start(bf16[288,288]{1,0:T(8,128)(2,1)} %get-tuple-element.13.refs_1_) | copy-start | bytes 497668
  107.3 37.0 %copy-start.5 = (bf16[288,288]{1,0:T(8,128)(2,1)S(1)}, bf16[288,288]{1,0:T(8,128)(2,1)}, u32[]{:S(2)}) copy-start(bf16[288,288]{1,0:T(8,128)(2,1)} %get-tuple-element.18.refs_2_) | copy-start | bytes 497668
  108.3 3.5 %collective-permute-start.17 = (bf16[4,144,288]{2,1,0:T(8,128)(2,1)}, bf16[4,144,288]{2,1,0:T(8,128)(2,1)}, u32[]{:S(2)}, u32[]{:S(2)}) collective-permute-start(bf16[4,144,288]{2,1,0:T(8,128)(2,1)} %pad_maximum_fusion), channel_id=1, source_target_pairs={{0,4},{4,0},{8,12},{12,8},{16,20},{20,16},{24,28},{28,24},{1,5},{5... | collective-permute-start | bytes 995336 | tf_op jit(solution)/shard_map/ppermute | solution.py:216
  108.3 16.3 %collective-permute-start.14 = (bf16[288,640]{1,0:T(8,128)(2,1)S(1)}, bf16[288,640]{1,0:T(8,128)(2,1)S(1)}, u32[]{:S(2)}, u32[]{:S(2)}) collective-permute-start(bf16[288,640]{1,0:T(8,128)(2,1)S(1)} %fusion.2.refs_4_.grad_ref), channel_id=1, source_target_pairs={{0,1},{1,0},{2,3},{3,2},{4,5},{5,4},{6,7},{7,6},{8,9},{9,8},{10,11... | collective-permute-start | bytes 1105928 | tf_op jit(solution)/shard_map/ppermute | solution.py:216
  108.3 27.8 %collective-permute-start.15 = (bf16[288,640]{1,0:T(8,128)(2,1)S(1)}, bf16[288,640]{1,0:T(8,128)(2,1)}, u32[]{:S(2)}, u32[]{:S(2)}) collective-permute-start(bf16[288,640]{1,0:T(8,128)(2,1)S(1)} %fusion.2.refs_4_.grad_ref), channel_id=1, source_target_pairs={{0,2},{1,3},{2,0},{3,1},{4,6},{5,7},{6,4},{7,5},{8,10},{9,11},{10,... | collective-permute-start | bytes 1105928 | tf_op jit(solution)/shard_map/ppermute | solution.py:216
  111.3 33.0 %collective-permute-start.16 = (bf16[288,640]{1,0:T(8,128)(2,1)S(1)}, bf16[288,640]{1,0:T(8,128)(2,1)}, u32[]{:S(2)}, u32[]{:S(2)}) collective-permute-start(bf16[288,640]{1,0:T(8,128)(2,1)S(1)} %fusion.2.refs_4_.grad_ref), channel_id=1, source_target_pairs={{0,3},{1,2},{2,1},{3,0},{4,7},{5,6},{6,5},{7,4},{8,11},{9,10},{10,... | collective-permute-start | bytes 1105928 | tf_op jit(solution)/shard_map/ppermute | solution.py:216
  113.6 33.6 %collective-permute-start.18 = (bf16[144,288]{1,0:T(8,128)(2,1)}, bf16[144,288]{1,0:T(8,128)(2,1)}, u32[]{:S(2)}, u32[]{:S(2)}) collective-permute-start(bf16[144,288]{1,0:T(8,128)(2,1)} %get-tuple-element.19), channel_id=1, source_target_pairs={{0,8},{4,12},{8,0},{12,4},{16,24},{20,28},{24,16},{28,20},{1,9},{5... | collective-permute-start | bytes 248840 | tf_op jit(solution)/shard_map/ppermute | solution.py:216
  114.1 33.1 %collective-permute-start.19 = (bf16[144,288]{1,0:T(8,128)(2,1)}, bf16[144,288]{1,0:T(8,128)(2,1)}, u32[]{:S(2)}, u32[]{:S(2)}) collective-permute-start(bf16[144,288]{1,0:T(8,128)(2,1)} %get-tuple-element.21), channel_id=1, source_target_pairs={{0,16},{4,20},{8,24},{12,28},{16,0},{20,4},{24,8},{28,12},{1,17},{... | collective-permute-start | bytes 248840 | tf_op jit(solution)/shard_map/ppermute | solution.py:216
  124.6 22.6 %collective-permute-start.20 = (bf16[144,288]{1,0:T(8,128)(2,1)}, bf16[144,288]{1,0:T(8,128)(2,1)}, u32[]{:S(2)}, u32[]{:S(2)}) collective-permute-start(bf16[144,288]{1,0:T(8,128)(2,1)} %get-tuple-element.20), channel_id=1, source_target_pairs={{0,24},{4,28},{8,16},{12,20},{16,8},{20,12},{24,0},{28,4},{1,25},{... | collective-permute-start | bytes 248840 | tf_op jit(solution)/shard_map/ppermute | solution.py:216

commit v3 on v1

v3 whole, which is shorter than its diff:
```python
import functools
import math

import jax
import jax.numpy as jnp
from jax import lax
from jax.experimental import pallas as pl
from jax.experimental.pallas import tpu as pltpu
from jax.sharding import PartitionSpec as P

F32 = jnp.float32
BF16 = jnp.bfloat16
CHUNK = 16
MIB = 1024 * 1024


def largest_divisor(number, limit):
    return max(d for d in range(1, limit + 1) if number % d == 0)


def tile_kernel(
    slots,
    tile,
    group,
    shard_order,
    gathers,
    scatters,
    coords_ref,
    counts_ref,
    me_ref,
    bias_ref,
    cotangent_ref,
    tiles_ref,
    *rest,
):
    shards, block_count = len(shard_order), sum(gathers)
    hidden_refs, rest = rest[: shards * len(gathers)], rest[shards * len(gathers) :]
    act_ref, *part_refs = rest[:-5]
    tiles, hidden, partial, tile_sems, hidden_sems = rest[-5:]
    groups = slots // group
    me = me_ref[0]
    width = act_ref.shape[0]

    def tile_copy(i, q):
        span = pl.ds(q * group, group)
        return pltpu.make_async_copy(
            tiles_ref.at[i, span], tiles.at[i, span], tile_sems.at[i, q]
        )

    hidden_copies = []
    for s in range(shards):
        owner = me ^ shard_order[s]
        block = 0
        for c, count in enumerate(gathers):
            for b in range(count):
                hidden_copies.append(
                    pltpu.make_async_copy(
                        hidden_refs[c * shards + s].at[:, pl.ds(b * tile, tile)],
                        hidden.at[owner * block_count + block],
                        hidden_sems.at[s, block],
                    )
                )
                block += 1
    for copy in hidden_copies:
        copy.start()
    for i in range(block_count):
        for q in range(groups):

            @pl.when(q * group < counts_ref[i])
            def _():
                tile_copy(i, q).start()

    partial[...] = jnp.zeros_like(partial)
    for copy in hidden_copies:
        copy.wait()

    chunk = largest_divisor(slots, CHUNK)

    def several(i, p):
        parts, places = [], []
        for t in range(chunk):
            k = p * chunk + t
            value = tiles[i, k]
            if t:
                value = jnp.where(k < counts_ref[i], value, jnp.zeros_like(value))
            parts.append(value)
            places.append(coords_ref[i * slots + k])
        return jnp.concatenate(parts, axis=1), places

    for i in range(block_count):
        for q in range(groups):

            @pl.when(q * group < counts_ref[i])
            def _():
                tile_copy(i, q).wait()

        steps = (counts_ref[i] + (chunk - 1)) // chunk
        lanes = pl.ds(i * tile, tile)

        def forward(p, total):
            values, places = several(i, p)
            panel = jnp.concatenate([hidden[c] for c in places], axis=1)
            return total + lax.dot_general(
                panel, values, (((1,), (1,)), ((), ())), preferred_element_type=F32
            )

        total = lax.fori_loop(0, steps, forward, jnp.zeros((width, tile), F32))
        pre = total + bias_ref[...]
        s = jax.nn.sigmoid(pre)
        act_ref[:, lanes] = (pre * s).astype(BF16)
        slope = s * (1.0 + pre * (1.0 - s))
        grad = (cotangent_ref[:, lanes].astype(F32) * slope).astype(BF16)

        def backward(p, carry):
            values, places = several(i, p)
            out = jnp.dot(grad, values, preferred_element_type=F32)
            for t, c in enumerate(places):
                partial[c] += out[:, t * tile : (t + 1) * tile]
            return carry

        lax.fori_loop(0, steps, backward, 0)

    half = shards // 2
    first = 0
    for c, count in enumerate(scatters):
        keep_own, keep, send_own, send = part_refs[4 * c : 4 * c + 4]
        for s in range(shards):
            own, others = (keep_own, keep) if s < half else (send_own, send)
            out_ref = own if s % half == 0 else others.at[s % half - 1]
            owner = me ^ shard_order[s]
            for b in range(count):
                value = partial[owner * block_count + first + b].astype(BF16)
                out_ref[:, b * tile : (b + 1) * tile] = value
        first += count


def tile_products(
    shard_order, gathers, scatters, hidden, coords, counts, me, bias, cotangent, tiles
):
    block_count, slots, tile, unused_side = tiles.shape
    width, rows_dev = cotangent.shape
    shards = len(shard_order)
    group = largest_divisor(slots, 8)
    smem = pl.BlockSpec(memory_space=pltpu.SMEM)
    vmem = pl.BlockSpec(memory_space=pltpu.VMEM)
    hbm = pl.BlockSpec(memory_space=pltpu.HBM)
    vmem_bytes = 2 * tiles.size + (6 + 2) * shards * width * rows_dev + 16 * cotangent.size
    flops = 4 * block_count * slots * tile * tile * width
    parts = []
    for count in scatters:
        own = jax.ShapeDtypeStruct((width, count * tile), BF16)
        others = jax.ShapeDtypeStruct((max(shards // 2 - 1, 1), width, count * tile), BF16)
        parts += [own, others] * 2
    flat = [v for chunk in hidden for v in chunk]
    return pl.pallas_call(
        functools.partial(tile_kernel, slots, tile, group, shard_order, gathers, scatters),
        out_shape=(jax.ShapeDtypeStruct((width, rows_dev), BF16), *parts),
        in_specs=[smem, smem, smem, vmem, vmem, hbm] + [hbm] * len(flat),
        out_specs=(vmem,) * (1 + len(parts)),
        scratch_shapes=[
            pltpu.VMEM(tiles.shape, BF16),
            pltpu.VMEM((shards * block_count, width, tile), BF16),
            pltpu.VMEM((shards * block_count, width, tile), F32),
            pltpu.SemaphoreType.DMA((block_count, slots // group)),
            pltpu.SemaphoreType.DMA((shards, block_count)),
        ],
        compiler_params=pltpu.CompilerParams(vmem_limit_bytes=vmem_bytes + MIB),
        cost_estimate=pl.CostEstimate(
            flops=flops, bytes_accessed=2 * tiles.size, transcendentals=width * rows_dev
        ),
    )(
        coords.reshape(-1),
        counts,
        me.reshape(1),
        bias[:, None],
        cotangent,
        *[in_hbm(v) for v in (tiles, *flat)],
    )


def in_vmem(value):
    return pltpu.with_memory_space_constraint(value, pltpu.VMEM)


def in_hbm(value):
    return pltpu.with_memory_space_constraint(value, pltpu.HBM)


VMEM = pl.BlockSpec(memory_space=pltpu.VMEM)
ANY = pl.BlockSpec(memory_space=pl.ANY)


def small_call(kernel, out_shape, values, after, pinned=True):
    outs = jax.tree.leaves(out_shape)
    touched = sum(v.size * v.dtype.itemsize for v in (*values, *outs))
    return pl.pallas_call(
        kernel,
        out_shape=out_shape,
        in_specs=[VMEM] * len(values) + [ANY] * len(after),
        out_specs=jax.tree.map(lambda _: VMEM, out_shape),
        compiler_params=pltpu.CompilerParams(vmem_limit_bytes=2 * touched + 2 * MIB),
        cost_estimate=pl.CostEstimate(flops=0, bytes_accessed=0, transcendentals=0),
    )(*[in_vmem(v) for v in values] if pinned else values, *after)


def sum_dots(lefts, rights, dims, before=(), after=()):
    (left_dim,), unused_right = dims
    number = len(lefts)
    rows, cols = lefts[0].shape[1 - left_dim], rights[0].shape[1]
    skip = sum(v.shape[1] for v in before)

    def kernel(*refs):
        total = None
        for left, right in zip(refs[:number], refs[number : 2 * number]):
            term = lax.dot_general(
                left[...], right[...], (dims, ((), ())), preferred_element_type=F32
            )
            total = term if total is None else total + term
        start = 0
        for ref in refs[2 * number : 2 * number + len(before)]:
            refs[-1][:, start : start + ref.shape[1]] = ref[...]
            start += ref.shape[1]
        refs[-1][:, skip:] = total.astype(BF16)

    out = jax.ShapeDtypeStruct((rows, skip + cols), BF16)
    return small_call(kernel, out, (*lefts, *rights, *before), after, False)


def add_up(values, dtype, after=()):
    number = len(values)

    def kernel(*refs):
        total = refs[0][...].astype(F32)
        for ref in refs[1:number]:
            total = total + ref[...].astype(F32)
        refs[-1][...] = total.astype(dtype)

    out = jax.ShapeDtypeStruct(values[0].shape, dtype)
    return small_call(kernel, out, values, after)


def chip_sums(keep, got, after=()):
    number = keep.shape[0]

    def kernel(keep_ref, got_ref, *refs):
        for j, out_ref in enumerate(refs[len(after) :]):
            out_ref[...] = (keep_ref[j].astype(F32) + got_ref[j].astype(F32)).astype(BF16)

    out = (jax.ShapeDtypeStruct(keep.shape[1:], BF16),) * number
    return small_call(kernel, out, (keep, got), after)


def weight_parts(scale, cols_order, rows_order, col, me, grads, x_parts, after=()):
    width = grads[0].shape[0]
    rows_dev = sum(g.shape[1] for g in grads)
    n_rows = len(rows_order)
    half = n_rows // 2
    rows_out = width * len(cols_order) // n_rows
    pieces = len(x_parts[0])
    values = (*grads, *[p for parts in x_parts for p in parts])

    def kernel(col_ref, me_ref, *refs):
        inputs = refs[: len(values)]
        own_ref, keep_ref, send_own_ref, send_ref, grad, xs, part, sems = refs[-8:]
        copies = []

        def fill(target, sources, first_sem):
            start = 0
            for j, source in enumerate(sources):
                lanes = pl.ds(start, source.shape[1])
                copy = pltpu.make_async_copy(source, target.at[:, lanes], sems.at[first_sem + j])
                copy.start()
                copies.append(copy)
                start += source.shape[1]

        fill(grad, inputs[: len(grads)], 0)
        for j in range(len(cols_order)):
            first = len(grads) + j * pieces
            fill(xs.at[j], inputs[first : first + pieces], first)
        for copy in copies:
            copy.wait()
        for j, k in enumerate(cols_order):
            start = pl.multiple_of((col_ref[0] ^ k) * width, 16)
            product = lax.dot_general(
                xs[j], grad[...], (((1,), (1,)), ((), ())), preferred_element_type=F32
            )
            part[pl.ds(start, width), :] = product * scale
        for j, k in enumerate(rows_order):
            start = pl.multiple_of((me_ref[0] ^ k) * rows_out, 8)
            value = part[pl.ds(start, rows_out), :]
            if j == 0:
                own_ref[...] = value
            elif j < half:
                keep_ref[j - 1] = value
            elif j == half:
                send_own_ref[...] = value.astype(BF16)
            else:
                send_ref[j - half - 1] = value.astype(BF16)

    touched = 2 * width * rows_dev * (len(cols_order) + 1) + 8 * width * width * len(cols_order)
    smem = pl.BlockSpec(memory_space=pltpu.SMEM)
    others = max(half - 1, 1)
    return pl.pallas_call(
        kernel,
        out_shape=(
            jax.ShapeDtypeStruct((rows_out, width), F32),
            jax.ShapeDtypeStruct((others, rows_out, width), F32),
            jax.ShapeDtypeStruct((rows_out, width), BF16),
            jax.ShapeDtypeStruct((others, rows_out, width), BF16),
        ),
        in_specs=[smem, smem] + [ANY] * (len(values) + len(after)),
        out_specs=(VMEM,) * 4,
        scratch_shapes=[
            pltpu.VMEM((width, rows_dev), BF16),
            pltpu.VMEM((len(cols_order), width, rows_dev), BF16),
            pltpu.VMEM((width * len(cols_order), width), F32),
            pltpu.SemaphoreType.DMA((len(values),)),
        ],
        compiler_params=pltpu.CompilerParams(vmem_limit_bytes=2 * touched + 2 * MIB),
        cost_estimate=pl.CostEstimate(flops=0, bytes_accessed=0, transcendentals=0),
    )(col.reshape(1), me.reshape(1), *values, *after)


def swap(value, axis, k):
    return lax.ppermute(value, axis, [(i, i ^ k) for i in range(lax.axis_size(axis))])


def local(features, weight, bias, tile_values, tile_coords, tile_counts, cotangent):
    rows_dev, width = features.shape
    n_rows, n_cols = lax.axis_size("rows"), lax.axis_size("cols")
    me, col = lax.axis_index("rows"), lax.axis_index("cols")
    simple = all(n > 1 and n & (n - 1) == 0 for n in (n_rows, n_cols)) and n_rows > 2
    if not simple or width * n_cols % (8 * n_rows) or width % 16:
        return local_any(features, weight, bias, tile_values, tile_coords, tile_counts, cotangent)
    cols_order = tuple(range(n_cols))
    chips = tuple(range(0, n_rows, 2))
    block_count, unused_slots, tile, unused_side = tile_values.shape
    small = block_count // 2
    gathers = (block_count - small, small) if small else (block_count,)
    scatters = gathers[::-1]

    x = features.T
    x_parts, start = [], 0
    for count in gathers:
        piece = x[:, start * tile : (start + count) * tile]
        x_parts.append([piece] + [swap(piece, "cols", k) for k in cols_order[1:]])
        start += count
    weight_down = [
        lax.dynamic_slice(weight, ((col ^ k) * width, col * width), (width, width))
        for k in cols_order
    ]
    weight_across = [
        lax.dynamic_slice(weight, (col * width, (col ^ k) * width), (width, width))
        for k in cols_order
    ]

    order = tuple(k + c for c in (0, 1) for k in chips)
    shards = []
    for parts in x_parts:
        hidden = sum_dots(weight_down, parts, ((0,), (0,)))
        own = [hidden] + [swap(hidden, "rows", k) for k in chips[1:]]
        shards.append(own + [swap(part, "rows", 1) for part in own])

    act, *part = tile_products(
        order,
        gathers,
        scatters,
        shards,
        tile_coords,
        tile_counts,
        me,
        bias,
        cotangent.T,
        tile_values,
    )

    grads, arrived, input_grad = [], (), ()
    for c in range(len(scatters)):
        keep_own, keep, send_own, send = part[4 * c : 4 * c + 4]
        got, got_own = swap(send, "rows", 1), swap(send_own, "rows", 1)
        sums = chip_sums(keep, got, arrived)
        arrived = tuple(swap(v, "rows", k) for v, k in zip(sums, chips[1:]))
        grad = add_up((keep_own, got_own, *arrived), BF16)
        grads.append([grad] + [swap(grad, "cols", k) for k in cols_order[1:]])

    own, keep, send_own, send = weight_parts(
        1.0 / math.sqrt(rows_dev * n_rows),
        cols_order,
        order,
        col,
        me,
        [g[0] for g in grads],
        list(zip(*x_parts)),
        tuple(grads[0][1:]) if len(grads) > 1 else (),
    )
    got, got_own = swap(send, "rows", 1), swap(send_own, "rows", 1)
    weight_grad = add_up(
        (own, got_own, *[swap(v, "rows", k) for v, k in zip(chip_sums(keep, got), chips[1:])]), F32
    )

    for c, values in enumerate(grads):
        last = (weight_grad,) if c + 1 == len(grads) else ()
        input_grad = (sum_dots(weight_across, values, ((1,), (0,)), input_grad, last),)
    return (act.T, input_grad[0].T, weight_grad)


def contract_first(a, b):
    return lax.dot_general(a, b, (((0,), (0,)), ((), ())), preferred_element_type=F32)


def local_any(features, weight, bias, tile_values, tile_coords, tile_counts, cotangent):
    rows_dev, col_width = features.shape
    n_rows = lax.axis_size("rows")
    col_start = lax.axis_index("cols") * col_width
    x_full = lax.all_gather(features.T, "cols", axis=0, tiled=True)
    w_cols = lax.dynamic_slice_in_dim(weight, col_start, col_width, 1)
    hidden = contract_first(w_cols, x_full).astype(BF16)
    all_hidden = lax.all_gather(hidden, "rows", axis=0)
    order = tuple(range(n_rows))
    act, keep_own, keep, send_own, send = tile_products(
        order,
        (tile_values.shape[0],),
        (tile_values.shape[0],),
        [[all_hidden[s] for s in order]],
        tile_coords,
        tile_counts,
        jnp.zeros((), jnp.int32),
        bias,
        cotangent.T,
        tile_values,
    )
    part = jnp.concatenate([keep_own[None], keep, send_own[None], send], axis=0)
    grad_hidden = lax.psum_scatter(part, "rows", scatter_dimension=0, tiled=False)
    w_rows = lax.dynamic_slice_in_dim(weight, col_start, col_width, 0)
    grad_full = lax.all_gather(grad_hidden, "cols", axis=0, tiled=True)
    input_grad = jnp.dot(w_rows, grad_full, preferred_element_type=F32).astype(BF16)
    scale_factor = 1.0 / math.sqrt(rows_dev * n_rows)
    weight_part_sum = lax.dot_general(
        x_full, grad_hidden, (((1,), (1,)), ((), ())), preferred_element_type=F32
    )
    weight_grad = lax.psum_scatter(
        weight_part_sum * scale_factor, "rows", scatter_dimension=0, tiled=True
    )
    return (act.T, input_grad.T, weight_grad)


def solution(mesh):
    return jax.shard_map(
        local,
        mesh=mesh,
        in_specs=(
            P("rows", "cols"),
            P(),
            P("cols"),
            P("rows", None, None, None),
            P("rows", None),
            P("rows"),
            P("rows", "cols"),
        ),
        out_specs=(P("rows", "cols"), P("rows", "cols"), P("rows", "cols")),
        check_vma=False,
    )
```

time: 251 us -> 131 us (0.52); the launches traced: 246 us -> 130 us
  waiting for transfers between devices: 193 us -> 54.9 us
  starting transfers between devices: 0.2 us -> 51 us
  between operations: 13.9 us -> 0.9 us
  matrix products: 9.33 us -> 0 us
  Pallas kernels: 24.6 us -> 16.8 us
    all_gather x3 -> x0, waiting for transfers between devices: 100 us -> none  [the longest x1 39.8 us: local(): x_full = lax.all_gather(features.T, 'cols', axis=0, tiled=True)]
    ppermute x0 -> x41, waiting for transfers between devices: none -> 54.9 us  [swap(): lax.ppermute(value, axis, [(i, i ^ k) for i in range(lax.axis_size(axis))])]
    reduce_scatter x1 -> x0, waiting for transfers between devices: 52.3 us -> none  [local(): lax.psum_scatter(part, 'rows', scatter_dimension=0, tiled=False)]
    ppermute x0 -> x41, starting transfers between devices: none -> 51 us  [swap(): lax.ppermute(value, axis, [(i, i ^ k) for i in range(lax.axis_size(axis))])]
    unnamed x6 -> x0, waiting for transfers between devices: 40 us -> none
    dot_general x3 -> x0, matrix products: 9.33 us -> none  [the longest x1 3.33 us: local(): lax.dot_general(x_full, grad_hidden, (((1,), (1,)), ((), ())), preferred_...]
    pallas_call x1 -> x12, Pallas kernels: 24.6 us -> 16.8 us  [the longest x1 11 us: tile_products(): pl.pallas_call(functools.partial(tile_kernel, slots, tile, group, shard_o...]
    dynamic_slice x0 -> x1, local copies, waits for them, and re-layouts: none -> 2.7 us  [local(): lax.dynamic_slice(weight, (col * width, (col ^ k) * width), (width, width))]
  transfers between devices with their start and end apart: 5 -> 41, of which waited for: 5 -> 16; matrix products, arithmetic and copies ran while one was open for 4% -> 3% of each run, Pallas kernels for 0% -> 2%
where the time goes in v3:
time: 131 us; the launch traced here: 130 us
  waiting for transfers between devices  54.9 us (42%)
  starting transfers between devices  51 us (39%)
  Pallas kernels  16.8 us (13%)
  local copies, waits for them, and re-layouts  6.4 us (5%)
    ppermute x41, waiting for transfers between devices, swap(): lax.ppermute(value, axis, [(i, i ^ k) for i in range(lax.axis_size(axis))])  54.9 us
    ppermute x41, starting transfers between devices, swap(): lax.ppermute(value, axis, [(i, i ^ k) for i in range(lax.axis_size(axis))])  51 us
    pallas_call x1, Pallas kernels, tile_products(): pl.pallas_call(functools.partial(tile_kernel, slots, tile, group, shard_o...  11 us
    pallas_call x10, Pallas kernels, small_call(): pl.pallas_call(kernel, out_shape=out_shape, in_specs=[VMEM] * len(values)...  4.47 us
    dynamic_slice x1, local copies, waits for them, and re-layouts, local(): lax.dynamic_slice(weight, (col * width, (col ^ k) * width), (width, width))  2.7 us
  transfers between devices with their start and end apart: 41, of which 16 were waited for; matrix products, arithmetic and copies ran while one was open for 3% of the time, Pallas kernels for 2%

profile of v3, /device:TPU:0, one launch (start us, length us, event | category | flops | bytes accessed | tf_op | source)
XLA Modules:
  0.0 130.1 jit_solution(1907195296368010066)
XLA Ops:
  0.6 0.9 slice.9.refs_4_.refs_3_
  1.6 5.1 %collective-permute-start.12 = (bf16[288,256]{1,0:T(8,128)(2,1)S(1)}, bf16[288,256]{1,0:T(8,128)(2,1)S(1)}, u32[]{:S(2)}, u32[]{:S(2)}) collective-permute-start(bf16[288,256]{1,0:T(8,128)(2,1)S(1)} %slice.9.refs_4_.refs_3_), channel_id=1, source_target_pairs={{0,3},{1,2},{2,1},{3,0},{4,7},{5,6},{6,5},{7,4},{8,11},{9,10},{10,... | collective-permute-start | bytes 442376 | tf_op jit(solution)/shard_map/ppermute | solution.py:325
  6.7 0.6 collective-permute-start.10
  7.3 1.0 slice.8.refs_4_.refs_2_
  8.3 3.8 %collective-permute-start.2 = (bf16[288,384]{1,0:T(8,128)(2,1)S(1)}, bf16[288,384]{1,0:T(8,128)(2,1)S(1)}, u32[]{:S(2)}, u32[]{:S(2)}) collective-permute-start(bf16[288,384]{1,0:T(8,128)(2,1)S(1)} %slice.8.refs_4_.refs_2_), channel_id=1, source_target_pairs={{0,3},{1,2},{2,1},{3,0},{4,7},{5,6},{6,5},{7,4},{8,11},{9,10},{10,... | collective-permute-start | bytes 663560 | tf_op jit(solution)/shard_map/ppermute | solution.py:325
  12.1 6.3 %collective-permute-start = (bf16[288,384]{1,0:T(8,128)(2,1)S(1)}, bf16[288,384]{1,0:T(8,128)(2,1)S(1)}, u32[]{:S(2)}, u32[]{:S(2)}) collective-permute-start(bf16[288,384]{1,0:T(8,128)(2,1)S(1)} %slice.8.refs_4_.refs_2_), channel_id=1, source_target_pairs={{0,1},{1,0},{2,3},{3,2},{4,5},{5,4},{6,7},{7,6},{8,9},{9,8},{10,11... | collective-permute-start | bytes 663560 | tf_op jit(solution)/shard_map/ppermute | solution.py:325
  18.4 2.7 %fusion = (bf16[288,288]{1,0:T(8,128)(2,1)S(1)}, bf16[288,288]{1,0:T(8,128)(2,1)S(1)}, bf16[288,288]{1,0:T(8,128)(2,1)S(1)}, bf16[288,288]{1,0:T(8,128)(2,1)S(1)...) fusion(bf16[1152,1152]{1,0:T(8,128)(2,1)} %param.8, s32[]{:T(128)S(6)} %select_n.8, ...), kind=kLoop, calls=%fused_computation | loop fusion | bytes 2322448 | tf_op jit(solution)/shard_map/dynamic_slice | solution.py:353
  21.1 8.5 %collective-permute-done.11.refs_6_.refs_7_ = bf16[288,256]{1,0:T(8,128)(2,1)S(1)} collective-permute-done((bf16[288,256]{1,0:T(8,128)(2,1)S(1)}, bf16[288,256]{1,0:T(8,128)(2,1)S(1)}, u32[]{:S(2)}, u32[]{:S(2)}) %collective-permute-start.11) | collective-permute-done | bytes 147488 | tf_op jit(solution)/shard_map/ppermute | solution.py:325
  29.6 0.5 shard_map.95.rest_8_
  30.2 2.5 %collective-permute-start.15 = (bf16[288,256]{1,0:T(8,128)(2,1)S(1)}, bf16[288,256]{1,0:T(8,128)(2,1)S(1)}, u32[]{:S(2)}, u32[]{:S(2)}) collective-permute-start(bf16[288,256]{1,0:T(8,128)(2,1)S(1)} %shard_map.95.rest_8_), channel_id=1, source_target_pairs={{0,24},{4,28},{8,16},{12,20},{16,8},{20,12},{24,0},{28,4},{1,25},{... | collective-permute-start | bytes 442376 | tf_op jit(solution)/shard_map/ppermute | solution.py:325
  32.7 0.5 collective-permute-start.14
  33.2 4.9 %collective-permute-done.1.refs_6_ = bf16[288,384]{1,0:T(8,128)(2,1)S(1)} collective-permute-done((bf16[288,384]{1,0:T(8,128)(2,1)S(1)}, bf16[288,384]{1,0:T(8,128)(2,1)S(1)}, u32[]{:S(2)}, u32[]{:S(2)}) %collective-permute-start.1) | collective-permute-done | bytes 221216 | tf_op jit(solution)/shard_map/ppermute | solution.py:325
  38.1 1.5 %collective-permute-start.13 = (bf16[288,256]{1,0:T(8,128)(2,1)S(1)}, bf16[288,256]{1,0:T(8,128)(2,1)}, u32[]{:S(2)}, u32[]{:S(2)}) collective-permute-start(bf16[288,256]{1,0:T(8,128)(2,1)S(1)} %shard_map.95.rest_8_), channel_id=1, source_target_pairs={{0,8},{4,12},{8,0},{12,4},{16,24},{20,28},{24,16},{28,20},{1,9},{5... | collective-permute-start | bytes 442376 | tf_op jit(solution)/shard_map/ppermute | solution.py:325
  39.6 0.7 shard_map.94.rest_0_
  40.4 1.6 %collective-permute-start.5 = (bf16[288,384]{1,0:T(8,128)(2,1)S(1)}, bf16[288,384]{1,0:T(8,128)(2,1)S(1)}, u32[]{:S(2)}, u32[]{:S(2)}) collective-permute-start(bf16[288,384]{1,0:T(8,128)(2,1)S(1)} %shard_map.94.rest_0_), channel_id=1, source_target_pairs={{0,24},{4,28},{8,16},{12,20},{16,8},{20,12},{24,0},{28,4},{1,25},{... | collective-permute-start | bytes 663560 | tf_op jit(solution)/shard_map/ppermute | solution.py:325
  42.4 1.5 %collective-permute-start.3 = (bf16[288,384]{1,0:T(8,128)(2,1)S(1)}, bf16[288,384]{1,0:T(8,128)(2,1)}, u32[]{:S(2)}, u32[]{:S(2)}) collective-permute-start(bf16[288,384]{1,0:T(8,128)(2,1)S(1)} %shard_map.94.rest_0_), channel_id=1, source_target_pairs={{0,8},{4,12},{8,0},{12,4},{16,24},{20,28},{24,16},{28,20},{1,9},{5... | collective-permute-start | bytes 663560 | tf_op jit(solution)/shard_map/ppermute | solution.py:325
  44.5 0.9 collective-permute-done.19.rest_15_
  45.5 5.0 %collective-permute-done.5.rest_3_ = bf16[288,384]{1,0:T(8,128)(2,1)S(1)} collective-permute-done((bf16[288,384]{1,0:T(8,128)(2,1)S(1)}, bf16[288,384]{1,0:T(8,128)(2,1)S(1)}, u32[]{:S(2)}, u32[]{:S(2)}) %collective-permute-start.5) | collective-permute-done | bytes 221216 | tf_op jit(solution)/shard_map/ppermute | solution.py:325
  50.4 2.0 %collective-permute-done.4.rest_2_ = bf16[288,384]{1,0:T(8,128)(2,1)S(1)} collective-permute-done((bf16[288,384]{1,0:T(8,128)(2,1)S(1)}, bf16[288,384]{1,0:T(8,128)(2,1)S(1)}, u32[]{:S(2)}, u32[]{:S(2)}) %collective-permute-start.4) | collective-permute-done | bytes 221216 | tf_op jit(solution)/shard_map/ppermute | solution.py:325
  53.0 0.7 copy-done.13
  54.3 1.2 collective-permute-done.17.rest_13_
  55.5 11.0 %shard_map.96 = (bf16[288,640]{1,0:T(8,128)(2,1)}, bf16[288,256]{1,0:T(8,128)(2,1)S(1)}, bf16[3,288,256]{2,1,0:T(8,128)(2,1)S(1)}, bf16[288,256]{1,0:T(8,128)(2,...) custom-call(s32[240]{0:T(256)S(1)} %reshape.16.coords_ref, ...), custom_call_target="tpu_custom_call" | custom-call | flops 4529848320 | bytes 7864320 | tf_op jit(solution)/shard_map/pallas_call | solution.py:155
  66.5 5.1 %collective-permute-start.21 = (bf16[3,288,384]{2,1,0:T(8,128)(2,1)S(1)}, bf16[3,288,384]{2,1,0:T(8,128)(2,1)S(1)}, u32[]{:S(2)}, u32[]{:S(2)}) collective-permute-start(bf16[3,288,384]{2,1,0:T(8,128)(2,1)S(1)} %get-tuple-element.29), channel_id=1, source_target_pairs={{0,4},{4,0},{8,12},{12,8},{16,20},{20,16},{24,28},{28,24},{1,5},{5... | collective-permute-start | bytes 1990664 | tf_op jit(solution)/shard_map/ppermute | solution.py:325
  71.7 2.3 %collective-permute-done.22.got_ref = bf16[3,288,256]{2,1,0:T(8,128)(2,1)S(1)} collective-permute-done((bf16[3,288,256]{2,1,0:T(8,128)(2,1)S(1)}, bf16[3,288,256]{2,1,0:T(8,128)(2,1)S(1)}, u32[]{:S(2)}, u32[]{:S(2)}) %collective-permute-start.22) | collective-permute-done | bytes 442400 | tf_op jit(solution)/shard_map/ppermute | solution.py:325
  74.1 1.6 %collective-permute-start.23 = (bf16[288,256]{1,0:T(8,128)(2,1)S(1)}, bf16[288,256]{1,0:T(8,128)(2,1)S(1)}, u32[]{:S(2)}, u32[]{:S(2)}) collective-permute-start(bf16[288,256]{1,0:T(8,128)(2,1)S(1)} %get-tuple-element.32), channel_id=1, source_target_pairs={{0,8},{4,12},{8,0},{12,4},{16,24},{20,28},{24,16},{28,20},{1,9},{5... | collective-permute-start | bytes 442376 | tf_op jit(solution)/shard_map/ppermute | solution.py:325
  75.7 3.5 %collective-permute-start.24 = (bf16[288,256]{1,0:T(8,128)(2,1)S(1)}, bf16[288,256]{1,0:T(8,128)(2,1)S(1)}, u32[]{:S(2)}, u32[]{:S(2)}) collective-permute-start(bf16[288,256]{1,0:T(8,128)(2,1)S(1)} %get-tuple-element.33), channel_id=1, source_target_pairs={{0,16},{4,20},{8,24},{12,28},{16,0},{20,4},{24,8},{28,12},{1,17},{... | collective-permute-start | bytes 442376 | tf_op jit(solution)/shard_map/ppermute | solution.py:325
  79.2 1.1 collective-permute-done.23.refs_0_.refs_2_
  80.3 6.1 %collective-permute-done.24.refs_1_.refs_3_ = bf16[288,256]{1,0:T(8,128)(2,1)S(1)} collective-permute-done((bf16[288,256]{1,0:T(8,128)(2,1)S(1)}, bf16[288,256]{1,0:T(8,128)(2,1)S(1)}, u32[]{:S(2)}, u32[]{:S(2)}) %collective-permute-start.24) | collective-permute-done | bytes 147488 | tf_op jit(solution)/shard_map/ppermute | solution.py:325
  86.6 1.5 %collective-permute-start.26 = (bf16[288,384]{1,0:T(8,128)(2,1)S(1)}, bf16[288,384]{1,0:T(8,128)(2,1)S(1)}, u32[]{:S(2)}, u32[]{:S(2)}) collective-permute-start(bf16[288,384]{1,0:T(8,128)(2,1)S(1)} %get-tuple-element.35), channel_id=1, source_target_pairs={{0,8},{4,12},{8,0},{12,4},{16,24},{20,28},{24,16},{28,20},{1,9},{5... | collective-permute-start | bytes 663560 | tf_op jit(solution)/shard_map/ppermute | solution.py:325
  88.2 0.6 collective-permute-start.27
  88.8 1.4 %collective-permute-start.28 = (bf16[288,384]{1,0:T(8,128)(2,1)S(1)}, bf16[288,384]{1,0:T(8,128)(2,1)S(1)}, u32[]{:S(2)}, u32[]{:S(2)}) collective-permute-start(bf16[288,384]{1,0:T(8,128)(2,1)S(1)} %get-tuple-element.37), channel_id=1, source_target_pairs={{0,24},{4,28},{8,16},{12,20},{16,8},{20,12},{24,0},{28,4},{1,25},{... | collective-permute-start | bytes 663560 | tf_op jit(solution)/shard_map/ppermute | solution.py:325
  90.3 2.4 %collective-permute-start.35 = (bf16[288,256]{1,0:T(8,128)(2,1)S(1)}, bf16[288,256]{1,0:T(8,128)(2,1)S(1)}, u32[]{:S(2)}, u32[]{:S(2)}) collective-permute-start(bf16[288,256]{1,0:T(8,128)(2,1)S(1)} %shard_map.100.refs_4_.refs_0_), channel_id=1, source_target_pairs={{0,3},{1,2},{2,1},{3,0},{4,7},{5,6},{6,5},{7,4},{8,11},{9,10},{10,... | collective-permute-start | bytes 442376 | tf_op jit(solution)/shard_map/ppermute | solution.py:325
  92.6 1.4 %collective-permute-done.26.refs_2_ = bf16[288,384]{1,0:T(8,128)(2,1)S(1)} collective-permute-done((bf16[288,384]{1,0:T(8,128)(2,1)S(1)}, bf16[288,384]{1,0:T(8,128)(2,1)S(1)}, u32[]{:S(2)}, u32[]{:S(2)}) %collective-permute-start.26) | collective-permute-done | bytes 221216 | tf_op jit(solution)/shard_map/ppermute | solution.py:325
  94.1 0.7 collective-permute-start.33
  94.7 6.0 %collective-permute-done.27.refs_3_ = bf16[288,384]{1,0:T(8,128)(2,1)S(1)} collective-permute-done((bf16[288,384]{1,0:T(8,128)(2,1)S(1)}, bf16[288,384]{1,0:T(8,128)(2,1)S(1)}, u32[]{:S(2)}, u32[]{:S(2)}) %collective-permute-start.27) | collective-permute-done | bytes 221216 | tf_op jit(solution)/shard_map/ppermute | solution.py:325
  100.9 3.5 %collective-permute-done.34.refs_6_.refs_11_ = bf16[288,256]{1,0:T(8,128)(2,1)S(1)} collective-permute-done((bf16[288,256]{1,0:T(8,128)(2,1)S(1)}, bf16[288,256]{1,0:T(8,128)(2,1)S(1)}, u32[]{:S(2)}, u32[]{:S(2)}) %collective-permute-start.34) | collective-permute-done | bytes 147488 | tf_op jit(solution)/shard_map/ppermute | solution.py:325
  104.4 1.4 %shard_map.102 = (f32[144,288]{1,0:T(8,128)S(1)}, f32[3,144,288]{2,1,0:T(8,128)S(1)}, bf16[144,288]{1,0:T(8,128)(2,1)S(1)}, bf16[3,144,288]{2,1,0:T(8,128)(2,1)S(1)}) custom-call(s32[1]{0:T(128)} %bitcast.4.col_ref, s32[1]{0:T(128)} %bitcast.me_ref, bf16[288,256]{1,0:T(8,128)(2,1)S(1)} %shard_map.100.refs_4_.refs_0_, ...), custom_call_target="tpu_custom_call" | custom-call | tf_op jit(solution)/shard_map/pallas_call | solution.py:303
  105.9 2.1 %collective-permute-start.31 = (bf16[288,384]{1,0:T(8,128)(2,1)S(1)}, bf16[288,384]{1,0:T(8,128)(2,1)S(1)}, u32[]{:S(2)}, u32[]{:S(2)}) collective-permute-start(bf16[288,384]{1,0:T(8,128)(2,1)S(1)} %shard_map.99.refs_1_.refs_4_), channel_id=1, source_target_pairs={{0,3},{1,2},{2,1},{3,0},{4,7},{5,6},{6,5},{7,4},{8,11},{9,10},{10,... | collective-permute-start | bytes 663560 | tf_op jit(solution)/shard_map/ppermute | solution.py:325
  108.1 2.3 %collective-permute-start.29 = (bf16[288,384]{1,0:T(8,128)(2,1)S(1)}, bf16[288,384]{1,0:T(8,128)(2,1)S(1)}, u32[]{:S(2)}, u32[]{:S(2)}) collective-permute-start(bf16[288,384]{1,0:T(8,128)(2,1)S(1)} %shard_map.99.refs_1_.refs_4_), channel_id=1, source_target_pairs={{0,1},{1,0},{2,3},{3,2},{4,5},{5,4},{6,7},{7,6},{8,9},{9,8},{10,11... | collective-permute-start | bytes 663560 | tf_op jit(solution)/shard_map/ppermute | solution.py:325
  110.5 1.5 %collective-permute-start.38 = (bf16[144,288]{1,0:T(8,128)(2,1)S(1)}, bf16[144,288]{1,0:T(8,128)(2,1)S(1)}, u32[]{:S(2)}, u32[]{:S(2)}) collective-permute-start(bf16[144,288]{1,0:T(8,128)(2,1)S(1)} %get-tuple-element.44), channel_id=1, source_target_pairs={{0,8},{4,12},{8,0},{12,4},{16,24},{20,28},{24,16},{28,20},{1,9},{5... | collective-permute-start | bytes 248840 | tf_op jit(solution)/shard_map/ppermute | solution.py:325
  112.0 1.5 %collective-permute-start.39 = (bf16[144,288]{1,0:T(8,128)(2,1)S(1)}, bf16[144,288]{1,0:T(8,128)(2,1)S(1)}, u32[]{:S(2)}, u32[]{:S(2)}) collective-permute-start(bf16[144,288]{1,0:T(8,128)(2,1)S(1)} %get-tuple-element.45), channel_id=1, source_target_pairs={{0,16},{4,20},{8,24},{12,28},{16,0},{20,4},{24,8},{28,12},{1,17},{... | collective-permute-start | bytes 248840 | tf_op jit(solution)/shard_map/ppermute | solution.py:325
  113.5 2.5 %collective-permute-done.38.refs_2_ = bf16[144,288]{1,0:T(8,128)(2,1)S(1)} collective-permute-done((bf16[144,288]{1,0:T(8,128)(2,1)S(1)}, bf16[144,288]{1,0:T(8,128)(2,1)S(1)}, u32[]{:S(2)}, u32[]{:S(2)}) %collective-permute-start.38) | collective-permute-done | bytes 82976 | tf_op jit(solution)/shard_map/ppermute | solution.py:325
  116.0 1.5 %collective-permute-start.40 = (bf16[144,288]{1,0:T(8,128)(2,1)S(1)}, bf16[144,288]{1,0:T(8,128)(2,1)S(1)}, u32[]{:S(2)}, u32[]{:S(2)}) collective-permute-start(bf16[144,288]{1,0:T(8,128)(2,1)S(1)} %get-tuple-element.46), channel_id=1, source_target_pairs={{0,24},{4,28},{8,16},{12,20},{16,8},{20,12},{24,0},{28,4},{1,25},{... | collective-permute-start | bytes 248840 | tf_op jit(solution)/shard_map/ppermute | solution.py:325
  118.0 3.6 %collective-permute-done.40.refs_4_ = bf16[144,288]{1,0:T(8,128)(2,1)S(1)} collective-permute-done((bf16[144,288]{1,0:T(8,128)(2,1)S(1)}, bf16[144,288]{1,0:T(8,128)(2,1)S(1)}, u32[]{:S(2)}, u32[]{:S(2)}) %collective-permute-start.40) | collective-permute-done | bytes 82976 | tf_op jit(solution)/shard_map/ppermute | solution.py:325
  121.6 0.8 shard_map.104.refs_9_
  122.4 5.3 %collective-permute-done.30.refs_6_ = bf16[288,384]{1,0:T(8,128)(2,1)S(1)} collective-permute-done((bf16[288,384]{1,0:T(8,128)(2,1)S(1)}, bf16[288,384]{1,0:T(8,128)(2,1)S(1)}, u32[]{:S(2)}, u32[]{:S(2)}) %collective-permute-start.30) | collective-permute-done | bytes 221216 | tf_op jit(solution)/shard_map/ppermute | solution.py:325
  127.7 0.9 copy-done
  128.7 1.4 %shard_map.105 = bf16[288,640]{1,0:T(8,128)(2,1)} custom-call(bf16[288,288]{1,0:T(8,128)(2,1)S(1)} %get-tuple-element.52.refs_0_, bf16[288,288]{1,0:T(8,128)(2,1)S(1)} %get-tuple-element.48.refs_1_, bf16[288,288]{1,0:T(8,128)(2,1)S(1)} %get-tuple-element.53.refs_2_, bf16[288,288]{1,0:T(8,128)(2,1)S(1)} %get-tuple-element.47.refs_3_, ...), custom_call_target="tpu_custom_call" | custom-call | tf_op jit(solution)/shard_map/pallas_call | solution.py:196
  (79 shorter events, 3.7 us)
Async XLA Ops:
  1.6 10.5 %collective-permute-start.12 = (bf16[288,256]{1,0:T(8,128)(2,1)S(1)}, bf16[288,256]{1,0:T(8,128)(2,1)S(1)}, u32[]{:S(2)}, u32[]{:S(2)}) collective-permute-start(bf16[288,256]{1,0:T(8,128)(2,1)S(1)} %slice.9.refs_4_.refs_3_), channel_id=1, source_target_pairs={{0,3},{1,2},{2,1},{3,0},{4,7},{5,6},{6,5},{7,4},{8,11},{9,10},{10,... | collective-permute-start | bytes 442376 | tf_op jit(solution)/shard_map/ppermute | solution.py:325
  6.7 22.9 %collective-permute-start.11 = (bf16[288,256]{1,0:T(8,128)(2,1)S(1)}, bf16[288,256]{1,0:T(8,128)(2,1)S(1)}, u32[]{:S(2)}, u32[]{:S(2)}) collective-permute-start(bf16[288,256]{1,0:T(8,128)(2,1)S(1)} %slice.9.refs_4_.refs_3_), channel_id=1, source_target_pairs={{0,2},{1,3},{2,0},{3,1},{4,6},{5,7},{6,4},{7,5},{8,10},{9,11},{10,... | collective-permute-start | bytes 442376 | tf_op jit(solution)/shard_map/ppermute | solution.py:325
  6.7 22.9 %collective-permute-start.10 = (bf16[288,256]{1,0:T(8,128)(2,1)S(1)}, bf16[288,256]{1,0:T(8,128)(2,1)S(1)}, u32[]{:S(2)}, u32[]{:S(2)}) collective-permute-start(bf16[288,256]{1,0:T(8,128)(2,1)S(1)} %slice.9.refs_4_.refs_3_), channel_id=1, source_target_pairs={{0,1},{1,0},{2,3},{3,2},{4,5},{5,4},{6,7},{7,6},{8,9},{9,8},{10,11... | collective-permute-start | bytes 442376 | tf_op jit(solution)/shard_map/ppermute | solution.py:325
  8.3 24.4 %collective-permute-start.2 = (bf16[288,384]{1,0:T(8,128)(2,1)S(1)}, bf16[288,384]{1,0:T(8,128)(2,1)S(1)}, u32[]{:S(2)}, u32[]{:S(2)}) collective-permute-start(bf16[288,384]{1,0:T(8,128)(2,1)S(1)} %slice.8.refs_4_.refs_2_), channel_id=1, source_target_pairs={{0,3},{1,2},{2,1},{3,0},{4,7},{5,6},{6,5},{7,4},{8,11},{9,10},{10,... | collective-permute-start | bytes 663560 | tf_op jit(solution)/shard_map/ppermute | solution.py:325
  12.1 26.0 %collective-permute-start.1 = (bf16[288,384]{1,0:T(8,128)(2,1)S(1)}, bf16[288,384]{1,0:T(8,128)(2,1)S(1)}, u32[]{:S(2)}, u32[]{:S(2)}) collective-permute-start(bf16[288,384]{1,0:T(8,128)(2,1)S(1)} %slice.8.refs_4_.refs_2_), channel_id=1, source_target_pairs={{0,2},{1,3},{2,0},{3,1},{4,6},{5,7},{6,4},{7,5},{8,10},{9,11},{10,... | collective-permute-start | bytes 663560 | tf_op jit(solution)/shard_map/ppermute | solution.py:325
  12.1 42.0 %copy-start.5 = (s32[5,48]{1,0:T(8,128)S(1)}, s32[5,48]{1,0:T(8,128)}, u32[]{:S(2)}) copy-start(s32[5,48]{1,0:T(8,128)} %param.11) | copy-start | bytes 2884
  12.1 42.1 %copy-start.6 = (f32[288]{0:T(512)S(1)}, f32[288]{0:T(512)}, u32[]{:S(2)}) copy-start(f32[288]{0:T(512)} %param.9) | copy-start | bytes 3460
  12.1 27.5 %collective-permute-start = (bf16[288,384]{1,0:T(8,128)(2,1)S(1)}, bf16[288,384]{1,0:T(8,128)(2,1)S(1)}, u32[]{:S(2)}, u32[]{:S(2)}) collective-permute-start(bf16[288,384]{1,0:T(8,128)(2,1)S(1)} %slice.8.refs_4_.refs_2_), channel_id=1, source_target_pairs={{0,1},{1,0},{2,3},{3,2},{4,5},{5,4},{6,7},{7,6},{8,9},{9,8},{10,11... | collective-permute-start | bytes 663560 | tf_op jit(solution)/shard_map/ppermute | solution.py:325
  21.1 34.4 %copy-start.3 = (bf16[640,288]{0,1:T(8,128)(2,1)S(1)}, bf16[640,288]{0,1:T(8,128)(2,1)}, u32[]{:S(2)}) copy-start(bf16[640,288]{0,1:T(8,128)(2,1)} %param.13) | copy-start | bytes 1105924
  21.1 34.4 %copy-start.4 = (s32[5]{0:T(128)S(1)}, s32[5]{0:T(128)}, u32[]{:S(2)}) copy-start(s32[5]{0:T(128)} %counts_ref.1) | copy-start | bytes 64
  30.1 25.3 %copy-start.2 = (bf16[288,256]{1,0:T(8,128)(2,1)}, bf16[288,256]{1,0:T(8,128)(2,1)S(1)}, u32[]{:S(2)}) copy-start(bf16[288,256]{1,0:T(8,128)(2,1)S(1)} %shard_map.95.rest_8_) | copy-start | bytes 442372
  30.1 11.8 %collective-permute-start.16 = (bf16[288,256]{1,0:T(8,128)(2,1)S(1)}, bf16[288,256]{1,0:T(8,128)(2,1)S(1)}, u32[]{:S(2)}, u32[]{:S(2)}) collective-permute-start(bf16[288,256]{1,0:T(8,128)(2,1)S(1)} %shard_map.95.rest_8_), channel_id=1, source_target_pairs={{0,4},{4,0},{8,12},{12,8},{16,20},{20,16},{24,28},{28,24},{1,5},{5... | collective-permute-start | bytes 442376 | tf_op jit(solution)/shard_map/ppermute | solution.py:325
  30.2 12.2 %collective-permute-start.15 = (bf16[288,256]{1,0:T(8,128)(2,1)S(1)}, bf16[288,256]{1,0:T(8,128)(2,1)S(1)}, u32[]{:S(2)}, u32[]{:S(2)}) collective-permute-start(bf16[288,256]{1,0:T(8,128)(2,1)S(1)} %shard_map.95.rest_8_), channel_id=1, source_target_pairs={{0,24},{4,28},{8,16},{12,20},{16,8},{20,12},{24,0},{28,4},{1,25},{... | collective-permute-start | bytes 442376 | tf_op jit(solution)/shard_map/ppermute | solution.py:325
  32.7 11.2 %collective-permute-start.14 = (bf16[288,256]{1,0:T(8,128)(2,1)S(1)}, bf16[288,256]{1,0:T(8,128)(2,1)S(1)}, u32[]{:S(2)}, u32[]{:S(2)}) collective-permute-start(bf16[288,256]{1,0:T(8,128)(2,1)S(1)} %shard_map.95.rest_8_), channel_id=1, source_target_pairs={{0,16},{4,20},{8,24},{12,28},{16,0},{20,4},{24,8},{28,12},{1,17},{... | collective-permute-start | bytes 442376 | tf_op jit(solution)/shard_map/ppermute | solution.py:325
  38.1 5.8 %collective-permute-start.13 = (bf16[288,256]{1,0:T(8,128)(2,1)S(1)}, bf16[288,256]{1,0:T(8,128)(2,1)}, u32[]{:S(2)}, u32[]{:S(2)}) collective-permute-start(bf16[288,256]{1,0:T(8,128)(2,1)S(1)} %shard_map.95.rest_8_), channel_id=1, source_target_pairs={{0,8},{4,12},{8,0},{12,4},{16,24},{20,28},{24,16},{28,20},{1,9},{5... | collective-permute-start | bytes 442376 | tf_op jit(solution)/shard_map/ppermute | solution.py:325
  40.4 15.1 %copy-start.1 = (bf16[288,384]{1,0:T(8,128)(2,1)}, bf16[288,384]{1,0:T(8,128)(2,1)S(1)}, u32[]{:S(2)}) copy-start(bf16[288,384]{1,0:T(8,128)(2,1)S(1)} %shard_map.94.rest_0_) | copy-start | bytes 663556
  40.4 10.0 %collective-permute-start.5 = (bf16[288,384]{1,0:T(8,128)(2,1)S(1)}, bf16[288,384]{1,0:T(8,128)(2,1)S(1)}, u32[]{:S(2)}, u32[]{:S(2)}) collective-permute-start(bf16[288,384]{1,0:T(8,128)(2,1)S(1)} %shard_map.94.rest_0_), channel_id=1, source_target_pairs={{0,24},{4,28},{8,16},{12,20},{16,8},{20,12},{24,0},{28,4},{1,25},{... | collective-permute-start | bytes 663560 | tf_op jit(solution)/shard_map/ppermute | solution.py:325
  41.9 11.0 %copy-start.9 = (bf16[288,256]{1,0:T(8,128)(2,1)}, bf16[288,256]{1,0:T(8,128)(2,1)S(1)}, u32[]{:S(2)}) copy-start(bf16[288,256]{1,0:T(8,128)(2,1)S(1)} %collective-permute-done.16.rest_12_) | copy-start | bytes 442372
  41.9 10.5 %collective-permute-start.4 = (bf16[288,384]{1,0:T(8,128)(2,1)S(1)}, bf16[288,384]{1,0:T(8,128)(2,1)S(1)}, u32[]{:S(2)}, u32[]{:S(2)}) collective-permute-start(bf16[288,384]{1,0:T(8,128)(2,1)S(1)} %shard_map.94.rest_0_), channel_id=1, source_target_pairs={{0,16},{4,20},{8,24},{12,28},{16,0},{20,4},{24,8},{28,12},{1,17},{... | collective-permute-start | bytes 663560 | tf_op jit(solution)/shard_map/ppermute | solution.py:325
  42.4 10.4 %collective-permute-start.3 = (bf16[288,384]{1,0:T(8,128)(2,1)S(1)}, bf16[288,384]{1,0:T(8,128)(2,1)}, u32[]{:S(2)}, u32[]{:S(2)}) collective-permute-start(bf16[288,384]{1,0:T(8,128)(2,1)S(1)} %shard_map.94.rest_0_), channel_id=1, source_target_pairs={{0,8},{4,12},{8,0},{12,4},{16,24},{20,28},{24,16},{28,20},{1,9},{5... | collective-permute-start | bytes 663560 | tf_op jit(solution)/shard_map/ppermute | solution.py:325
  43.9 1.4 %collective-permute-start.19 = (bf16[288,256]{1,0:T(8,128)(2,1)S(1)}, bf16[288,256]{1,0:T(8,128)(2,1)S(1)}, u32[]{:S(2)}, u32[]{:S(2)}) collective-permute-start(bf16[288,256]{1,0:T(8,128)(2,1)S(1)} %collective-permute-done.15.rest_11_), channel_id=1, source_target_pairs={{0,4},{4,0},{8,12},{12,8},{16,20},{20,16},{24,28},{28,24},{1,5},{5... | collective-permute-start | bytes 442376 | tf_op jit(solution)/shard_map/ppermute | solution.py:325
  44.0 9.0 %collective-permute-start.18 = (bf16[288,256]{1,0:T(8,128)(2,1)S(1)}, bf16[288,256]{1,0:T(8,128)(2,1)S(1)}, u32[]{:S(2)}, u32[]{:S(2)}) collective-permute-start(bf16[288,256]{1,0:T(8,128)(2,1)S(1)} %collective-permute-done.14.rest_10_), channel_id=1, source_target_pairs={{0,4},{4,0},{8,12},{12,8},{16,20},{20,16},{24,28},{28,24},{1,5},{5... | collective-permute-start | bytes 442376 | tf_op jit(solution)/shard_map/ppermute | solution.py:325
  45.3 10.1 %collective-permute-start.6 = (bf16[288,384]{1,0:T(8,128)(2,1)S(1)}, bf16[288,384]{1,0:T(8,128)(2,1)}, u32[]{:S(2)}, u32[]{:S(2)}) collective-permute-start(bf16[288,384]{1,0:T(8,128)(2,1)S(1)} %shard_map.94.rest_0_), channel_id=1, source_target_pairs={{0,4},{4,0},{8,12},{12,8},{16,20},{20,16},{24,28},{28,24},{1,5},{5... | collective-permute-start | bytes 663560 | tf_op jit(solution)/shard_map/ppermute | solution.py:325
  50.4 5.0 %collective-permute-start.9 = (bf16[288,384]{1,0:T(8,128)(2,1)S(1)}, bf16[288,384]{1,0:T(8,128)(2,1)}, u32[]{:S(2)}, u32[]{:S(2)}) collective-permute-start(bf16[288,384]{1,0:T(8,128)(2,1)S(1)} %collective-permute-done.5.rest_3_), channel_id=1, source_target_pairs={{0,4},{4,0},{8,12},{12,8},{16,20},{20,16},{24,28},{28,24},{1,5},{5... | collective-permute-start | bytes 663560 | tf_op jit(solution)/shard_map/ppermute | solution.py:325
  52.4 3.0 %collective-permute-start.8 = (bf16[288,384]{1,0:T(8,128)(2,1)S(1)}, bf16[288,384]{1,0:T(8,128)(2,1)}, u32[]{:S(2)}, u32[]{:S(2)}) collective-permute-start(bf16[288,384]{1,0:T(8,128)(2,1)S(1)} %collective-permute-done.4.rest_2_), channel_id=1, source_target_pairs={{0,4},{4,0},{8,12},{12,8},{16,20},{20,16},{24,28},{28,24},{1,5},{5... | collective-permute-start | bytes 663560 | tf_op jit(solution)/shard_map/ppermute | solution.py:325
  52.9 2.6 %collective-permute-start.7 = (bf16[288,384]{1,0:T(8,128)(2,1)}, bf16[288,384]{1,0:T(8,128)(2,1)}, u32[]{:S(2)}, u32[]{:S(2)}) collective-permute-start(bf16[288,384]{1,0:T(8,128)(2,1)} %collective-permute-done.3.rest_1_), channel_id=1, source_target_pairs={{0,4},{4,0},{8,12},{12,8},{16,20},{20,16},{24,28},{28,24},{1,5},{5... | collective-permute-start | bytes 663560 | tf_op jit(solution)/shard_map/ppermute | solution.py:325
  53.6 1.8 %collective-permute-start.17 = (bf16[288,256]{1,0:T(8,128)(2,1)}, bf16[288,256]{1,0:T(8,128)(2,1)}, u32[]{:S(2)}, u32[]{:S(2)}) collective-permute-start(bf16[288,256]{1,0:T(8,128)(2,1)} %collective-permute-done.13.rest_9_), channel_id=1, source_target_pairs={{0,4},{4,0},{8,12},{12,8},{16,20},{20,16},{24,28},{28,24},{1,5},{5... | collective-permute-start | bytes 442376 | tf_op jit(solution)/shard_map/ppermute | solution.py:325
  66.5 20.0 %collective-permute-start.21 = (bf16[3,288,384]{2,1,0:T(8,128)(2,1)S(1)}, bf16[3,288,384]{2,1,0:T(8,128)(2,1)S(1)}, u32[]{:S(2)}, u32[]{:S(2)}) collective-permute-start(bf16[3,288,384]{2,1,0:T(8,128)(2,1)S(1)} %get-tuple-element.29), channel_id=1, source_target_pairs={{0,4},{4,0},{8,12},{12,8},{16,20},{20,16},{24,28},{28,24},{1,5},{5... | collective-permute-start | bytes 1990664 | tf_op jit(solution)/shard_map/ppermute | solution.py:325
  71.6 2.4 %collective-permute-start.22 = (bf16[3,288,256]{2,1,0:T(8,128)(2,1)S(1)}, bf16[3,288,256]{2,1,0:T(8,128)(2,1)S(1)}, u32[]{:S(2)}, u32[]{:S(2)}) collective-permute-start(bf16[3,288,256]{2,1,0:T(8,128)(2,1)S(1)} %get-tuple-element.31), channel_id=1, source_target_pairs={{0,4},{4,0},{8,12},{12,8},{16,20},{20,16},{24,28},{28,24},{1,5},{5... | collective-permute-start | bytes 1327112 | tf_op jit(solution)/shard_map/ppermute | solution.py:325
  74.1 6.2 %collective-permute-start.23 = (bf16[288,256]{1,0:T(8,128)(2,1)S(1)}, bf16[288,256]{1,0:T(8,128)(2,1)S(1)}, u32[]{:S(2)}, u32[]{:S(2)}) collective-permute-start(bf16[288,256]{1,0:T(8,128)(2,1)S(1)} %get-tuple-element.32), channel_id=1, source_target_pairs={{0,8},{4,12},{8,0},{12,4},{16,24},{20,28},{24,16},{28,20},{1,9},{5... | collective-permute-start | bytes 442376 | tf_op jit(solution)/shard_map/ppermute | solution.py:325
  75.7 10.8 %collective-permute-start.24 = (bf16[288,256]{1,0:T(8,128)(2,1)S(1)}, bf16[288,256]{1,0:T(8,128)(2,1)S(1)}, u32[]{:S(2)}, u32[]{:S(2)}) collective-permute-start(bf16[288,256]{1,0:T(8,128)(2,1)S(1)} %get-tuple-element.33), channel_id=1, source_target_pairs={{0,16},{4,20},{8,24},{12,28},{16,0},{20,4},{24,8},{28,12},{1,17},{... | collective-permute-start | bytes 442376 | tf_op jit(solution)/shard_map/ppermute | solution.py:325
  79.2 7.3 %collective-permute-start.25 = (bf16[288,256]{1,0:T(8,128)(2,1)S(1)}, bf16[288,256]{1,0:T(8,128)(2,1)S(1)}, u32[]{:S(2)}, u32[]{:S(2)}) collective-permute-start(bf16[288,256]{1,0:T(8,128)(2,1)S(1)} %get-tuple-element.34), channel_id=1, source_target_pairs={{0,24},{4,28},{8,16},{12,20},{16,8},{20,12},{24,0},{28,4},{1,25},{... | collective-permute-start | bytes 442376 | tf_op jit(solution)/shard_map/ppermute | solution.py:325
  79.2 13.4 %collective-permute-start.20 = (bf16[288,384]{1,0:T(8,128)(2,1)S(1)}, bf16[288,384]{1,0:T(8,128)(2,1)S(1)}, u32[]{:S(2)}, u32[]{:S(2)}) collective-permute-start(bf16[288,384]{1,0:T(8,128)(2,1)S(1)} %get-tuple-element.27), channel_id=1, source_target_pairs={{0,4},{4,0},{8,12},{12,8},{16,20},{20,16},{24,28},{28,24},{1,5},{5... | collective-permute-start | bytes 663560 | tf_op jit(solution)/shard_map/ppermute | solution.py:325
  86.6 7.5 %collective-permute-start.26 = (bf16[288,384]{1,0:T(8,128)(2,1)S(1)}, bf16[288,384]{1,0:T(8,128)(2,1)S(1)}, u32[]{:S(2)}, u32[]{:S(2)}) collective-permute-start(bf16[288,384]{1,0:T(8,128)(2,1)S(1)} %get-tuple-element.35), channel_id=1, source_target_pairs={{0,8},{4,12},{8,0},{12,4},{16,24},{20,28},{24,16},{28,20},{1,9},{5... | collective-permute-start | bytes 663560 | tf_op jit(solution)/shard_map/ppermute | solution.py:325
  88.1 2.0 %collective-permute-start.32 = (bf16[288,256]{1,0:T(8,128)(2,1)S(1)}, bf16[288,256]{1,0:T(8,128)(2,1)S(1)}, u32[]{:S(2)}, u32[]{:S(2)}) collective-permute-start(bf16[288,256]{1,0:T(8,128)(2,1)S(1)} %get-tuple-element.39), channel_id=1, source_target_pairs={{0,4},{4,0},{8,12},{12,8},{16,20},{20,16},{24,28},{28,24},{1,5},{5... | collective-permute-start | bytes 442376 | tf_op jit(solution)/shard_map/ppermute | solution.py:325
  88.2 12.6 %collective-permute-start.27 = (bf16[288,384]{1,0:T(8,128)(2,1)S(1)}, bf16[288,384]{1,0:T(8,128)(2,1)S(1)}, u32[]{:S(2)}, u32[]{:S(2)}) collective-permute-start(bf16[288,384]{1,0:T(8,128)(2,1)S(1)} %get-tuple-element.36), channel_id=1, source_target_pairs={{0,16},{4,20},{8,24},{12,28},{16,0},{20,4},{24,8},{28,12},{1,17},{... | collective-permute-start | bytes 663560 | tf_op jit(solution)/shard_map/ppermute | solution.py:325
  88.8 11.9 %collective-permute-start.28 = (bf16[288,384]{1,0:T(8,128)(2,1)S(1)}, bf16[288,384]{1,0:T(8,128)(2,1)S(1)}, u32[]{:S(2)}, u32[]{:S(2)}) collective-permute-start(bf16[288,384]{1,0:T(8,128)(2,1)S(1)} %get-tuple-element.37), channel_id=1, source_target_pairs={{0,24},{4,28},{8,16},{12,20},{16,8},{20,12},{24,0},{28,4},{1,25},{... | collective-permute-start | bytes 663560 | tf_op jit(solution)/shard_map/ppermute | solution.py:325
  90.3 10.6 %collective-permute-start.35 = (bf16[288,256]{1,0:T(8,128)(2,1)S(1)}, bf16[288,256]{1,0:T(8,128)(2,1)S(1)}, u32[]{:S(2)}, u32[]{:S(2)}) collective-permute-start(bf16[288,256]{1,0:T(8,128)(2,1)S(1)} %shard_map.100.refs_4_.refs_0_), channel_id=1, source_target_pairs={{0,3},{1,2},{2,1},{3,0},{4,7},{5,6},{6,5},{7,4},{8,11},{9,10},{10,... | collective-permute-start | bytes 442376 | tf_op jit(solution)/shard_map/ppermute | solution.py:325
  92.6 11.8 %collective-permute-start.34 = (bf16[288,256]{1,0:T(8,128)(2,1)S(1)}, bf16[288,256]{1,0:T(8,128)(2,1)S(1)}, u32[]{:S(2)}, u32[]{:S(2)}) collective-permute-start(bf16[288,256]{1,0:T(8,128)(2,1)S(1)} %shard_map.100.refs_4_.refs_0_), channel_id=1, source_target_pairs={{0,2},{1,3},{2,0},{3,1},{4,6},{5,7},{6,4},{7,5},{8,10},{9,11},{10,... | collective-permute-start | bytes 442376 | tf_op jit(solution)/shard_map/ppermute | solution.py:325
  94.1 10.4 %collective-permute-start.33 = (bf16[288,256]{1,0:T(8,128)(2,1)S(1)}, bf16[288,256]{1,0:T(8,128)(2,1)S(1)}, u32[]{:S(2)}, u32[]{:S(2)}) collective-permute-start(bf16[288,256]{1,0:T(8,128)(2,1)S(1)} %shard_map.100.refs_4_.refs_0_), channel_id=1, source_target_pairs={{0,1},{1,0},{2,3},{3,2},{4,5},{5,4},{6,7},{7,6},{8,9},{9,8},{10,11... | collective-permute-start | bytes 442376 | tf_op jit(solution)/shard_map/ppermute | solution.py:325
  105.9 4.5 %collective-permute-start.37 = (bf16[3,144,288]{2,1,0:T(8,128)(2,1)S(1)}, bf16[3,144,288]{2,1,0:T(8,128)(2,1)S(1)}, u32[]{:S(2)}, u32[]{:S(2)}) collective-permute-start(bf16[3,144,288]{2,1,0:T(8,128)(2,1)S(1)} %get-tuple-element.43), channel_id=1, source_target_pairs={{0,4},{4,0},{8,12},{12,8},{16,20},{20,16},{24,28},{28,24},{1,5},{5... | collective-permute-start | bytes 746504 | tf_op jit(solution)/shard_map/ppermute | solution.py:325
  105.9 16.5 %collective-permute-start.31 = (bf16[288,384]{1,0:T(8,128)(2,1)S(1)}, bf16[288,384]{1,0:T(8,128)(2,1)S(1)}, u32[]{:S(2)}, u32[]{:S(2)}) collective-permute-start(bf16[288,384]{1,0:T(8,128)(2,1)S(1)} %shard_map.99.refs_1_.refs_4_), channel_id=1, source_target_pairs={{0,3},{1,2},{2,1},{3,0},{4,7},{5,6},{6,5},{7,4},{8,11},{9,10},{10,... | collective-permute-start | bytes 663560 | tf_op jit(solution)/shard_map/ppermute | solution.py:325
  108.1 19.7 %collective-permute-start.30 = (bf16[288,384]{1,0:T(8,128)(2,1)S(1)}, bf16[288,384]{1,0:T(8,128)(2,1)S(1)}, u32[]{:S(2)}, u32[]{:S(2)}) collective-permute-start(bf16[288,384]{1,0:T(8,128)(2,1)S(1)} %shard_map.99.refs_1_.refs_4_), channel_id=1, source_target_pairs={{0,2},{1,3},{2,0},{3,1},{4,6},{5,7},{6,4},{7,5},{8,10},{9,11},{10,... | collective-permute-start | bytes 663560 | tf_op jit(solution)/shard_map/ppermute | solution.py:325
  108.1 19.7 %collective-permute-start.29 = (bf16[288,384]{1,0:T(8,128)(2,1)S(1)}, bf16[288,384]{1,0:T(8,128)(2,1)S(1)}, u32[]{:S(2)}, u32[]{:S(2)}) collective-permute-start(bf16[288,384]{1,0:T(8,128)(2,1)S(1)} %shard_map.99.refs_1_.refs_4_), channel_id=1, source_target_pairs={{0,1},{1,0},{2,3},{3,2},{4,5},{5,4},{6,7},{7,6},{8,9},{9,8},{10,11... | collective-permute-start | bytes 663560 | tf_op jit(solution)/shard_map/ppermute | solution.py:325
  110.4 1.6 %collective-permute-start.36 = (bf16[144,288]{1,0:T(8,128)(2,1)S(1)}, bf16[144,288]{1,0:T(8,128)(2,1)S(1)}, u32[]{:S(2)}, u32[]{:S(2)}) collective-permute-start(bf16[144,288]{1,0:T(8,128)(2,1)S(1)} %get-tuple-element.41), channel_id=1, source_target_pairs={{0,4},{4,0},{8,12},{12,8},{16,20},{20,16},{24,28},{28,24},{1,5},{5... | collective-permute-start | bytes 248840 | tf_op jit(solution)/shard_map/ppermute | solution.py:325
  110.5 5.5 %collective-permute-start.38 = (bf16[144,288]{1,0:T(8,128)(2,1)S(1)}, bf16[144,288]{1,0:T(8,128)(2,1)S(1)}, u32[]{:S(2)}, u32[]{:S(2)}) collective-permute-start(bf16[144,288]{1,0:T(8,128)(2,1)S(1)} %get-tuple-element.44), channel_id=1, source_target_pairs={{0,8},{4,12},{8,0},{12,4},{16,24},{20,28},{24,16},{28,20},{1,9},{5... | collective-permute-start | bytes 248840 | tf_op jit(solution)/shard_map/ppermute | solution.py:325
  112.0 6.0 %collective-permute-start.39 = (bf16[144,288]{1,0:T(8,128)(2,1)S(1)}, bf16[144,288]{1,0:T(8,128)(2,1)S(1)}, u32[]{:S(2)}, u32[]{:S(2)}) collective-permute-start(bf16[144,288]{1,0:T(8,128)(2,1)S(1)} %get-tuple-element.45), channel_id=1, source_target_pairs={{0,16},{4,20},{8,24},{12,28},{16,0},{20,4},{24,8},{28,12},{1,17},{... | collective-permute-start | bytes 248840 | tf_op jit(solution)/shard_map/ppermute | solution.py:325
  116.0 5.6 %collective-permute-start.40 = (bf16[144,288]{1,0:T(8,128)(2,1)S(1)}, bf16[144,288]{1,0:T(8,128)(2,1)S(1)}, u32[]{:S(2)}, u32[]{:S(2)}) collective-permute-start(bf16[144,288]{1,0:T(8,128)(2,1)S(1)} %get-tuple-element.46), channel_id=1, source_target_pairs={{0,24},{4,28},{8,16},{12,20},{16,8},{20,12},{24,0},{28,4},{1,25},{... | collective-permute-start | bytes 248840 | tf_op jit(solution)/shard_map/ppermute | solution.py:325
  (7 other events, 36.9 us)

commit v4 on v3

--- a/solution.py
+++ b/solution.py
@@ -25,6 +25,8 @@
     shard_order,
     gathers,
     scatters,
+    places,
+    inputs,
     coords_ref,
     counts_ref,
     me_ref,
@@ -34,8 +36,7 @@
     *rest,
 ):
     shards, block_count = len(shard_order), sum(gathers)
-    hidden_refs, rest = rest[: shards * len(gathers)], rest[shards * len(gathers) :]
-    act_ref, *part_refs = rest[:-5]
+    hidden_refs, act_ref, part_refs = rest[:inputs], rest[inputs], rest[inputs + 1 : -5]
     tiles, hidden, partial, tile_sems, hidden_sems = rest[-5:]
     groups = slots // group
     me = me_ref[0]
@@ -46,6 +47,10 @@
         return pltpu.make_async_copy(
             tiles_ref.at[i, span], tiles.at[i, span], tile_sems.at[i, q]
         )
+
+    def source(c, s):
+        place, entry = places[c][s]
+        return hidden_refs[place] if entry is None else hidden_refs[place].at[entry]
 
     hidden_copies = []
     for s in range(shards):
@@ -55,7 +60,7 @@
             for b in range(count):
                 hidden_copies.append(
                     pltpu.make_async_copy(
-                        hidden_refs[c * shards + s].at[:, pl.ds(b * tile, tile)],
+                        source(c, s).at[:, pl.ds(b * tile, tile)],
                         hidden.at[owner * block_count + block],
                         hidden_sems.at[s, block],
                     )
@@ -123,10 +128,8 @@
     half = shards // 2
     first = 0
     for c, count in enumerate(scatters):
-        keep_own, keep, send_own, send = part_refs[4 * c : 4 * c + 4]
         for s in range(shards):
-            own, others = (keep_own, keep) if s < half else (send_own, send)
-            out_ref = own if s % half == 0 else others.at[s % half - 1]
+            out_ref = part_refs[2 * c + s // half].at[s % half]
             owner = me ^ shard_order[s]
             for b in range(count):
                 value = partial[owner * block_count + first + b].astype(BF16)
@@ -148,12 +151,19 @@
     flops = 4 * block_count * slots * tile * tile * width
     parts = []
     for count in scatters:
-        own = jax.ShapeDtypeStruct((width, count * tile), BF16)
-        others = jax.ShapeDtypeStruct((max(shards // 2 - 1, 1), width, count * tile), BF16)
-        parts += [own, others] * 2
-    flat = [v for chunk in hidden for v in chunk]
+        parts += [jax.ShapeDtypeStruct((shards // 2, width, count * tile), BF16)] * 2
+    flat, places = [], []
+    for chunk in hidden:
+        entries = []
+        for value in chunk:
+            inner = [None] if value.ndim == 2 else range(value.shape[0])
+            entries += [(len(flat), entry) for entry in inner]
+            flat.append(value)
+        places.append(entries)
     return pl.pallas_call(
-        functools.partial(tile_kernel, slots, tile, group, shard_order, gathers, scatters),
+        functools.partial(
+            tile_kernel, slots, tile, group, shard_order, gathers, scatters, places, len(flat)
+        ),
         out_shape=(jax.ShapeDtypeStruct((width, rows_dev), BF16), *parts),
         in_specs=[smem, smem, smem, vmem, vmem, hbm] + [hbm] * len(flat),
         out_specs=(vmem,) * (1 + len(parts)),
@@ -226,24 +236,35 @@
     return small_call(kernel, out, (*lefts, *rights, *before), after, False)
 
 
+def pack(values):
+    out = jax.ShapeDtypeStruct((len(values),) + values[0].shape, values[0].dtype)
+
+    def kernel(*refs):
+        for j, ref in enumerate(refs[:-1]):
+            refs[-1][j] = ref[...]
+
+    return small_call(kernel, out, values, (), False)
+
+
 def add_up(values, dtype, after=()):
     number = len(values)
 
     def kernel(*refs):
-        total = refs[0][...].astype(F32)
-        for ref in refs[1:number]:
-            total = total + ref[...].astype(F32)
+        total = None
+        for ref in refs[:number]:
+            value = (ref[0] if len(ref.shape) == 3 else ref[...]).astype(F32)
+            total = value if total is None else total + value
         refs[-1][...] = total.astype(dtype)
 
-    out = jax.ShapeDtypeStruct(values[0].shape, dtype)
+    out = jax.ShapeDtypeStruct(values[0].shape[-2:], dtype)
     return small_call(kernel, out, values, after)
 
 
 def chip_sums(keep, got, after=()):
-    number = keep.shape[0]
+    number = keep.shape[0] - 1
 
     def kernel(keep_ref, got_ref, *refs):
-        for j, out_ref in enumerate(refs[len(after) :]):
+        for j, out_ref in enumerate(refs[len(after) :], 1):
             out_ref[...] = (keep_ref[j].astype(F32) + got_ref[j].astype(F32)).astype(BF16)
 
     out = (jax.ShapeDtypeStruct(keep.shape[1:], BF16),) * number
@@ -261,7 +282,7 @@
 
     def kernel(col_ref, me_ref, *refs):
         inputs = refs[: len(values)]
-        own_ref, keep_ref, send_own_ref, send_ref, grad, xs, part, sems = refs[-8:]
+        keep_ref, send_ref, grad, xs, part, sems = refs[-6:]
         copies = []
 
         def fill(target, sources, first_sem):
@@ -288,28 +309,21 @@
         for j, k in enumerate(rows_order):
             start = pl.multiple_of((me_ref[0] ^ k) * rows_out, 8)
             value = part[pl.ds(start, rows_out), :]
-            if j == 0:
-                own_ref[...] = value
-            elif j < half:
-                keep_ref[j - 1] = value
-            elif j == half:
-                send_own_ref[...] = value.astype(BF16)
+            if j < half:
+                keep_ref[j] = value
             else:
-                send_ref[j - half - 1] = value.astype(BF16)
+                send_ref[j - half] = value.astype(BF16)
 
     touched = 2 * width * rows_dev * (len(cols_order) + 1) + 8 * width * width * len(cols_order)
     smem = pl.BlockSpec(memory_space=pltpu.SMEM)
-    others = max(half - 1, 1)
     return pl.pallas_call(
         kernel,
         out_shape=(
-            jax.ShapeDtypeStruct((rows_out, width), F32),
-            jax.ShapeDtypeStruct((others, rows_out, width), F32),
-            jax.ShapeDtypeStruct((rows_out, width), BF16),
-            jax.ShapeDtypeStruct((others, rows_out, width), BF16),
+            jax.ShapeDtypeStruct((half, rows_out, width), F32),
+            jax.ShapeDtypeStruct((half, rows_out, width), BF16),
         ),
         in_specs=[smem, smem] + [ANY] * (len(values) + len(after)),
-        out_specs=(VMEM,) * 4,
+        out_specs=(VMEM,) * 2,
         scratch_shapes=[
             pltpu.VMEM((width, rows_dev), BF16),
             pltpu.VMEM((len(cols_order), width, rows_dev), BF16),
@@ -376,14 +390,14 @@
 
     grads, arrived, input_grad = [], (), ()
     for c in range(len(scatters)):
-        keep_own, keep, send_own, send = part[4 * c : 4 * c + 4]
-        got, got_own = swap(send, "rows", 1), swap(send_own, "rows", 1)
+        keep, send = part[2 * c : 2 * c + 2]
+        got = swap(send, "rows", 1)
         sums = chip_sums(keep, got, arrived)
         arrived = tuple(swap(v, "rows", k) for v, k in zip(sums, chips[1:]))
-        grad = add_up((keep_own, got_own, *arrived), BF16)
+        grad = add_up((keep, got, *arrived), BF16)
         grads.append([grad] + [swap(grad, "cols", k) for k in cols_order[1:]])
 
-    own, keep, send_own, send = weight_parts(
+    keep, send = weight_parts(
         1.0 / math.sqrt(rows_dev * n_rows),
         cols_order,
         order,
@@ -393,10 +407,9 @@
         list(zip(*x_parts)),
         tuple(grads[0][1:]) if len(grads) > 1 else (),
     )
-    got, got_own = swap(send, "rows", 1), swap(send_own, "rows", 1)
-    weight_grad = add_up(
-        (own, got_own, *[swap(v, "rows", k) for v, k in zip(chip_sums(keep, got), chips[1:])]), F32
-    )
+    got = swap(send, "rows", 1)
+    sums = chip_sums(keep, got)
+    weight_grad = add_up((keep, got, *[swap(v, "rows", k) for v, k in zip(sums, chips[1:])]), F32)
 
     for c, values in enumerate(grads):
         last = (weight_grad,) if c + 1 == len(grads) else ()
@@ -417,7 +430,7 @@
     hidden = contract_first(w_cols, x_full).astype(BF16)
     all_hidden = lax.all_gather(hidden, "rows", axis=0)
     order = tuple(range(n_rows))
-    act, keep_own, keep, send_own, send = tile_products(
+    act, keep, send = tile_products(
         order,
         (tile_values.shape[0],),
         (tile_values.shape[0],),
@@ -429,7 +442,7 @@
         cotangent.T,
         tile_values,
     )
-    part = jnp.concatenate([keep_own[None], keep, send_own[None], send], axis=0)
+    part = jnp.concatenate([keep, send], axis=0)
     grad_hidden = lax.psum_scatter(part, "rows", scatter_dimension=0, tiled=False)
     w_rows = lax.dynamic_slice_in_dim(weight, col_start, col_width, 0)
     grad_full = lax.all_gather(grad_hidden, "cols", axis=0, tiled=True)

time: 131 us -> 129 us (0.985); the launches traced: 130 us -> 127 us
  starting transfers between devices: 51 us -> 44.9 us
  Pallas kernels: 16.8 us -> 19.3 us
    ppermute x41 -> x38, starting transfers between devices: 51 us -> 44.9 us  [swap(): lax.ppermute(value, axis, [(i, i ^ k) for i in range(lax.axis_size(axis))])]
    pallas_call x1, Pallas kernels: 11 us -> 13.4 us  [tile_products(): pl.pallas_call(functools.partial(tile_kernel, slots, tile, group, shard_o...]
    ppermute x41 -> x38, waiting for transfers between devices: 54.9 us -> 55.3 us  [swap(): lax.ppermute(value, axis, [(i, i ^ k) for i in range(lax.axis_size(axis))])]
  transfers between devices with their start and end apart: 41 -> 38, of which waited for: 16 -> 16; matrix products, arithmetic and copies ran while one was open for 3% -> 3% of each run, Pallas kernels for 2% -> 2%
where the time goes in v4:
time: 129 us; the launch traced here: 127 us
  waiting for transfers between devices  55.3 us (43%)
  starting transfers between devices  44.9 us (35%)
  Pallas kernels  19.3 us (15%)
  local copies, waits for them, and re-layouts  6.4 us (5%)
    ppermute x38, waiting for transfers between devices, swap(): lax.ppermute(value, axis, [(i, i ^ k) for i in range(lax.axis_size(axis))])  55.3 us
    ppermute x38, starting transfers between devices, swap(): lax.ppermute(value, axis, [(i, i ^ k) for i in range(lax.axis_size(axis))])  44.9 us
    pallas_call x1, Pallas kernels, tile_products(): pl.pallas_call(functools.partial(tile_kernel, slots, tile, group, shard_o...  13.4 us
    pallas_call x10, Pallas kernels, small_call(): pl.pallas_call(kernel, out_shape=out_shape, in_specs=[VMEM] * len(values)...  4.5 us
    dynamic_slice x1, local copies, waits for them, and re-layouts, local(): lax.dynamic_slice(weight, (col * width, (col ^ k) * width), (width, width))  2.7 us
  transfers between devices with their start and end apart: 38, of which 16 were waited for; matrix products, arithmetic and copies ran while one was open for 3% of the time, Pallas kernels for 2%

profile of v4, /device:TPU:0, one launch (start us, length us, event | category | flops | bytes accessed | tf_op | source)
XLA Modules:
  0.0 126.8 jit_solution(10989616905959293543)
XLA Ops:
  0.6 0.9 slice.9.refs_4_.refs_3_
  1.6 5.1 %collective-permute-start.12 = (bf16[288,256]{1,0:T(8,128)(2,1)S(1)}, bf16[288,256]{1,0:T(8,128)(2,1)S(1)}, u32[]{:S(2)}, u32[]{:S(2)}) collective-permute-start(bf16[288,256]{1,0:T(8,128)(2,1)S(1)} %slice.9.refs_4_.refs_3_), channel_id=1, source_target_pairs={{0,3},{1,2},{2,1},{3,0},{4,7},{5,6},{6,5},{7,4},{8,11},{9,10},{10,... | collective-permute-start | bytes 442376 | tf_op jit(solution)/shard_map/ppermute | solution.py:339
  6.7 0.6 collective-permute-start.10
  7.3 1.0 slice.8.refs_4_.refs_2_
  8.3 3.8 %collective-permute-start.2 = (bf16[288,384]{1,0:T(8,128)(2,1)S(1)}, bf16[288,384]{1,0:T(8,128)(2,1)S(1)}, u32[]{:S(2)}, u32[]{:S(2)}) collective-permute-start(bf16[288,384]{1,0:T(8,128)(2,1)S(1)} %slice.8.refs_4_.refs_2_), channel_id=1, source_target_pairs={{0,3},{1,2},{2,1},{3,0},{4,7},{5,6},{6,5},{7,4},{8,11},{9,10},{10,... | collective-permute-start | bytes 663560 | tf_op jit(solution)/shard_map/ppermute | solution.py:339
  12.1 6.3 %collective-permute-start = (bf16[288,384]{1,0:T(8,128)(2,1)S(1)}, bf16[288,384]{1,0:T(8,128)(2,1)S(1)}, u32[]{:S(2)}, u32[]{:S(2)}) collective-permute-start(bf16[288,384]{1,0:T(8,128)(2,1)S(1)} %slice.8.refs_4_.refs_2_), channel_id=1, source_target_pairs={{0,1},{1,0},{2,3},{3,2},{4,5},{5,4},{6,7},{7,6},{8,9},{9,8},{10,11... | collective-permute-start | bytes 663560 | tf_op jit(solution)/shard_map/ppermute | solution.py:339
  18.4 2.7 %fusion = (bf16[288,288]{1,0:T(8,128)(2,1)S(1)}, bf16[288,288]{1,0:T(8,128)(2,1)S(1)}, bf16[288,288]{1,0:T(8,128)(2,1)S(1)}, bf16[288,288]{1,0:T(8,128)(2,1)S(1)...) fusion(bf16[1152,1152]{1,0:T(8,128)(2,1)} %param.8, s32[]{:T(128)S(6)} %select_n.8, ...), kind=kLoop, calls=%fused_computation | loop fusion | bytes 2322448 | tf_op jit(solution)/shard_map/dynamic_slice | solution.py:367
  21.1 8.5 %collective-permute-done.11.refs_6_.refs_7_ = bf16[288,256]{1,0:T(8,128)(2,1)S(1)} collective-permute-done((bf16[288,256]{1,0:T(8,128)(2,1)S(1)}, bf16[288,256]{1,0:T(8,128)(2,1)S(1)}, u32[]{:S(2)}, u32[]{:S(2)}) %collective-permute-start.11) | collective-permute-done | bytes 147488 | tf_op jit(solution)/shard_map/ppermute | solution.py:339
  29.6 0.5 shard_map.95.rest_8_
  30.2 2.5 %collective-permute-start.15 = (bf16[288,256]{1,0:T(8,128)(2,1)S(1)}, bf16[288,256]{1,0:T(8,128)(2,1)S(1)}, u32[]{:S(2)}, u32[]{:S(2)}) collective-permute-start(bf16[288,256]{1,0:T(8,128)(2,1)S(1)} %shard_map.95.rest_8_), channel_id=1, source_target_pairs={{0,24},{4,28},{8,16},{12,20},{16,8},{20,12},{24,0},{28,4},{1,25},{... | collective-permute-start | bytes 442376 | tf_op jit(solution)/shard_map/ppermute | solution.py:339
  32.7 0.5 collective-permute-start.14
  33.2 4.9 %collective-permute-done.1.refs_6_ = bf16[288,384]{1,0:T(8,128)(2,1)S(1)} collective-permute-done((bf16[288,384]{1,0:T(8,128)(2,1)S(1)}, bf16[288,384]{1,0:T(8,128)(2,1)S(1)}, u32[]{:S(2)}, u32[]{:S(2)}) %collective-permute-start.1) | collective-permute-done | bytes 221216 | tf_op jit(solution)/shard_map/ppermute | solution.py:339
  38.1 1.5 %collective-permute-start.13 = (bf16[288,256]{1,0:T(8,128)(2,1)S(1)}, bf16[288,256]{1,0:T(8,128)(2,1)}, u32[]{:S(2)}, u32[]{:S(2)}) collective-permute-start(bf16[288,256]{1,0:T(8,128)(2,1)S(1)} %shard_map.95.rest_8_), channel_id=1, source_target_pairs={{0,8},{4,12},{8,0},{12,4},{16,24},{20,28},{24,16},{28,20},{1,9},{5... | collective-permute-start | bytes 442376 | tf_op jit(solution)/shard_map/ppermute | solution.py:339
  39.6 0.7 shard_map.94.rest_0_
  40.4 1.6 %collective-permute-start.5 = (bf16[288,384]{1,0:T(8,128)(2,1)S(1)}, bf16[288,384]{1,0:T(8,128)(2,1)S(1)}, u32[]{:S(2)}, u32[]{:S(2)}) collective-permute-start(bf16[288,384]{1,0:T(8,128)(2,1)S(1)} %shard_map.94.rest_0_), channel_id=1, source_target_pairs={{0,24},{4,28},{8,16},{12,20},{16,8},{20,12},{24,0},{28,4},{1,25},{... | collective-permute-start | bytes 663560 | tf_op jit(solution)/shard_map/ppermute | solution.py:339
  41.9 0.5 collective-permute-start.4
  42.4 1.5 %collective-permute-start.3 = (bf16[288,384]{1,0:T(8,128)(2,1)S(1)}, bf16[288,384]{1,0:T(8,128)(2,1)}, u32[]{:S(2)}, u32[]{:S(2)}) collective-permute-start(bf16[288,384]{1,0:T(8,128)(2,1)S(1)} %shard_map.94.rest_0_), channel_id=1, source_target_pairs={{0,8},{4,12},{8,0},{12,4},{16,24},{20,28},{24,16},{28,20},{1,9},{5... | collective-permute-start | bytes 663560 | tf_op jit(solution)/shard_map/ppermute | solution.py:339
  44.0 0.5 collective-permute-start.18
  44.5 0.9 collective-permute-done.19.rest_15_
  45.5 5.0 %collective-permute-done.5.rest_3_ = bf16[288,384]{1,0:T(8,128)(2,1)S(1)} collective-permute-done((bf16[288,384]{1,0:T(8,128)(2,1)S(1)}, bf16[288,384]{1,0:T(8,128)(2,1)S(1)}, u32[]{:S(2)}, u32[]{:S(2)}) %collective-permute-start.5) | collective-permute-done | bytes 221216 | tf_op jit(solution)/shard_map/ppermute | solution.py:339
  50.4 2.0 %collective-permute-done.4.rest_2_ = bf16[288,384]{1,0:T(8,128)(2,1)S(1)} collective-permute-done((bf16[288,384]{1,0:T(8,128)(2,1)S(1)}, bf16[288,384]{1,0:T(8,128)(2,1)S(1)}, u32[]{:S(2)}, u32[]{:S(2)}) %collective-permute-start.4) | collective-permute-done | bytes 221216 | tf_op jit(solution)/shard_map/ppermute | solution.py:339
  53.0 0.7 copy-done.13
  54.3 1.2 collective-permute-done.17.rest_13_
  55.5 13.4 %shard_map.96 = (bf16[288,640]{1,0:T(8,128)(2,1)}, bf16[4,288,256]{2,1,0:T(8,128)(2,1)S(1)}, bf16[4,288,256]{2,1,0:T(8,128)(2,1)S(1)}, bf16[4,288,384]{2,1,0:T(8,128)(2,1)S(1)}, bf16[4,288,384]{2,1,0:T(8,128)(2,1)S(1)}) custom-call(s32[240]{0:T(256)S(1)} %reshape.16.coords_ref, s32[5]{0:T(128)S(1)} %copy-done.4, s32[1]{0:T(128)} %bitcast.me_ref, ...), custom_call_target="tpu_custom_call" | custom-call | flops 4529848320 | bytes 7864320 | tf_op jit(solution)/shard_map/pallas_call | solution.py:163
  69.5 2.8 %collective-permute-done.21.got_ref.refs_1_ = bf16[4,288,256]{2,1,0:T(8,128)(2,1)S(1)} collective-permute-done((bf16[4,288,256]{2,1,0:T(8,128)(2,1)S(1)}, bf16[4,288,256]{2,1,0:T(8,128)(2,1)S(1)}, u32[]{:S(2)}, u32[]{:S(2)}) %collective-permute-start.21) | collective-permute-done | bytes 589856 | tf_op jit(solution)/shard_map/ppermute | solution.py:339
  72.4 1.3 %collective-permute-start.22 = (bf16[288,256]{1,0:T(8,128)(2,1)S(1)}, bf16[288,256]{1,0:T(8,128)(2,1)S(1)}, u32[]{:S(2)}, u32[]{:S(2)}) collective-permute-start(bf16[288,256]{1,0:T(8,128)(2,1)S(1)} %get-tuple-element.24), channel_id=1, source_target_pairs={{0,8},{4,12},{8,0},{12,4},{16,24},{20,28},{24,16},{28,20},{1,9},{5... | collective-permute-start | bytes 442376 | tf_op jit(solution)/shard_map/ppermute | solution.py:339
  73.7 3.7 %collective-permute-start.23 = (bf16[288,256]{1,0:T(8,128)(2,1)S(1)}, bf16[288,256]{1,0:T(8,128)(2,1)S(1)}, u32[]{:S(2)}, u32[]{:S(2)}) collective-permute-start(bf16[288,256]{1,0:T(8,128)(2,1)S(1)} %get-tuple-element.25), channel_id=1, source_target_pairs={{0,16},{4,20},{8,24},{12,28},{16,0},{20,4},{24,8},{28,12},{1,17},{... | collective-permute-start | bytes 442376 | tf_op jit(solution)/shard_map/ppermute | solution.py:339
  77.4 1.1 collective-permute-done.22.refs_0_.refs_2_
  78.5 6.1 %collective-permute-done.23.refs_1_.refs_3_ = bf16[288,256]{1,0:T(8,128)(2,1)S(1)} collective-permute-done((bf16[288,256]{1,0:T(8,128)(2,1)S(1)}, bf16[288,256]{1,0:T(8,128)(2,1)S(1)}, u32[]{:S(2)}, u32[]{:S(2)}) %collective-permute-start.23) | collective-permute-done | bytes 147488 | tf_op jit(solution)/shard_map/ppermute | solution.py:339
  84.8 1.5 %collective-permute-start.25 = (bf16[288,384]{1,0:T(8,128)(2,1)S(1)}, bf16[288,384]{1,0:T(8,128)(2,1)S(1)}, u32[]{:S(2)}, u32[]{:S(2)}) collective-permute-start(bf16[288,384]{1,0:T(8,128)(2,1)S(1)} %get-tuple-element.27), channel_id=1, source_target_pairs={{0,8},{4,12},{8,0},{12,4},{16,24},{20,28},{24,16},{28,20},{1,9},{5... | collective-permute-start | bytes 663560 | tf_op jit(solution)/shard_map/ppermute | solution.py:339
  86.3 0.6 collective-permute-start.26
  86.9 1.4 %collective-permute-start.27 = (bf16[288,384]{1,0:T(8,128)(2,1)S(1)}, bf16[288,384]{1,0:T(8,128)(2,1)S(1)}, u32[]{:S(2)}, u32[]{:S(2)}) collective-permute-start(bf16[288,384]{1,0:T(8,128)(2,1)S(1)} %get-tuple-element.29), channel_id=1, source_target_pairs={{0,24},{4,28},{8,16},{12,20},{16,8},{20,12},{24,0},{28,4},{1,25},{... | collective-permute-start | bytes 663560 | tf_op jit(solution)/shard_map/ppermute | solution.py:339
  88.4 2.4 %collective-permute-start.33 = (bf16[288,256]{1,0:T(8,128)(2,1)S(1)}, bf16[288,256]{1,0:T(8,128)(2,1)S(1)}, u32[]{:S(2)}, u32[]{:S(2)}) collective-permute-start(bf16[288,256]{1,0:T(8,128)(2,1)S(1)} %shard_map.100.refs_4_.refs_0_), channel_id=1, source_target_pairs={{0,3},{1,2},{2,1},{3,0},{4,7},{5,6},{6,5},{7,4},{8,11},{9,10},{10,... | collective-permute-start | bytes 442376 | tf_op jit(solution)/shard_map/ppermute | solution.py:339
  90.8 2.4 %collective-permute-done.25.refs_2_ = bf16[288,384]{1,0:T(8,128)(2,1)S(1)} collective-permute-done((bf16[288,384]{1,0:T(8,128)(2,1)S(1)}, bf16[288,384]{1,0:T(8,128)(2,1)S(1)}, u32[]{:S(2)}, u32[]{:S(2)}) %collective-permute-start.25) | collective-permute-done | bytes 221216 | tf_op jit(solution)/shard_map/ppermute | solution.py:339
  93.2 4.4 %collective-permute-done.26.refs_3_ = bf16[288,384]{1,0:T(8,128)(2,1)S(1)} collective-permute-done((bf16[288,384]{1,0:T(8,128)(2,1)S(1)}, bf16[288,384]{1,0:T(8,128)(2,1)S(1)}, u32[]{:S(2)}, u32[]{:S(2)}) %collective-permute-start.26) | collective-permute-done | bytes 221216 | tf_op jit(solution)/shard_map/ppermute | solution.py:339
  97.8 4.2 %collective-permute-done.32.refs_6_.refs_11_ = bf16[288,256]{1,0:T(8,128)(2,1)S(1)} collective-permute-done((bf16[288,256]{1,0:T(8,128)(2,1)S(1)}, bf16[288,256]{1,0:T(8,128)(2,1)S(1)}, u32[]{:S(2)}, u32[]{:S(2)}) %collective-permute-start.32) | collective-permute-done | bytes 147488 | tf_op jit(solution)/shard_map/ppermute | solution.py:339
  102.0 1.4 %shard_map.102 = (f32[4,144,288]{2,1,0:T(8,128)S(1)}, bf16[4,144,288]{2,1,0:T(8,128)(2,1)S(1)}) custom-call(s32[1]{0:T(128)} %bitcast.4.col_ref, s32[1]{0:T(128)} %bitcast.me_ref, bf16[288,256]{1,0:T(8,128)(2,1)S(1)} %shard_map.100.refs_4_.refs_0_, bf16[288,384]{1,0:T(8,128)(2,1)S(1)} %shard_map.99.refs_1_.refs_4_, ...), custom_call_target="tpu_custom_call" | custom-call | tf_op jit(solution)/shard_map/pallas_call | solution.py:319
  103.5 1.6 %collective-permute-start.30 = (bf16[288,384]{1,0:T(8,128)(2,1)S(1)}, bf16[288,384]{1,0:T(8,128)(2,1)S(1)}, u32[]{:S(2)}, u32[]{:S(2)}) collective-permute-start(bf16[288,384]{1,0:T(8,128)(2,1)S(1)} %shard_map.99.refs_1_.refs_4_), channel_id=1, source_target_pairs={{0,3},{1,2},{2,1},{3,0},{4,7},{5,6},{6,5},{7,4},{8,11},{9,10},{10,... | collective-permute-start | bytes 663560 | tf_op jit(solution)/shard_map/ppermute | solution.py:339
  105.1 2.9 %collective-permute-start.28 = (bf16[288,384]{1,0:T(8,128)(2,1)S(1)}, bf16[288,384]{1,0:T(8,128)(2,1)S(1)}, u32[]{:S(2)}, u32[]{:S(2)}) collective-permute-start(bf16[288,384]{1,0:T(8,128)(2,1)S(1)} %shard_map.99.refs_1_.refs_4_), channel_id=1, source_target_pairs={{0,1},{1,0},{2,3},{3,2},{4,5},{5,4},{6,7},{7,6},{8,9},{9,8},{10,11... | collective-permute-start | bytes 663560 | tf_op jit(solution)/shard_map/ppermute | solution.py:339
  108.1 1.5 %collective-permute-start.35 = (bf16[144,288]{1,0:T(8,128)(2,1)S(1)}, bf16[144,288]{1,0:T(8,128)(2,1)S(1)}, u32[]{:S(2)}, u32[]{:S(2)}) collective-permute-start(bf16[144,288]{1,0:T(8,128)(2,1)S(1)} %get-tuple-element.32), channel_id=1, source_target_pairs={{0,8},{4,12},{8,0},{12,4},{16,24},{20,28},{24,16},{28,20},{1,9},{5... | collective-permute-start | bytes 248840 | tf_op jit(solution)/shard_map/ppermute | solution.py:339
  109.6 0.7 collective-permute-start.36
  110.3 2.6 %collective-permute-done.35.refs_2_ = bf16[144,288]{1,0:T(8,128)(2,1)S(1)} collective-permute-done((bf16[144,288]{1,0:T(8,128)(2,1)S(1)}, bf16[144,288]{1,0:T(8,128)(2,1)S(1)}, u32[]{:S(2)}, u32[]{:S(2)}) %collective-permute-start.35) | collective-permute-done | bytes 82976 | tf_op jit(solution)/shard_map/ppermute | solution.py:339
  112.9 1.5 %collective-permute-start.37 = (bf16[144,288]{1,0:T(8,128)(2,1)S(1)}, bf16[144,288]{1,0:T(8,128)(2,1)S(1)}, u32[]{:S(2)}, u32[]{:S(2)}) collective-permute-start(bf16[144,288]{1,0:T(8,128)(2,1)S(1)} %get-tuple-element.34), channel_id=1, source_target_pairs={{0,24},{4,28},{8,16},{12,20},{16,8},{20,12},{24,0},{28,4},{1,25},{... | collective-permute-start | bytes 248840 | tf_op jit(solution)/shard_map/ppermute | solution.py:339
  114.9 3.6 %collective-permute-done.37.refs_4_ = bf16[144,288]{1,0:T(8,128)(2,1)S(1)} collective-permute-done((bf16[144,288]{1,0:T(8,128)(2,1)S(1)}, bf16[144,288]{1,0:T(8,128)(2,1)S(1)}, u32[]{:S(2)}, u32[]{:S(2)}) %collective-permute-start.37) | collective-permute-done | bytes 82976 | tf_op jit(solution)/shard_map/ppermute | solution.py:339
  118.5 0.8 shard_map.104.refs_9_
  119.3 5.1 %collective-permute-done.29.refs_6_ = bf16[288,384]{1,0:T(8,128)(2,1)S(1)} collective-permute-done((bf16[288,384]{1,0:T(8,128)(2,1)S(1)}, bf16[288,384]{1,0:T(8,128)(2,1)S(1)}, u32[]{:S(2)}, u32[]{:S(2)}) %collective-permute-start.29) | collective-permute-done | bytes 221216 | tf_op jit(solution)/shard_map/ppermute | solution.py:339
  124.4 0.9 copy-done
  125.3 1.4 %shard_map.105 = bf16[288,640]{1,0:T(8,128)(2,1)} custom-call(bf16[288,288]{1,0:T(8,128)(2,1)S(1)} %get-tuple-element.40.refs_0_, bf16[288,288]{1,0:T(8,128)(2,1)S(1)} %get-tuple-element.36.refs_1_, bf16[288,288]{1,0:T(8,128)(2,1)S(1)} %get-tuple-element.41.refs_2_, bf16[288,288]{1,0:T(8,128)(2,1)S(1)} %get-tuple-element.35.refs_3_, ...), custom_call_target="tpu_custom_call" | custom-call | tf_op jit(solution)/shard_map/pallas_call | solution.py:206
  (73 shorter events, 3.2 us)
Async XLA Ops:
  1.6 10.5 %collective-permute-start.12 = (bf16[288,256]{1,0:T(8,128)(2,1)S(1)}, bf16[288,256]{1,0:T(8,128)(2,1)S(1)}, u32[]{:S(2)}, u32[]{:S(2)}) collective-permute-start(bf16[288,256]{1,0:T(8,128)(2,1)S(1)} %slice.9.refs_4_.refs_3_), channel_id=1, source_target_pairs={{0,3},{1,2},{2,1},{3,0},{4,7},{5,6},{6,5},{7,4},{8,11},{9,10},{10,... | collective-permute-start | bytes 442376 | tf_op jit(solution)/shard_map/ppermute | solution.py:339
  6.7 22.9 %collective-permute-start.11 = (bf16[288,256]{1,0:T(8,128)(2,1)S(1)}, bf16[288,256]{1,0:T(8,128)(2,1)S(1)}, u32[]{:S(2)}, u32[]{:S(2)}) collective-permute-start(bf16[288,256]{1,0:T(8,128)(2,1)S(1)} %slice.9.refs_4_.refs_3_), channel_id=1, source_target_pairs={{0,2},{1,3},{2,0},{3,1},{4,6},{5,7},{6,4},{7,5},{8,10},{9,11},{10,... | collective-permute-start | bytes 442376 | tf_op jit(solution)/shard_map/ppermute | solution.py:339
  6.7 22.9 %collective-permute-start.10 = (bf16[288,256]{1,0:T(8,128)(2,1)S(1)}, bf16[288,256]{1,0:T(8,128)(2,1)S(1)}, u32[]{:S(2)}, u32[]{:S(2)}) collective-permute-start(bf16[288,256]{1,0:T(8,128)(2,1)S(1)} %slice.9.refs_4_.refs_3_), channel_id=1, source_target_pairs={{0,1},{1,0},{2,3},{3,2},{4,5},{5,4},{6,7},{7,6},{8,9},{9,8},{10,11... | collective-permute-start | bytes 442376 | tf_op jit(solution)/shard_map/ppermute | solution.py:339
  8.3 24.5 %collective-permute-start.2 = (bf16[288,384]{1,0:T(8,128)(2,1)S(1)}, bf16[288,384]{1,0:T(8,128)(2,1)S(1)}, u32[]{:S(2)}, u32[]{:S(2)}) collective-permute-start(bf16[288,384]{1,0:T(8,128)(2,1)S(1)} %slice.8.refs_4_.refs_2_), channel_id=1, source_target_pairs={{0,3},{1,2},{2,1},{3,0},{4,7},{5,6},{6,5},{7,4},{8,11},{9,10},{10,... | collective-permute-start | bytes 663560 | tf_op jit(solution)/shard_map/ppermute | solution.py:339
  12.1 26.0 %collective-permute-start.1 = (bf16[288,384]{1,0:T(8,128)(2,1)S(1)}, bf16[288,384]{1,0:T(8,128)(2,1)S(1)}, u32[]{:S(2)}, u32[]{:S(2)}) collective-permute-start(bf16[288,384]{1,0:T(8,128)(2,1)S(1)} %slice.8.refs_4_.refs_2_), channel_id=1, source_target_pairs={{0,2},{1,3},{2,0},{3,1},{4,6},{5,7},{6,4},{7,5},{8,10},{9,11},{10,... | collective-permute-start | bytes 663560 | tf_op jit(solution)/shard_map/ppermute | solution.py:339
  12.1 42.0 %copy-start.5 = (s32[5,48]{1,0:T(8,128)S(1)}, s32[5,48]{1,0:T(8,128)}, u32[]{:S(2)}) copy-start(s32[5,48]{1,0:T(8,128)} %param.11) | copy-start | bytes 2884
  12.1 42.1 %copy-start.6 = (f32[288]{0:T(512)S(1)}, f32[288]{0:T(512)}, u32[]{:S(2)}) copy-start(f32[288]{0:T(512)} %param.9) | copy-start | bytes 3460
  12.1 27.5 %collective-permute-start = (bf16[288,384]{1,0:T(8,128)(2,1)S(1)}, bf16[288,384]{1,0:T(8,128)(2,1)S(1)}, u32[]{:S(2)}, u32[]{:S(2)}) collective-permute-start(bf16[288,384]{1,0:T(8,128)(2,1)S(1)} %slice.8.refs_4_.refs_2_), channel_id=1, source_target_pairs={{0,1},{1,0},{2,3},{3,2},{4,5},{5,4},{6,7},{7,6},{8,9},{9,8},{10,11... | collective-permute-start | bytes 663560 | tf_op jit(solution)/shard_map/ppermute | solution.py:339
  21.1 34.4 %copy-start.3 = (bf16[640,288]{0,1:T(8,128)(2,1)S(1)}, bf16[640,288]{0,1:T(8,128)(2,1)}, u32[]{:S(2)}) copy-start(bf16[640,288]{0,1:T(8,128)(2,1)} %param.13) | copy-start | bytes 1105924
  21.1 34.4 %copy-start.4 = (s32[5]{0:T(128)S(1)}, s32[5]{0:T(128)}, u32[]{:S(2)}) copy-start(s32[5]{0:T(128)} %counts_ref.1) | copy-start | bytes 64
  30.1 25.3 %copy-start.2 = (bf16[288,256]{1,0:T(8,128)(2,1)}, bf16[288,256]{1,0:T(8,128)(2,1)S(1)}, u32[]{:S(2)}) copy-start(bf16[288,256]{1,0:T(8,128)(2,1)S(1)} %shard_map.95.rest_8_) | copy-start | bytes 442372
  30.1 11.8 %collective-permute-start.16 = (bf16[288,256]{1,0:T(8,128)(2,1)S(1)}, bf16[288,256]{1,0:T(8,128)(2,1)S(1)}, u32[]{:S(2)}, u32[]{:S(2)}) collective-permute-start(bf16[288,256]{1,0:T(8,128)(2,1)S(1)} %shard_map.95.rest_8_), channel_id=1, source_target_pairs={{0,4},{4,0},{8,12},{12,8},{16,20},{20,16},{24,28},{28,24},{1,5},{5... | collective-permute-start | bytes 442376 | tf_op jit(solution)/shard_map/ppermute | solution.py:339
  30.2 12.2 %collective-permute-start.15 = (bf16[288,256]{1,0:T(8,128)(2,1)S(1)}, bf16[288,256]{1,0:T(8,128)(2,1)S(1)}, u32[]{:S(2)}, u32[]{:S(2)}) collective-permute-start(bf16[288,256]{1,0:T(8,128)(2,1)S(1)} %shard_map.95.rest_8_), channel_id=1, source_target_pairs={{0,24},{4,28},{8,16},{12,20},{16,8},{20,12},{24,0},{28,4},{1,25},{... | collective-permute-start | bytes 442376 | tf_op jit(solution)/shard_map/ppermute | solution.py:339
  32.7 11.2 %collective-permute-start.14 = (bf16[288,256]{1,0:T(8,128)(2,1)S(1)}, bf16[288,256]{1,0:T(8,128)(2,1)S(1)}, u32[]{:S(2)}, u32[]{:S(2)}) collective-permute-start(bf16[288,256]{1,0:T(8,128)(2,1)S(1)} %shard_map.95.rest_8_), channel_id=1, source_target_pairs={{0,16},{4,20},{8,24},{12,28},{16,0},{20,4},{24,8},{28,12},{1,17},{... | collective-permute-start | bytes 442376 | tf_op jit(solution)/shard_map/ppermute | solution.py:339
  38.1 5.8 %collective-permute-start.13 = (bf16[288,256]{1,0:T(8,128)(2,1)S(1)}, bf16[288,256]{1,0:T(8,128)(2,1)}, u32[]{:S(2)}, u32[]{:S(2)}) collective-permute-start(bf16[288,256]{1,0:T(8,128)(2,1)S(1)} %shard_map.95.rest_8_), channel_id=1, source_target_pairs={{0,8},{4,12},{8,0},{12,4},{16,24},{20,28},{24,16},{28,20},{1,9},{5... | collective-permute-start | bytes 442376 | tf_op jit(solution)/shard_map/ppermute | solution.py:339
  40.4 15.1 %copy-start.1 = (bf16[288,384]{1,0:T(8,128)(2,1)}, bf16[288,384]{1,0:T(8,128)(2,1)S(1)}, u32[]{:S(2)}) copy-start(bf16[288,384]{1,0:T(8,128)(2,1)S(1)} %shard_map.94.rest_0_) | copy-start | bytes 663556
  40.4 10.0 %collective-permute-start.5 = (bf16[288,384]{1,0:T(8,128)(2,1)S(1)}, bf16[288,384]{1,0:T(8,128)(2,1)S(1)}, u32[]{:S(2)}, u32[]{:S(2)}) collective-permute-start(bf16[288,384]{1,0:T(8,128)(2,1)S(1)} %shard_map.94.rest_0_), channel_id=1, source_target_pairs={{0,24},{4,28},{8,16},{12,20},{16,8},{20,12},{24,0},{28,4},{1,25},{... | collective-permute-start | bytes 663560 | tf_op jit(solution)/shard_map/ppermute | solution.py:339
  41.9 11.0 %copy-start.9 = (bf16[288,256]{1,0:T(8,128)(2,1)}, bf16[288,256]{1,0:T(8,128)(2,1)S(1)}, u32[]{:S(2)}) copy-start(bf16[288,256]{1,0:T(8,128)(2,1)S(1)} %collective-permute-done.16.rest_12_) | copy-start | bytes 442372
  41.9 10.5 %collective-permute-start.4 = (bf16[288,384]{1,0:T(8,128)(2,1)S(1)}, bf16[288,384]{1,0:T(8,128)(2,1)S(1)}, u32[]{:S(2)}, u32[]{:S(2)}) collective-permute-start(bf16[288,384]{1,0:T(8,128)(2,1)S(1)} %shard_map.94.rest_0_), channel_id=1, source_target_pairs={{0,16},{4,20},{8,24},{12,28},{16,0},{20,4},{24,8},{28,12},{1,17},{... | collective-permute-start | bytes 663560 | tf_op jit(solution)/shard_map/ppermute | solution.py:339
  42.4 10.5 %copy-start.10 = (bf16[288,256]{1,0:T(8,128)(2,1)}, bf16[288,256]{1,0:T(8,128)(2,1)S(1)}, u32[]{:S(2)}) copy-start(bf16[288,256]{1,0:T(8,128)(2,1)S(1)} %collective-permute-done.15.rest_11_) | copy-start | bytes 442372
  42.4 10.4 %collective-permute-start.3 = (bf16[288,384]{1,0:T(8,128)(2,1)S(1)}, bf16[288,384]{1,0:T(8,128)(2,1)}, u32[]{:S(2)}, u32[]{:S(2)}) collective-permute-start(bf16[288,384]{1,0:T(8,128)(2,1)S(1)} %shard_map.94.rest_0_), channel_id=1, source_target_pairs={{0,8},{4,12},{8,0},{12,4},{16,24},{20,28},{24,16},{28,20},{1,9},{5... | collective-permute-start | bytes 663560 | tf_op jit(solution)/shard_map/ppermute | solution.py:339
  43.9 9.0 %copy-start.11 = (bf16[288,256]{1,0:T(8,128)(2,1)}, bf16[288,256]{1,0:T(8,128)(2,1)S(1)}, u32[]{:S(2)}) copy-start(bf16[288,256]{1,0:T(8,128)(2,1)S(1)} %collective-permute-done.14.rest_10_) | copy-start | bytes 442372
  43.9 1.4 %collective-permute-start.19 = (bf16[288,256]{1,0:T(8,128)(2,1)S(1)}, bf16[288,256]{1,0:T(8,128)(2,1)S(1)}, u32[]{:S(2)}, u32[]{:S(2)}) collective-permute-start(bf16[288,256]{1,0:T(8,128)(2,1)S(1)} %collective-permute-done.15.rest_11_), channel_id=1, source_target_pairs={{0,4},{4,0},{8,12},{12,8},{16,20},{20,16},{24,28},{28,24},{1,5},{5... | collective-permute-start | bytes 442376 | tf_op jit(solution)/shard_map/ppermute | solution.py:339
  44.0 9.0 %collective-permute-start.18 = (bf16[288,256]{1,0:T(8,128)(2,1)S(1)}, bf16[288,256]{1,0:T(8,128)(2,1)S(1)}, u32[]{:S(2)}, u32[]{:S(2)}) collective-permute-start(bf16[288,256]{1,0:T(8,128)(2,1)S(1)} %collective-permute-done.14.rest_10_), channel_id=1, source_target_pairs={{0,4},{4,0},{8,12},{12,8},{16,20},{20,16},{24,28},{28,24},{1,5},{5... | collective-permute-start | bytes 442376 | tf_op jit(solution)/shard_map/ppermute | solution.py:339
  45.3 7.7 %copy-start.12 = (bf16[288,256]{1,0:T(8,128)(2,1)}, bf16[288,256]{1,0:T(8,128)(2,1)S(1)}, u32[]{:S(2)}) copy-start(bf16[288,256]{1,0:T(8,128)(2,1)S(1)} %collective-permute-done.19.rest_15_) | copy-start | bytes 442372
  45.3 10.1 %collective-permute-start.6 = (bf16[288,384]{1,0:T(8,128)(2,1)S(1)}, bf16[288,384]{1,0:T(8,128)(2,1)}, u32[]{:S(2)}, u32[]{:S(2)}) collective-permute-start(bf16[288,384]{1,0:T(8,128)(2,1)S(1)} %shard_map.94.rest_0_), channel_id=1, source_target_pairs={{0,4},{4,0},{8,12},{12,8},{16,20},{20,16},{24,28},{28,24},{1,5},{5... | collective-permute-start | bytes 663560 | tf_op jit(solution)/shard_map/ppermute | solution.py:339
  50.4 5.0 %collective-permute-start.9 = (bf16[288,384]{1,0:T(8,128)(2,1)S(1)}, bf16[288,384]{1,0:T(8,128)(2,1)}, u32[]{:S(2)}, u32[]{:S(2)}) collective-permute-start(bf16[288,384]{1,0:T(8,128)(2,1)S(1)} %collective-permute-done.5.rest_3_), channel_id=1, source_target_pairs={{0,4},{4,0},{8,12},{12,8},{16,20},{20,16},{24,28},{28,24},{1,5},{5... | collective-permute-start | bytes 663560 | tf_op jit(solution)/shard_map/ppermute | solution.py:339
  52.4 3.0 %collective-permute-start.8 = (bf16[288,384]{1,0:T(8,128)(2,1)S(1)}, bf16[288,384]{1,0:T(8,128)(2,1)}, u32[]{:S(2)}, u32[]{:S(2)}) collective-permute-start(bf16[288,384]{1,0:T(8,128)(2,1)S(1)} %collective-permute-done.4.rest_2_), channel_id=1, source_target_pairs={{0,4},{4,0},{8,12},{12,8},{16,20},{20,16},{24,28},{28,24},{1,5},{5... | collective-permute-start | bytes 663560 | tf_op jit(solution)/shard_map/ppermute | solution.py:339
  52.9 2.6 %collective-permute-start.7 = (bf16[288,384]{1,0:T(8,128)(2,1)}, bf16[288,384]{1,0:T(8,128)(2,1)}, u32[]{:S(2)}, u32[]{:S(2)}) collective-permute-start(bf16[288,384]{1,0:T(8,128)(2,1)} %collective-permute-done.3.rest_1_), channel_id=1, source_target_pairs={{0,4},{4,0},{8,12},{12,8},{16,20},{20,16},{24,28},{28,24},{1,5},{5... | collective-permute-start | bytes 663560 | tf_op jit(solution)/shard_map/ppermute | solution.py:339
  53.6 1.8 %collective-permute-start.17 = (bf16[288,256]{1,0:T(8,128)(2,1)}, bf16[288,256]{1,0:T(8,128)(2,1)}, u32[]{:S(2)}, u32[]{:S(2)}) collective-permute-start(bf16[288,256]{1,0:T(8,128)(2,1)} %collective-permute-done.13.rest_9_), channel_id=1, source_target_pairs={{0,4},{4,0},{8,12},{12,8},{16,20},{20,16},{24,28},{28,24},{1,5},{5... | collective-permute-start | bytes 442376 | tf_op jit(solution)/shard_map/ppermute | solution.py:339
  68.9 15.7 %collective-permute-start.20 = (bf16[4,288,384]{2,1,0:T(8,128)(2,1)S(1)}, bf16[4,288,384]{2,1,0:T(8,128)(2,1)S(1)}, u32[]{:S(2)}, u32[]{:S(2)}) collective-permute-start(bf16[4,288,384]{2,1,0:T(8,128)(2,1)S(1)} %get-tuple-element.21), channel_id=1, source_target_pairs={{0,4},{4,0},{8,12},{12,8},{16,20},{20,16},{24,28},{28,24},{1,5},{5... | collective-permute-start | bytes 2654216 | tf_op jit(solution)/shard_map/ppermute | solution.py:339
  69.3 3.0 %collective-permute-start.21 = (bf16[4,288,256]{2,1,0:T(8,128)(2,1)S(1)}, bf16[4,288,256]{2,1,0:T(8,128)(2,1)S(1)}, u32[]{:S(2)}, u32[]{:S(2)}) collective-permute-start(bf16[4,288,256]{2,1,0:T(8,128)(2,1)S(1)} %get-tuple-element.23), channel_id=1, source_target_pairs={{0,4},{4,0},{8,12},{12,8},{16,20},{20,16},{24,28},{28,24},{1,5},{5... | collective-permute-start | bytes 1769480 | tf_op jit(solution)/shard_map/ppermute | solution.py:339
  72.4 6.1 %collective-permute-start.22 = (bf16[288,256]{1,0:T(8,128)(2,1)S(1)}, bf16[288,256]{1,0:T(8,128)(2,1)S(1)}, u32[]{:S(2)}, u32[]{:S(2)}) collective-permute-start(bf16[288,256]{1,0:T(8,128)(2,1)S(1)} %get-tuple-element.24), channel_id=1, source_target_pairs={{0,8},{4,12},{8,0},{12,4},{16,24},{20,28},{24,16},{28,20},{1,9},{5... | collective-permute-start | bytes 442376 | tf_op jit(solution)/shard_map/ppermute | solution.py:339
  73.7 10.9 %collective-permute-start.23 = (bf16[288,256]{1,0:T(8,128)(2,1)S(1)}, bf16[288,256]{1,0:T(8,128)(2,1)S(1)}, u32[]{:S(2)}, u32[]{:S(2)}) collective-permute-start(bf16[288,256]{1,0:T(8,128)(2,1)S(1)} %get-tuple-element.25), channel_id=1, source_target_pairs={{0,16},{4,20},{8,24},{12,28},{16,0},{20,4},{24,8},{28,12},{1,17},{... | collective-permute-start | bytes 442376 | tf_op jit(solution)/shard_map/ppermute | solution.py:339
  77.4 7.2 %collective-permute-start.24 = (bf16[288,256]{1,0:T(8,128)(2,1)S(1)}, bf16[288,256]{1,0:T(8,128)(2,1)S(1)}, u32[]{:S(2)}, u32[]{:S(2)}) collective-permute-start(bf16[288,256]{1,0:T(8,128)(2,1)S(1)} %get-tuple-element.26), channel_id=1, source_target_pairs={{0,24},{4,28},{8,16},{12,20},{16,8},{20,12},{24,0},{28,4},{1,25},{... | collective-permute-start | bytes 442376 | tf_op jit(solution)/shard_map/ppermute | solution.py:339
  84.8 8.4 %collective-permute-start.25 = (bf16[288,384]{1,0:T(8,128)(2,1)S(1)}, bf16[288,384]{1,0:T(8,128)(2,1)S(1)}, u32[]{:S(2)}, u32[]{:S(2)}) collective-permute-start(bf16[288,384]{1,0:T(8,128)(2,1)S(1)} %get-tuple-element.27), channel_id=1, source_target_pairs={{0,8},{4,12},{8,0},{12,4},{16,24},{20,28},{24,16},{28,20},{1,9},{5... | collective-permute-start | bytes 663560 | tf_op jit(solution)/shard_map/ppermute | solution.py:339
  86.3 11.3 %collective-permute-start.26 = (bf16[288,384]{1,0:T(8,128)(2,1)S(1)}, bf16[288,384]{1,0:T(8,128)(2,1)S(1)}, u32[]{:S(2)}, u32[]{:S(2)}) collective-permute-start(bf16[288,384]{1,0:T(8,128)(2,1)S(1)} %get-tuple-element.28), channel_id=1, source_target_pairs={{0,16},{4,20},{8,24},{12,28},{16,0},{20,4},{24,8},{28,12},{1,17},{... | collective-permute-start | bytes 663560 | tf_op jit(solution)/shard_map/ppermute | solution.py:339
  86.9 10.7 %collective-permute-start.27 = (bf16[288,384]{1,0:T(8,128)(2,1)S(1)}, bf16[288,384]{1,0:T(8,128)(2,1)S(1)}, u32[]{:S(2)}, u32[]{:S(2)}) collective-permute-start(bf16[288,384]{1,0:T(8,128)(2,1)S(1)} %get-tuple-element.29), channel_id=1, source_target_pairs={{0,24},{4,28},{8,16},{12,20},{16,8},{20,12},{24,0},{28,4},{1,25},{... | collective-permute-start | bytes 663560 | tf_op jit(solution)/shard_map/ppermute | solution.py:339
  88.4 9.4 %collective-permute-start.33 = (bf16[288,256]{1,0:T(8,128)(2,1)S(1)}, bf16[288,256]{1,0:T(8,128)(2,1)S(1)}, u32[]{:S(2)}, u32[]{:S(2)}) collective-permute-start(bf16[288,256]{1,0:T(8,128)(2,1)S(1)} %shard_map.100.refs_4_.refs_0_), channel_id=1, source_target_pairs={{0,3},{1,2},{2,1},{3,0},{4,7},{5,6},{6,5},{7,4},{8,11},{9,10},{10,... | collective-permute-start | bytes 442376 | tf_op jit(solution)/shard_map/ppermute | solution.py:339
  90.8 11.2 %collective-permute-start.32 = (bf16[288,256]{1,0:T(8,128)(2,1)S(1)}, bf16[288,256]{1,0:T(8,128)(2,1)S(1)}, u32[]{:S(2)}, u32[]{:S(2)}) collective-permute-start(bf16[288,256]{1,0:T(8,128)(2,1)S(1)} %shard_map.100.refs_4_.refs_0_), channel_id=1, source_target_pairs={{0,2},{1,3},{2,0},{3,1},{4,6},{5,7},{6,4},{7,5},{8,10},{9,11},{10,... | collective-permute-start | bytes 442376 | tf_op jit(solution)/shard_map/ppermute | solution.py:339
  93.2 8.8 %collective-permute-start.31 = (bf16[288,256]{1,0:T(8,128)(2,1)S(1)}, bf16[288,256]{1,0:T(8,128)(2,1)S(1)}, u32[]{:S(2)}, u32[]{:S(2)}) collective-permute-start(bf16[288,256]{1,0:T(8,128)(2,1)S(1)} %shard_map.100.refs_4_.refs_0_), channel_id=1, source_target_pairs={{0,1},{1,0},{2,3},{3,2},{4,5},{5,4},{6,7},{7,6},{8,9},{9,8},{10,11... | collective-permute-start | bytes 442376 | tf_op jit(solution)/shard_map/ppermute | solution.py:339
  103.5 4.5 %collective-permute-start.34 = (bf16[4,144,288]{2,1,0:T(8,128)(2,1)S(1)}, bf16[4,144,288]{2,1,0:T(8,128)(2,1)S(1)}, u32[]{:S(2)}, u32[]{:S(2)}) collective-permute-start(bf16[4,144,288]{2,1,0:T(8,128)(2,1)S(1)} %get-tuple-element.31), channel_id=1, source_target_pairs={{0,4},{4,0},{8,12},{12,8},{16,20},{20,16},{24,28},{28,24},{1,5},{5... | collective-permute-start | bytes 995336 | tf_op jit(solution)/shard_map/ppermute | solution.py:339
  103.5 15.8 %collective-permute-start.30 = (bf16[288,384]{1,0:T(8,128)(2,1)S(1)}, bf16[288,384]{1,0:T(8,128)(2,1)S(1)}, u32[]{:S(2)}, u32[]{:S(2)}) collective-permute-start(bf16[288,384]{1,0:T(8,128)(2,1)S(1)} %shard_map.99.refs_1_.refs_4_), channel_id=1, source_target_pairs={{0,3},{1,2},{2,1},{3,0},{4,7},{5,6},{6,5},{7,4},{8,11},{9,10},{10,... | collective-permute-start | bytes 663560 | tf_op jit(solution)/shard_map/ppermute | solution.py:339
  105.1 19.3 %collective-permute-start.29 = (bf16[288,384]{1,0:T(8,128)(2,1)S(1)}, bf16[288,384]{1,0:T(8,128)(2,1)S(1)}, u32[]{:S(2)}, u32[]{:S(2)}) collective-permute-start(bf16[288,384]{1,0:T(8,128)(2,1)S(1)} %shard_map.99.refs_1_.refs_4_), channel_id=1, source_target_pairs={{0,2},{1,3},{2,0},{3,1},{4,6},{5,7},{6,4},{7,5},{8,10},{9,11},{10,... | collective-permute-start | bytes 663560 | tf_op jit(solution)/shard_map/ppermute | solution.py:339
  105.1 19.3 %collective-permute-start.28 = (bf16[288,384]{1,0:T(8,128)(2,1)S(1)}, bf16[288,384]{1,0:T(8,128)(2,1)S(1)}, u32[]{:S(2)}, u32[]{:S(2)}) collective-permute-start(bf16[288,384]{1,0:T(8,128)(2,1)S(1)} %shard_map.99.refs_1_.refs_4_), channel_id=1, source_target_pairs={{0,1},{1,0},{2,3},{3,2},{4,5},{5,4},{6,7},{7,6},{8,9},{9,8},{10,11... | collective-permute-start | bytes 663560 | tf_op jit(solution)/shard_map/ppermute | solution.py:339
  108.1 4.8 %collective-permute-start.35 = (bf16[144,288]{1,0:T(8,128)(2,1)S(1)}, bf16[144,288]{1,0:T(8,128)(2,1)S(1)}, u32[]{:S(2)}, u32[]{:S(2)}) collective-permute-start(bf16[144,288]{1,0:T(8,128)(2,1)S(1)} %get-tuple-element.32), channel_id=1, source_target_pairs={{0,8},{4,12},{8,0},{12,4},{16,24},{20,28},{24,16},{28,20},{1,9},{5... | collective-permute-start | bytes 248840 | tf_op jit(solution)/shard_map/ppermute | solution.py:339
  109.6 5.3 %collective-permute-start.36 = (bf16[144,288]{1,0:T(8,128)(2,1)S(1)}, bf16[144,288]{1,0:T(8,128)(2,1)S(1)}, u32[]{:S(2)}, u32[]{:S(2)}) collective-permute-start(bf16[144,288]{1,0:T(8,128)(2,1)S(1)} %get-tuple-element.33), channel_id=1, source_target_pairs={{0,16},{4,20},{8,24},{12,28},{16,0},{20,4},{24,8},{28,12},{1,17},{... | collective-permute-start | bytes 248840 | tf_op jit(solution)/shard_map/ppermute | solution.py:339
  112.9 5.6 %collective-permute-start.37 = (bf16[144,288]{1,0:T(8,128)(2,1)S(1)}, bf16[144,288]{1,0:T(8,128)(2,1)S(1)}, u32[]{:S(2)}, u32[]{:S(2)}) collective-permute-start(bf16[144,288]{1,0:T(8,128)(2,1)S(1)} %get-tuple-element.34), channel_id=1, source_target_pairs={{0,24},{4,28},{8,16},{12,20},{16,8},{20,12},{24,0},{28,4},{1,25},{... | collective-permute-start | bytes 248840 | tf_op jit(solution)/shard_map/ppermute | solution.py:339
  (4 other events, 9.7 us)

commit v5 on v4

--- a/solution.py
+++ b/solution.py
@@ -196,44 +196,48 @@
     return pltpu.with_memory_space_constraint(value, pltpu.HBM)
 
 
+SMEM = pl.BlockSpec(memory_space=pltpu.SMEM)
 VMEM = pl.BlockSpec(memory_space=pltpu.VMEM)
 ANY = pl.BlockSpec(memory_space=pl.ANY)
 
 
-def small_call(kernel, out_shape, values, after, pinned=True):
+def small_call(kernel, out_shape, values, after, pinned=True, scalars=()):
     outs = jax.tree.leaves(out_shape)
     touched = sum(v.size * v.dtype.itemsize for v in (*values, *outs))
     return pl.pallas_call(
         kernel,
         out_shape=out_shape,
-        in_specs=[VMEM] * len(values) + [ANY] * len(after),
+        in_specs=[SMEM] * len(scalars) + [VMEM] * len(values) + [ANY] * len(after),
         out_specs=jax.tree.map(lambda _: VMEM, out_shape),
         compiler_params=pltpu.CompilerParams(vmem_limit_bytes=2 * touched + 2 * MIB),
         cost_estimate=pl.CostEstimate(flops=0, bytes_accessed=0, transcendentals=0),
-    )(*[in_vmem(v) for v in values] if pinned else values, *after)
-
-
-def sum_dots(lefts, rights, dims, before=(), after=()):
+    )(*scalars, *[in_vmem(v) for v in values] if pinned else values, *after)
+
+
+def sum_dots(lefts, rights, dims, outer, before=(), after=()):
     (left_dim,), unused_right = dims
     number = len(lefts)
-    rows, cols = lefts[0].shape[1 - left_dim], rights[0].shape[1]
+    rows, cols = lefts[0].shape[1 - left_dim], rights[0][0].shape[1]
     skip = sum(v.shape[1] for v in before)
-
-    def kernel(*refs):
-        total = None
-        for left, right in zip(refs[:number], refs[number : 2 * number]):
-            term = lax.dot_general(
-                left[...], right[...], (dims, ((), ())), preferred_element_type=F32
-            )
+    flat = [v for right in rights for v in right]
+
+    def kernel(outer_ref, *refs):
+        total, place = None, number
+        for left, right in zip(refs[:number], rights):
+            value = refs[place][...]
+            if len(right) > 1:
+                value = jnp.where(outer_ref[0] == 1, refs[place + 1][...], value)
+            place += len(right)
+            term = lax.dot_general(left[...], value, (dims, ((), ())), preferred_element_type=F32)
             total = term if total is None else total + term
         start = 0
-        for ref in refs[2 * number : 2 * number + len(before)]:
+        for ref in refs[place : place + len(before)]:
             refs[-1][:, start : start + ref.shape[1]] = ref[...]
             start += ref.shape[1]
         refs[-1][:, skip:] = total.astype(BF16)
 
     out = jax.ShapeDtypeStruct((rows, skip + cols), BF16)
-    return small_call(kernel, out, (*lefts, *rights, *before), after, False)
+    return small_call(kernel, out, (*lefts, *flat, *before), after, False, (outer,))
 
 
 def pack(values):
@@ -271,34 +275,53 @@
     return small_call(kernel, out, (keep, got), after)
 
 
-def weight_parts(scale, cols_order, rows_order, col, me, grads, x_parts, after=()):
+def weight_parts(scale, cols_order, rows_order, col, me, outer, grads, x_parts, after=()):
     width = grads[0].shape[0]
     rows_dev = sum(g.shape[1] for g in grads)
     n_rows = len(rows_order)
     half = n_rows // 2
     rows_out = width * len(cols_order) // n_rows
-    pieces = len(x_parts[0])
-    values = (*grads, *[p for parts in x_parts for p in parts])
-
-    def kernel(col_ref, me_ref, *refs):
-        inputs = refs[: len(values)]
+    values = (*grads, *[v for parts in x_parts for choice in parts for v in choice])
+
+    def kernel(col_ref, me_ref, outer_ref, *refs):
         keep_ref, send_ref, grad, xs, part, sems = refs[-6:]
-        copies = []
-
-        def fill(target, sources, first_sem):
+        always, chosen, place = [], ([], []), 0
+
+        def copy_to(target, start):
+            nonlocal place
+            source = refs[place]
+            lanes = pl.ds(start, source.shape[1])
+            copy = pltpu.make_async_copy(source, target.at[:, lanes], sems.at[place])
+            place += 1
+            return copy
+
+        start = 0
+        for value in grads:
+            always.append(copy_to(grad, start))
+            start += value.shape[1]
+        for j, parts in enumerate(x_parts):
             start = 0
-            for j, source in enumerate(sources):
-                lanes = pl.ds(start, source.shape[1])
-                copy = pltpu.make_async_copy(source, target.at[:, lanes], sems.at[first_sem + j])
-                copy.start()
-                copies.append(copy)
-                start += source.shape[1]
-
-        fill(grad, inputs[: len(grads)], 0)
-        for j in range(len(cols_order)):
-            first = len(grads) + j * pieces
-            fill(xs.at[j], inputs[first : first + pieces], first)
-        for copy in copies:
+            for choice in parts:
+                copies = [copy_to(xs.at[j], start) for unused in choice]
+                if len(copies) == 1:
+                    always += copies
+                else:
+                    for group, copy in zip(chosen, copies):
+                        group.append(copy)
+                start += choice[0].shape[1]
+        for copy in always:
+            copy.start()
+        for flag, group in enumerate(chosen):
+            if group:
+
+                @pl.when(outer_ref[0] == flag)
+                def _():
+                    for copy in group:
+                        copy.start()
+                    for copy in group:
+                        copy.wait()
+
+        for copy in always:
             copy.wait()
         for j, k in enumerate(cols_order):
             start = pl.multiple_of((col_ref[0] ^ k) * width, 16)
@@ -315,14 +338,13 @@
                 send_ref[j - half] = value.astype(BF16)
 
     touched = 2 * width * rows_dev * (len(cols_order) + 1) + 8 * width * width * len(cols_order)
-    smem = pl.BlockSpec(memory_space=pltpu.SMEM)
     return pl.pallas_call(
         kernel,
         out_shape=(
             jax.ShapeDtypeStruct((half, rows_out, width), F32),
             jax.ShapeDtypeStruct((half, rows_out, width), BF16),
         ),
-        in_specs=[smem, smem] + [ANY] * (len(values) + len(after)),
+        in_specs=[SMEM] * 3 + [ANY] * (len(values) + len(after)),
         out_specs=(VMEM,) * 2,
         scratch_shapes=[
             pltpu.VMEM((width, rows_dev), BF16),
@@ -332,7 +354,7 @@
         ],
         compiler_params=pltpu.CompilerParams(vmem_limit_bytes=2 * touched + 2 * MIB),
         cost_estimate=pl.CostEstimate(flops=0, bytes_accessed=0, transcendentals=0),
-    )(col.reshape(1), me.reshape(1), *values, *after)
+    )(col.reshape(1), me.reshape(1), outer, *values, *after)
 
 
 def swap(value, axis, k):
@@ -350,15 +372,26 @@
     chips = tuple(range(0, n_rows, 2))
     block_count, unused_slots, tile, unused_side = tile_values.shape
     small = block_count // 2
-    gathers = (block_count - small, small) if small else (block_count,)
-    scatters = gathers[::-1]
+    gathers = (block_count,)
+    scatters = (block_count,)
+
+    line = n_cols == 4
+    outer = ((col == 0) | (col == n_cols - 1)).astype(jnp.int32).reshape(1)
+
+    def over_cols(value):
+        if not line:
+            return [(value,)] + [(swap(value, "cols", k),) for k in cols_order[1:]]
+        far = swap(value, "cols", 2)
+        across = lax.ppermute(value, "cols", [(1, 2), (2, 1)])
+        near = swap(value, "cols", 1)
+        return [(value,), (near,), (far,), (across, swap(far, "cols", 1))]
 
     x = features.T
     x_parts, start = [], 0
     for count in gathers:
-        piece = x[:, start * tile : (start + count) * tile]
-        x_parts.append([piece] + [swap(piece, "cols", k) for k in cols_order[1:]])
+        piece = x if len(gathers) == 1 else x[:, start * tile : (start + count) * tile]
         start += count
+        x_parts.append(over_cols(piece))
     weight_down = [
         lax.dynamic_slice(weight, ((col ^ k) * width, col * width), (width, width))
         for k in cols_order
@@ -371,7 +404,7 @@
     order = tuple(k + c for c in (0, 1) for k in chips)
     shards = []
     for parts in x_parts:
-        hidden = sum_dots(weight_down, parts, ((0,), (0,)))
+        hidden = sum_dots(weight_down, parts, ((0,), (0,)), outer)
         own = [hidden] + [swap(hidden, "rows", k) for k in chips[1:]]
         shards.append(own + [swap(part, "rows", 1) for part in own])
 
@@ -395,7 +428,7 @@
         sums = chip_sums(keep, got, arrived)
         arrived = tuple(swap(v, "rows", k) for v, k in zip(sums, chips[1:]))
         grad = add_up((keep, got, *arrived), BF16)
-        grads.append([grad] + [swap(grad, "cols", k) for k in cols_order[1:]])
+        grads.append(over_cols(grad))
 
     keep, send = weight_parts(
         1.0 / math.sqrt(rows_dev * n_rows),
@@ -403,9 +436,10 @@
         order,
         col,
         me,
-        [g[0] for g in grads],
+        outer,
+        [g[0][0] for g in grads],
         list(zip(*x_parts)),
-        tuple(grads[0][1:]) if len(grads) > 1 else (),
+        tuple(grads[0][1]),
     )
     got = swap(send, "rows", 1)
     sums = chip_sums(keep, got)
@@ -413,7 +447,7 @@
 
     for c, values in enumerate(grads):
         last = (weight_grad,) if c + 1 == len(grads) else ()
-        input_grad = (sum_dots(weight_across, values, ((1,), (0,)), input_grad, last),)
+        input_grad = (sum_dots(weight_across, values, ((1,), (0,)), outer, input_grad, last),)
     return (act.T, input_grad[0].T, weight_grad)
 
 

time: 129 us -> 129 us (level); the launches traced: 127 us -> 129 us
  waiting for transfers between devices: 55.3 us -> 73.6 us
  starting transfers between devices: 44.9 us -> 31.6 us
  local copies, waits for them, and re-layouts: 6.4 us -> 3.89 us
    ppermute x38 -> x21, waiting for transfers between devices: 55.3 us -> 73.6 us  [swap(): lax.ppermute(value, axis, [(i, i ^ k) for i in range(lax.axis_size(axis))])]
    ppermute x38 -> x21, starting transfers between devices: 44.9 us -> 30.2 us  [swap(): lax.ppermute(value, axis, [(i, i ^ k) for i in range(lax.axis_size(axis))])]
    slice x2 -> x0, local copies, waits for them, and re-layouts: 1.88 us -> none  [local(): piece = x[:, start * tile:(start + count) * tile]]
    ppermute x0 -> x2, starting transfers between devices: none -> 1.36 us  [over_cols(): across = lax.ppermute(value, 'cols', [(1, 2), (2, 1)])]
    pallas_call x10 -> x6, Pallas kernels: 4.5 us -> 4.16 us  [small_call(): pl.pallas_call(kernel, out_shape=out_shape, in_specs=[SMEM] * len(scalars...]
  transfers between devices with their start and end apart: 38 -> 23, of which waited for: 16 -> 12; matrix products, arithmetic and copies ran while one was open for 3% -> 2% of each run, Pallas kernels for 2% -> 2%
where the time goes in v5:
time: 129 us
  waiting for transfers between devices  73.6 us (57%)
  starting transfers between devices  31.6 us (24%)
  Pallas kernels  19.5 us (15%)
  local copies, waits for them, and re-layouts  3.89 us (3%)
    ppermute x21, waiting for transfers between devices, swap(): lax.ppermute(value, axis, [(i, i ^ k) for i in range(lax.axis_size(axis))])  73.6 us
    ppermute x21, starting transfers between devices, swap(): lax.ppermute(value, axis, [(i, i ^ k) for i in range(lax.axis_size(axis))])  30.2 us
    pallas_call x1, Pallas kernels, tile_products(): pl.pallas_call(functools.partial(tile_kernel, slots, tile, group, shard_o...  13.3 us
    pallas_call x6, Pallas kernels, small_call(): pl.pallas_call(kernel, out_shape=out_shape, in_specs=[SMEM] * len(scalars...  4.16 us
    dynamic_slice x1, local copies, waits for them, and re-layouts, local(): lax.dynamic_slice(weight, (col * width, (col ^ k) * width), (width, width))  2.76 us
  transfers between devices with their start and end apart: 23, of which 12 were waited for; matrix products, arithmetic and copies ran while one was open for 2% of the time, Pallas kernels for 2%

profile of v5, /device:TPU:0, one launch (start us, length us, event | category | flops | bytes accessed | tf_op | source)
XLA Modules:
  0.0 129.3 jit_solution(13401417303109351378)
XLA Ops:
  0.6 4.1 %collective-permute-start.1 = (bf16[288,640]{1,0:T(8,128)(2,1)}, bf16[288,640]{1,0:T(8,128)(2,1)S(1)}, u32[]{:S(2)}, u32[]{:S(2)}) collective-permute-start(bf16[288,640]{1,0:T(8,128)(2,1)} %bitcast.7), channel_id=1, source_target_pairs={{0,2},{1,3},{2,0},{3,1},{4,6},{5,7},{6,4},{7,5},{8,10},{9,11},{10,... | collective-permute-start | bytes 1105928 | tf_op jit(solution)/shard_map/ppermute | solution.py:361
  4.7 0.7 collective-permute-start.2
  5.4 2.9 %collective-permute-start = (bf16[288,640]{1,0:T(8,128)(2,1)}, bf16[288,640]{1,0:T(8,128)(2,1)S(1)}, u32[]{:S(2)}, u32[]{:S(2)}) collective-permute-start(bf16[288,640]{1,0:T(8,128)(2,1)} %bitcast.9), channel_id=1, source_target_pairs={{0,1},{1,0},{2,3},{3,2},{4,5},{5,4},{6,7},{7,6},{8,9},{9,8},{10,11... | collective-permute-start | bytes 1105928 | tf_op jit(solution)/shard_map/ppermute | solution.py:361
  8.3 14.0 %collective-permute-done.1.refs_6_.refs_3_ = bf16[288,640]{1,0:T(8,128)(2,1)S(1)} collective-permute-done((bf16[288,640]{1,0:T(8,128)(2,1)}, bf16[288,640]{1,0:T(8,128)(2,1)S(1)}, u32[]{:S(2)}, u32[]{:S(2)}) %collective-permute-start.1) | collective-permute-done | bytes 368672 | tf_op jit(solution)/shard_map/ppermute | solution.py:361
  22.3 0.1 collective-permute-start.3
  22.4 2.8 %fusion = (bf16[288,288]{1,0:T(8,128)(2,1)S(1)}, bf16[288,288]{1,0:T(8,128)(2,1)S(1)}, bf16[288,288]{1,0:T(8,128)(2,1)S(1)}, bf16[288,288]{1,0:T(8,128)(2,1)S(1)...) fusion(bf16[1152,1152]{1,0:T(8,128)(2,1)} %param.8, s32[]{:T(128)S(6)} %select_n.8, ...), kind=kLoop, calls=%fused_computation | loop fusion | bytes 2322448 | tf_op jit(solution)/shard_map/dynamic_slice | solution.py:400
  25.2 6.3 %collective-permute-done.3.refs_8_.refs_5_ = bf16[288,640]{1,0:T(8,128)(2,1)S(1)} collective-permute-done((bf16[288,640]{1,0:T(8,128)(2,1)S(1)}, bf16[288,640]{1,0:T(8,128)(2,1)S(1)}, u32[]{:S(2)}, u32[]{:S(2)}) %collective-permute-start.3) | collective-permute-done | bytes 368672 | tf_op jit(solution)/shard_map/ppermute | solution.py:361
  31.5 1.0 shard_map.94.rest_0_
  32.5 0.0 copy-start.2
  32.5 2.6 %collective-permute-start.6 = (bf16[288,640]{1,0:T(8,128)(2,1)S(1)}, bf16[288,640]{1,0:T(8,128)(2,1)}, u32[]{:S(2)}, u32[]{:S(2)}) collective-permute-start(bf16[288,640]{1,0:T(8,128)(2,1)S(1)} %shard_map.94.rest_0_), channel_id=1, source_target_pairs={{0,24},{4,28},{8,16},{12,20},{16,8},{20,12},{24,0},{28,4},{1,25},{... | collective-permute-start | bytes 1105928 | tf_op jit(solution)/shard_map/ppermute | solution.py:361
  35.1 0.5 collective-permute-start.5
  35.6 0.5 collective-permute-start.4
  36.1 9.0 %collective-permute-done.6.rest_3_ = bf16[288,640]{1,0:T(8,128)(2,1)} collective-permute-done((bf16[288,640]{1,0:T(8,128)(2,1)S(1)}, bf16[288,640]{1,0:T(8,128)(2,1)}, u32[]{:S(2)}, u32[]{:S(2)}) %collective-permute-start.6) | collective-permute-done | bytes 368672 | tf_op jit(solution)/shard_map/ppermute | solution.py:361
  45.1 0.0 collective-permute-start.10
  45.1 4.8 %collective-permute-done.5.rest_2_ = bf16[288,640]{1,0:T(8,128)(2,1)} collective-permute-done((bf16[288,640]{1,0:T(8,128)(2,1)S(1)}, bf16[288,640]{1,0:T(8,128)(2,1)}, u32[]{:S(2)}, u32[]{:S(2)}) %collective-permute-start.5) | collective-permute-done | bytes 368672 | tf_op jit(solution)/shard_map/ppermute | solution.py:361
  49.9 0.0 collective-permute-start.9
  50.0 0.5 collective-permute-start.8
  50.5 0.1 reshape.21.coords_ref
  50.5 0.1 broadcast_in_dim.4.bias_ref
  50.6 0.0 collective-permute-done.7.rest_4_
  50.7 1.3 %collective-permute-done.9.rest_6_ = bf16[288,640]{1,0:T(8,128)(2,1)} collective-permute-done((bf16[288,640]{1,0:T(8,128)(2,1)}, bf16[288,640]{1,0:T(8,128)(2,1)}, u32[]{:S(2)}, u32[]{:S(2)}) %collective-permute-start.9) | collective-permute-done | bytes 368672 | tf_op jit(solution)/shard_map/ppermute | solution.py:361
  52.0 0.5 collective-permute-done.8.rest_5_
  52.5 13.3 %shard_map.95 = (bf16[288,640]{1,0:T(8,128)(2,1)}, bf16[4,288,640]{2,1,0:T(8,128)(2,1)S(1)}, bf16[4,288,640]{2,1,0:T(8,128)(2,1)S(1)}) custom-call(s32[240]{0:T(256)S(1)} %reshape.21.coords_ref, s32[5]{0:T(128)S(1)} %copy-done.4, s32[1]{0:T(128)} %bitcast.me_ref, f32[288,1]{1,0:T(8,128)S(1)} %broadcast_in_dim.4.bias_ref, bf16[288,640]{1,0:T(8,128)(2,1)S(1)} %bitcast.12, ...), custom_call_target="tpu_custom_call" | custom-call | flops 4529848320 | bytes 7864320 | tf_op jit(solution)/shard_map/pallas_call | solution.py:163
  65.8 2.5 %collective-permute-start.11 = (bf16[4,288,640]{2,1,0:T(8,128)(2,1)S(1)}, bf16[4,288,640]{2,1,0:T(8,128)(2,1)S(1)}, u32[]{:S(2)}, u32[]{:S(2)}) collective-permute-start(bf16[4,288,640]{2,1,0:T(8,128)(2,1)S(1)} %get-tuple-element.16), channel_id=1, source_target_pairs={{0,4},{4,0},{8,12},{12,8},{16,20},{20,16},{24,28},{28,24},{1,5},{5... | collective-permute-start | bytes 4423688 | tf_op jit(solution)/shard_map/ppermute | solution.py:361
  68.4 2.9 %collective-permute-done.11.got_ref.refs_1_ = bf16[4,288,640]{2,1,0:T(8,128)(2,1)S(1)} collective-permute-done((bf16[4,288,640]{2,1,0:T(8,128)(2,1)S(1)}, bf16[4,288,640]{2,1,0:T(8,128)(2,1)S(1)}, u32[]{:S(2)}, u32[]{:S(2)}) %collective-permute-start.11) | collective-permute-done | bytes 1474592 | tf_op jit(solution)/shard_map/ppermute | solution.py:361
  71.3 0.3 shard_map.96
  71.6 1.8 %collective-permute-start.12 = (bf16[288,640]{1,0:T(8,128)(2,1)S(1)}, bf16[288,640]{1,0:T(8,128)(2,1)S(1)}, u32[]{:S(2)}, u32[]{:S(2)}) collective-permute-start(bf16[288,640]{1,0:T(8,128)(2,1)S(1)} %get-tuple-element.17), channel_id=1, source_target_pairs={{0,8},{4,12},{8,0},{12,4},{16,24},{20,28},{24,16},{28,20},{1,9},{5... | collective-permute-start | bytes 1105928 | tf_op jit(solution)/shard_map/ppermute | solution.py:361
  73.3 3.0 %collective-permute-start.13 = (bf16[288,640]{1,0:T(8,128)(2,1)S(1)}, bf16[288,640]{1,0:T(8,128)(2,1)S(1)}, u32[]{:S(2)}, u32[]{:S(2)}) collective-permute-start(bf16[288,640]{1,0:T(8,128)(2,1)S(1)} %get-tuple-element.18), channel_id=1, source_target_pairs={{0,16},{4,20},{8,24},{12,28},{16,0},{20,4},{24,8},{28,12},{1,17},{... | collective-permute-start | bytes 1105928 | tf_op jit(solution)/shard_map/ppermute | solution.py:361
  76.4 6.7 %collective-permute-done.12.refs_2_ = bf16[288,640]{1,0:T(8,128)(2,1)S(1)} collective-permute-done((bf16[288,640]{1,0:T(8,128)(2,1)S(1)}, bf16[288,640]{1,0:T(8,128)(2,1)S(1)}, u32[]{:S(2)}, u32[]{:S(2)}) %collective-permute-start.12) | collective-permute-done | bytes 368672 | tf_op jit(solution)/shard_map/ppermute | solution.py:361
  83.0 10.0 %collective-permute-done.13.refs_3_ = bf16[288,640]{1,0:T(8,128)(2,1)S(1)} collective-permute-done((bf16[288,640]{1,0:T(8,128)(2,1)S(1)}, bf16[288,640]{1,0:T(8,128)(2,1)S(1)}, u32[]{:S(2)}, u32[]{:S(2)}) %collective-permute-start.13) | collective-permute-done | bytes 368672 | tf_op jit(solution)/shard_map/ppermute | solution.py:361
  93.1 0.3 shard_map.97.refs_0_.refs_4_
  93.4 2.6 %collective-permute-start.15 = (bf16[288,640]{1,0:T(8,128)(2,1)S(1)}, bf16[288,640]{1,0:T(8,128)(2,1)S(1)}, u32[]{:S(2)}, u32[]{:S(2)}) collective-permute-start(bf16[288,640]{1,0:T(8,128)(2,1)S(1)} %shard_map.97.refs_0_.refs_4_), channel_id=1, source_target_pairs={{0,1},{1,0},{2,3},{3,2},{4,5},{5,4},{6,7},{7,6},{8,9},{9,8},{10,11... | collective-permute-start | bytes 1105928 | tf_op jit(solution)/shard_map/ppermute | solution.py:361
  95.9 3.3 %collective-permute-start.16 = (bf16[288,640]{1,0:T(8,128)(2,1)S(1)}, bf16[288,640]{1,0:T(8,128)(2,1)S(1)}, u32[]{:S(2)}, u32[]{:S(2)}) collective-permute-start(bf16[288,640]{1,0:T(8,128)(2,1)S(1)} %shard_map.97.refs_0_.refs_4_), channel_id=1, source_target_pairs={{0,2},{1,3},{2,0},{3,1},{4,6},{5,7},{6,4},{7,5},{8,10},{9,11},{10,... | collective-permute-start | bytes 1105928 | tf_op jit(solution)/shard_map/ppermute | solution.py:361
  99.2 12.9 %collective-permute-done.15.refs_6_.refs_5_ = bf16[288,640]{1,0:T(8,128)(2,1)S(1)} collective-permute-done((bf16[288,640]{1,0:T(8,128)(2,1)S(1)}, bf16[288,640]{1,0:T(8,128)(2,1)S(1)}, u32[]{:S(2)}, u32[]{:S(2)}) %collective-permute-start.15) | collective-permute-done | bytes 368672 | tf_op jit(solution)/shard_map/ppermute | solution.py:361
  112.1 2.0 %shard_map.98 = (f32[4,144,288]{2,1,0:T(8,128)S(1)}, bf16[4,144,288]{2,1,0:T(8,128)(2,1)S(1)}) custom-call(s32[1]{0:T(128)} %bitcast.5.col_ref, s32[1]{0:T(128)} %bitcast.me_ref, s32[1]{0:T(128)} %bitcast.2.outer_ref, bf16[288,640]{1,0:T(8,128)(2,1)S(1)} %shard_map.97.refs_0_.refs_4_, bf16[288,640]{1,0:T(8,128)(2,1)S(1)} %bitcast.11, ...), custom_call_target="tpu_custom_call" | custom-call | tf_op jit(solution)/shard_map/pallas_call | solution.py:341
  114.1 0.1 collective-permute-start.19
  114.2 0.7 collective-permute-start.17
  114.9 0.0 collective-permute-done.16.refs_6_
  114.9 2.3 %collective-permute-start.18 = (bf16[288,640]{1,0:T(8,128)(2,1)S(1)}, bf16[288,640]{1,0:T(8,128)(2,1)S(1)}, u32[]{:S(2)}, u32[]{:S(2)}) collective-permute-start(bf16[288,640]{1,0:T(8,128)(2,1)S(1)} %collective-permute-done.16.refs_6_), channel_id=1, source_target_pairs={{0,1},{1,0},{2,3},{3,2},{4,5},{5,4},{6,7},{7,6},{8,9},{9,8},{10,11... | collective-permute-start | bytes 1105928 | tf_op jit(solution)/shard_map/ppermute | solution.py:361
  117.2 0.1 shard_map.99
  117.3 1.5 %collective-permute-start.20 = (bf16[144,288]{1,0:T(8,128)(2,1)S(1)}, bf16[144,288]{1,0:T(8,128)(2,1)S(1)}, u32[]{:S(2)}, u32[]{:S(2)}) collective-permute-start(bf16[144,288]{1,0:T(8,128)(2,1)S(1)} %get-tuple-element.22), channel_id=1, source_target_pairs={{0,8},{4,12},{8,0},{12,4},{16,24},{20,28},{24,16},{28,20},{1,9},{5... | collective-permute-start | bytes 248840 | tf_op jit(solution)/shard_map/ppermute | solution.py:361
  118.8 0.6 collective-permute-start.21
  119.4 1.4 %collective-permute-start.22 = (bf16[144,288]{1,0:T(8,128)(2,1)S(1)}, bf16[144,288]{1,0:T(8,128)(2,1)S(1)}, u32[]{:S(2)}, u32[]{:S(2)}) collective-permute-start(bf16[144,288]{1,0:T(8,128)(2,1)S(1)} %get-tuple-element.24), channel_id=1, source_target_pairs={{0,24},{4,28},{8,16},{12,20},{16,8},{20,12},{24,0},{28,4},{1,25},{... | collective-permute-start | bytes 248840 | tf_op jit(solution)/shard_map/ppermute | solution.py:361
  120.8 1.4 %collective-permute-done.20.refs_2_ = bf16[144,288]{1,0:T(8,128)(2,1)S(1)} collective-permute-done((bf16[144,288]{1,0:T(8,128)(2,1)S(1)}, bf16[144,288]{1,0:T(8,128)(2,1)S(1)}, u32[]{:S(2)}, u32[]{:S(2)}) %collective-permute-start.20) | collective-permute-done | bytes 82976 | tf_op jit(solution)/shard_map/ppermute | solution.py:361
  122.2 3.6 %collective-permute-done.21.refs_3_ = bf16[144,288]{1,0:T(8,128)(2,1)S(1)} collective-permute-done((bf16[144,288]{1,0:T(8,128)(2,1)S(1)}, bf16[144,288]{1,0:T(8,128)(2,1)S(1)}, u32[]{:S(2)}, u32[]{:S(2)}) %collective-permute-start.21) | collective-permute-done | bytes 82976 | tf_op jit(solution)/shard_map/ppermute | solution.py:361
  125.8 0.8 shard_map.100.refs_9_
  126.6 0.9 copy-done.1
  127.5 1.8 %shard_map.101 = bf16[288,640]{1,0:T(8,128)(2,1)} custom-call(s32[1]{0:T(128)} %bitcast.2.outer_ref, bf16[288,288]{1,0:T(8,128)(2,1)S(1)} %get-tuple-element.30.refs_0_, bf16[288,288]{1,0:T(8,128)(2,1)S(1)} %get-tuple-element.26.refs_1_, bf16[288,288]{1,0:T(8,128)(2,1)S(1)} %get-tuple-element.31.refs_2_, bf16[288,288]{1,0:T(8,128)(2,1)S(1)} %get-tuple-element.25.refs_3_, ...), custom_call_target="tpu_custom_call" | custom-call | tf_op jit(solution)/shard_map/pallas_call | solution.py:207
  (23 shorter events, 0.1 us)
Async XLA Ops:
  0.6 30.8 %copy-start = (bf16[640,288]{0,1:T(8,128)(2,1)S(1)}, bf16[640,288]{0,1:T(8,128)(2,1)}, u32[]{:S(2)}) copy-start(bf16[640,288]{0,1:T(8,128)(2,1)} %param.7) | copy-start | bytes 1105924
  0.6 21.7 %collective-permute-start.1 = (bf16[288,640]{1,0:T(8,128)(2,1)}, bf16[288,640]{1,0:T(8,128)(2,1)S(1)}, u32[]{:S(2)}, u32[]{:S(2)}) collective-permute-start(bf16[288,640]{1,0:T(8,128)(2,1)} %bitcast.7), channel_id=1, source_target_pairs={{0,2},{1,3},{2,0},{3,1},{4,6},{5,7},{6,4},{7,5},{8,10},{9,11},{10,... | collective-permute-start | bytes 1105928 | tf_op jit(solution)/shard_map/ppermute | solution.py:361
  4.7 20.4 %collective-permute-start.2 = (bf16[288,640]{1,0:T(8,128)(2,1)}, bf16[288,640]{1,0:T(8,128)(2,1)S(1)}, u32[]{:S(2)}, u32[]{:S(2)}) collective-permute-start(bf16[288,640]{1,0:T(8,128)(2,1)} %bitcast.8), channel_id=1, source_target_pairs={{1,2},{2,1},{5,6},{6,5},{9,10},{10,9},{13,14},{14,13},{17,18},{18,... | collective-permute-start | bytes 1105928 | tf_op jit(solution)/shard_map/ppermute | solution.py:385
  5.4 19.8 %collective-permute-start = (bf16[288,640]{1,0:T(8,128)(2,1)}, bf16[288,640]{1,0:T(8,128)(2,1)S(1)}, u32[]{:S(2)}, u32[]{:S(2)}) collective-permute-start(bf16[288,640]{1,0:T(8,128)(2,1)} %bitcast.9), channel_id=1, source_target_pairs={{0,1},{1,0},{2,3},{3,2},{4,5},{5,4},{6,7},{7,6},{8,9},{9,8},{10,11... | collective-permute-start | bytes 1105928 | tf_op jit(solution)/shard_map/ppermute | solution.py:361
  22.3 9.1 %collective-permute-start.3 = (bf16[288,640]{1,0:T(8,128)(2,1)S(1)}, bf16[288,640]{1,0:T(8,128)(2,1)S(1)}, u32[]{:S(2)}, u32[]{:S(2)}) collective-permute-start(bf16[288,640]{1,0:T(8,128)(2,1)S(1)} %collective-permute-done.1.refs_6_.refs_3_), channel_id=1, source_target_pairs={{0,1},{1,0},{2,3},{3,2},{4,5},{5,4},{6,7},{7,6},{8,9},{9,8},{10,11... | collective-permute-start | bytes 1105928 | tf_op jit(solution)/shard_map/ppermute | solution.py:361
  22.4 28.0 %copy-start.5 = (s32[5,48]{1,0:T(8,128)S(1)}, s32[5,48]{1,0:T(8,128)}, u32[]{:S(2)}) copy-start(s32[5,48]{1,0:T(8,128)} %param.11) | copy-start | bytes 2884
  22.4 28.1 %copy-start.6 = (f32[288]{0:T(512)S(1)}, f32[288]{0:T(512)}, u32[]{:S(2)}) copy-start(f32[288]{0:T(512)} %param.9) | copy-start | bytes 3460
  22.4 30.1 %copy-start.3 = (bf16[640,288]{0,1:T(8,128)(2,1)S(1)}, bf16[640,288]{0,1:T(8,128)(2,1)}, u32[]{:S(2)}) copy-start(bf16[640,288]{0,1:T(8,128)(2,1)} %param.13) | copy-start | bytes 1105924
  22.4 30.1 %copy-start.4 = (s32[5]{0:T(128)S(1)}, s32[5]{0:T(128)}, u32[]{:S(2)}) copy-start(s32[5]{0:T(128)} %counts_ref.1) | copy-start | bytes 64
  32.5 20.0 %copy-start.2 = (bf16[288,640]{1,0:T(8,128)(2,1)}, bf16[288,640]{1,0:T(8,128)(2,1)S(1)}, u32[]{:S(2)}) copy-start(bf16[288,640]{1,0:T(8,128)(2,1)S(1)} %shard_map.94.rest_0_) | copy-start | bytes 1105924
  32.5 12.6 %collective-permute-start.6 = (bf16[288,640]{1,0:T(8,128)(2,1)S(1)}, bf16[288,640]{1,0:T(8,128)(2,1)}, u32[]{:S(2)}, u32[]{:S(2)}) collective-permute-start(bf16[288,640]{1,0:T(8,128)(2,1)S(1)} %shard_map.94.rest_0_), channel_id=1, source_target_pairs={{0,24},{4,28},{8,16},{12,20},{16,8},{20,12},{24,0},{28,4},{1,25},{... | collective-permute-start | bytes 1105928 | tf_op jit(solution)/shard_map/ppermute | solution.py:361
  35.1 14.8 %collective-permute-start.5 = (bf16[288,640]{1,0:T(8,128)(2,1)S(1)}, bf16[288,640]{1,0:T(8,128)(2,1)}, u32[]{:S(2)}, u32[]{:S(2)}) collective-permute-start(bf16[288,640]{1,0:T(8,128)(2,1)S(1)} %shard_map.94.rest_0_), channel_id=1, source_target_pairs={{0,16},{4,20},{8,24},{12,28},{16,0},{20,4},{24,8},{28,12},{1,17},{... | collective-permute-start | bytes 1105928 | tf_op jit(solution)/shard_map/ppermute | solution.py:361
  35.6 14.4 %collective-permute-start.4 = (bf16[288,640]{1,0:T(8,128)(2,1)S(1)}, bf16[288,640]{1,0:T(8,128)(2,1)}, u32[]{:S(2)}, u32[]{:S(2)}) collective-permute-start(bf16[288,640]{1,0:T(8,128)(2,1)S(1)} %shard_map.94.rest_0_), channel_id=1, source_target_pairs={{0,8},{4,12},{8,0},{12,4},{16,24},{20,28},{24,16},{28,20},{1,9},{5... | collective-permute-start | bytes 1105928 | tf_op jit(solution)/shard_map/ppermute | solution.py:361
  36.1 14.6 %collective-permute-start.7 = (bf16[288,640]{1,0:T(8,128)(2,1)S(1)}, bf16[288,640]{1,0:T(8,128)(2,1)}, u32[]{:S(2)}, u32[]{:S(2)}) collective-permute-start(bf16[288,640]{1,0:T(8,128)(2,1)S(1)} %shard_map.94.rest_0_), channel_id=1, source_target_pairs={{0,4},{4,0},{8,12},{12,8},{16,20},{20,16},{24,28},{28,24},{1,5},{5... | collective-permute-start | bytes 1105928 | tf_op jit(solution)/shard_map/ppermute | solution.py:361
  45.1 5.5 %collective-permute-start.10 = (bf16[288,640]{1,0:T(8,128)(2,1)}, bf16[288,640]{1,0:T(8,128)(2,1)}, u32[]{:S(2)}, u32[]{:S(2)}) collective-permute-start(bf16[288,640]{1,0:T(8,128)(2,1)} %collective-permute-done.6.rest_3_), channel_id=1, source_target_pairs={{0,4},{4,0},{8,12},{12,8},{16,20},{20,16},{24,28},{28,24},{1,5},{5... | collective-permute-start | bytes 1105928 | tf_op jit(solution)/shard_map/ppermute | solution.py:361
  49.9 2.0 %collective-permute-start.9 = (bf16[288,640]{1,0:T(8,128)(2,1)}, bf16[288,640]{1,0:T(8,128)(2,1)}, u32[]{:S(2)}, u32[]{:S(2)}) collective-permute-start(bf16[288,640]{1,0:T(8,128)(2,1)} %collective-permute-done.5.rest_2_), channel_id=1, source_target_pairs={{0,4},{4,0},{8,12},{12,8},{16,20},{20,16},{24,28},{28,24},{1,5},{5... | collective-permute-start | bytes 1105928 | tf_op jit(solution)/shard_map/ppermute | solution.py:361
  50.0 2.5 %collective-permute-start.8 = (bf16[288,640]{1,0:T(8,128)(2,1)}, bf16[288,640]{1,0:T(8,128)(2,1)}, u32[]{:S(2)}, u32[]{:S(2)}) collective-permute-start(bf16[288,640]{1,0:T(8,128)(2,1)} %collective-permute-done.4.rest_1_), channel_id=1, source_target_pairs={{0,4},{4,0},{8,12},{12,8},{16,20},{20,16},{24,28},{28,24},{1,5},{5... | collective-permute-start | bytes 1105928 | tf_op jit(solution)/shard_map/ppermute | solution.py:361
  65.8 5.4 %collective-permute-start.11 = (bf16[4,288,640]{2,1,0:T(8,128)(2,1)S(1)}, bf16[4,288,640]{2,1,0:T(8,128)(2,1)S(1)}, u32[]{:S(2)}, u32[]{:S(2)}) collective-permute-start(bf16[4,288,640]{2,1,0:T(8,128)(2,1)S(1)} %get-tuple-element.16), channel_id=1, source_target_pairs={{0,4},{4,0},{8,12},{12,8},{16,20},{20,16},{24,28},{28,24},{1,5},{5... | collective-permute-start | bytes 4423688 | tf_op jit(solution)/shard_map/ppermute | solution.py:361
  71.6 11.5 %collective-permute-start.12 = (bf16[288,640]{1,0:T(8,128)(2,1)S(1)}, bf16[288,640]{1,0:T(8,128)(2,1)S(1)}, u32[]{:S(2)}, u32[]{:S(2)}) collective-permute-start(bf16[288,640]{1,0:T(8,128)(2,1)S(1)} %get-tuple-element.17), channel_id=1, source_target_pairs={{0,8},{4,12},{8,0},{12,4},{16,24},{20,28},{24,16},{28,20},{1,9},{5... | collective-permute-start | bytes 1105928 | tf_op jit(solution)/shard_map/ppermute | solution.py:361
  73.3 19.8 %collective-permute-start.13 = (bf16[288,640]{1,0:T(8,128)(2,1)S(1)}, bf16[288,640]{1,0:T(8,128)(2,1)S(1)}, u32[]{:S(2)}, u32[]{:S(2)}) collective-permute-start(bf16[288,640]{1,0:T(8,128)(2,1)S(1)} %get-tuple-element.18), channel_id=1, source_target_pairs={{0,16},{4,20},{8,24},{12,28},{16,0},{20,4},{24,8},{28,12},{1,17},{... | collective-permute-start | bytes 1105928 | tf_op jit(solution)/shard_map/ppermute | solution.py:361
  76.4 16.7 %collective-permute-start.14 = (bf16[288,640]{1,0:T(8,128)(2,1)S(1)}, bf16[288,640]{1,0:T(8,128)(2,1)S(1)}, u32[]{:S(2)}, u32[]{:S(2)}) collective-permute-start(bf16[288,640]{1,0:T(8,128)(2,1)S(1)} %get-tuple-element.19), channel_id=1, source_target_pairs={{0,24},{4,28},{8,16},{12,20},{16,8},{20,12},{24,0},{28,4},{1,25},{... | collective-permute-start | bytes 1105928 | tf_op jit(solution)/shard_map/ppermute | solution.py:361
  93.4 18.8 %collective-permute-start.15 = (bf16[288,640]{1,0:T(8,128)(2,1)S(1)}, bf16[288,640]{1,0:T(8,128)(2,1)S(1)}, u32[]{:S(2)}, u32[]{:S(2)}) collective-permute-start(bf16[288,640]{1,0:T(8,128)(2,1)S(1)} %shard_map.97.refs_0_.refs_4_), channel_id=1, source_target_pairs={{0,1},{1,0},{2,3},{3,2},{4,5},{5,4},{6,7},{7,6},{8,9},{9,8},{10,11... | collective-permute-start | bytes 1105928 | tf_op jit(solution)/shard_map/ppermute | solution.py:361
  95.9 19.0 %collective-permute-start.16 = (bf16[288,640]{1,0:T(8,128)(2,1)S(1)}, bf16[288,640]{1,0:T(8,128)(2,1)S(1)}, u32[]{:S(2)}, u32[]{:S(2)}) collective-permute-start(bf16[288,640]{1,0:T(8,128)(2,1)S(1)} %shard_map.97.refs_0_.refs_4_), channel_id=1, source_target_pairs={{0,2},{1,3},{2,0},{3,1},{4,6},{5,7},{6,4},{7,5},{8,10},{9,11},{10,... | collective-permute-start | bytes 1105928 | tf_op jit(solution)/shard_map/ppermute | solution.py:361
  114.1 3.1 %collective-permute-start.19 = (bf16[4,144,288]{2,1,0:T(8,128)(2,1)S(1)}, bf16[4,144,288]{2,1,0:T(8,128)(2,1)S(1)}, u32[]{:S(2)}, u32[]{:S(2)}) collective-permute-start(bf16[4,144,288]{2,1,0:T(8,128)(2,1)S(1)} %get-tuple-element.21), channel_id=1, source_target_pairs={{0,4},{4,0},{8,12},{12,8},{16,20},{20,16},{24,28},{28,24},{1,5},{5... | collective-permute-start | bytes 995336 | tf_op jit(solution)/shard_map/ppermute | solution.py:361
  114.2 12.4 %collective-permute-start.17 = (bf16[288,640]{1,0:T(8,128)(2,1)S(1)}, bf16[288,640]{1,0:T(8,128)(2,1)S(1)}, u32[]{:S(2)}, u32[]{:S(2)}) collective-permute-start(bf16[288,640]{1,0:T(8,128)(2,1)S(1)} %shard_map.97.refs_0_.refs_4_), channel_id=1, source_target_pairs={{1,2},{2,1},{5,6},{6,5},{9,10},{10,9},{13,14},{14,13},{17,18},{18,... | collective-permute-start | bytes 1105928 | tf_op jit(solution)/shard_map/ppermute | solution.py:385
  114.9 11.7 %collective-permute-start.18 = (bf16[288,640]{1,0:T(8,128)(2,1)S(1)}, bf16[288,640]{1,0:T(8,128)(2,1)S(1)}, u32[]{:S(2)}, u32[]{:S(2)}) collective-permute-start(bf16[288,640]{1,0:T(8,128)(2,1)S(1)} %collective-permute-done.16.refs_6_), channel_id=1, source_target_pairs={{0,1},{1,0},{2,3},{3,2},{4,5},{5,4},{6,7},{7,6},{8,9},{9,8},{10,11... | collective-permute-start | bytes 1105928 | tf_op jit(solution)/shard_map/ppermute | solution.py:361
  117.3 5.0 %collective-permute-start.20 = (bf16[144,288]{1,0:T(8,128)(2,1)S(1)}, bf16[144,288]{1,0:T(8,128)(2,1)S(1)}, u32[]{:S(2)}, u32[]{:S(2)}) collective-permute-start(bf16[144,288]{1,0:T(8,128)(2,1)S(1)} %get-tuple-element.22), channel_id=1, source_target_pairs={{0,8},{4,12},{8,0},{12,4},{16,24},{20,28},{24,16},{28,20},{1,9},{5... | collective-permute-start | bytes 248840 | tf_op jit(solution)/shard_map/ppermute | solution.py:361
  118.8 7.1 %collective-permute-start.21 = (bf16[144,288]{1,0:T(8,128)(2,1)S(1)}, bf16[144,288]{1,0:T(8,128)(2,1)S(1)}, u32[]{:S(2)}, u32[]{:S(2)}) collective-permute-start(bf16[144,288]{1,0:T(8,128)(2,1)S(1)} %get-tuple-element.23), channel_id=1, source_target_pairs={{0,16},{4,20},{8,24},{12,28},{16,0},{20,4},{24,8},{28,12},{1,17},{... | collective-permute-start | bytes 248840 | tf_op jit(solution)/shard_map/ppermute | solution.py:361
  119.4 6.4 %collective-permute-start.22 = (bf16[144,288]{1,0:T(8,128)(2,1)S(1)}, bf16[144,288]{1,0:T(8,128)(2,1)S(1)}, u32[]{:S(2)}, u32[]{:S(2)}) collective-permute-start(bf16[144,288]{1,0:T(8,128)(2,1)S(1)} %get-tuple-element.24), channel_id=1, source_target_pairs={{0,24},{4,28},{8,16},{12,20},{16,8},{20,12},{24,0},{28,4},{1,25},{... | collective-permute-start | bytes 248840 | tf_op jit(solution)/shard_map/ppermute | solution.py:361
  126.6 0.9 copy-start.1

commit v6 on v3

--- a/solution.py
+++ b/solution.py
@@ -230,20 +230,21 @@
     number = len(values)
 
     def kernel(*refs):
-        total = refs[0][...].astype(F32)
-        for ref in refs[1:number]:
-            total = total + ref[...].astype(F32)
+        total = None
+        for ref in refs[:number]:
+            value = (ref[0] if len(ref.shape) == 3 else ref[...]).astype(F32)
+            total = value if total is None else total + value
         refs[-1][...] = total.astype(dtype)
 
-    out = jax.ShapeDtypeStruct(values[0].shape, dtype)
+    out = jax.ShapeDtypeStruct(values[0].shape[-2:], dtype)
     return small_call(kernel, out, values, after)
 
 
-def chip_sums(keep, got, after=()):
-    number = keep.shape[0]
+def chip_sums(keep, got, after=(), first=0):
+    number = keep.shape[0] - first
 
     def kernel(keep_ref, got_ref, *refs):
-        for j, out_ref in enumerate(refs[len(after) :]):
+        for j, out_ref in enumerate(refs[len(after) :], first):
             out_ref[...] = (keep_ref[j].astype(F32) + got_ref[j].astype(F32)).astype(BF16)
 
     out = (jax.ShapeDtypeStruct(keep.shape[1:], BF16),) * number
@@ -261,7 +262,7 @@
 
     def kernel(col_ref, me_ref, *refs):
         inputs = refs[: len(values)]
-        own_ref, keep_ref, send_own_ref, send_ref, grad, xs, part, sems = refs[-8:]
+        keep_ref, send_ref, grad, xs, part, sems = refs[-6:]
         copies = []
 
         def fill(target, sources, first_sem):
@@ -288,28 +289,21 @@
         for j, k in enumerate(rows_order):
             start = pl.multiple_of((me_ref[0] ^ k) * rows_out, 8)
             value = part[pl.ds(start, rows_out), :]
-            if j == 0:
-                own_ref[...] = value
-            elif j < half:
-                keep_ref[j - 1] = value
-            elif j == half:
-                send_own_ref[...] = value.astype(BF16)
+            if j < half:
+                keep_ref[j] = value
             else:
-                send_ref[j - half - 1] = value.astype(BF16)
+                send_ref[j - half] = value.astype(BF16)
 
     touched = 2 * width * rows_dev * (len(cols_order) + 1) + 8 * width * width * len(cols_order)
     smem = pl.BlockSpec(memory_space=pltpu.SMEM)
-    others = max(half - 1, 1)
     return pl.pallas_call(
         kernel,
         out_shape=(
-            jax.ShapeDtypeStruct((rows_out, width), F32),
-            jax.ShapeDtypeStruct((others, rows_out, width), F32),
-            jax.ShapeDtypeStruct((rows_out, width), BF16),
-            jax.ShapeDtypeStruct((others, rows_out, width), BF16),
+            jax.ShapeDtypeStruct((half, rows_out, width), F32),
+            jax.ShapeDtypeStruct((half, rows_out, width), BF16),
         ),
         in_specs=[smem, smem] + [ANY] * (len(values) + len(after)),
-        out_specs=(VMEM,) * 4,
+        out_specs=(VMEM,) * 2,
         scratch_shapes=[
             pltpu.VMEM((width, rows_dev), BF16),
             pltpu.VMEM((len(cols_order), width, rows_dev), BF16),
@@ -383,7 +377,7 @@
         grad = add_up((keep_own, got_own, *arrived), BF16)
         grads.append([grad] + [swap(grad, "cols", k) for k in cols_order[1:]])
 
-    own, keep, send_own, send = weight_parts(
+    keep, send = weight_parts(
         1.0 / math.sqrt(rows_dev * n_rows),
         cols_order,
         order,
@@ -393,10 +387,9 @@
         list(zip(*x_parts)),
         tuple(grads[0][1:]) if len(grads) > 1 else (),
     )
-    got, got_own = swap(send, "rows", 1), swap(send_own, "rows", 1)
-    weight_grad = add_up(
-        (own, got_own, *[swap(v, "rows", k) for v, k in zip(chip_sums(keep, got), chips[1:])]), F32
-    )
+    got = swap(send, "rows", 1)
+    sums = chip_sums(keep, got, first=1)
+    weight_grad = add_up((keep, got, *[swap(v, "rows", k) for v, k in zip(sums, chips[1:])]), F32)
 
     for c, values in enumerate(grads):
         last = (weight_grad,) if c + 1 == len(grads) else ()

time: 131 us -> 130 us (level); the launches traced: 130 us -> 131 us
    ppermute x41 -> x40, waiting for transfers between devices: 54.9 us -> 55.9 us  [swap(): lax.ppermute(value, axis, [(i, i ^ k) for i in range(lax.axis_size(axis))])]
    ppermute x41 -> x40, starting transfers between devices: 51 us -> 50.6 us  [swap(): lax.ppermute(value, axis, [(i, i ^ k) for i in range(lax.axis_size(axis))])]
  transfers between devices with their start and end apart: 41 -> 40, of which waited for: 16 -> 17; matrix products, arithmetic and copies ran while one was open for 3% -> 3% of each run, Pallas kernels for 2% -> 2%
where the time goes in v6:
time: 130 us; the launch traced here: 131 us
  waiting for transfers between devices  55.9 us (43%)
  starting transfers between devices  50.6 us (39%)
  Pallas kernels  16.8 us (13%)
  local copies, waits for them, and re-layouts  6.39 us (5%)
    ppermute x40, waiting for transfers between devices, swap(): lax.ppermute(value, axis, [(i, i ^ k) for i in range(lax.axis_size(axis))])  55.9 us
    ppermute x40, starting transfers between devices, swap(): lax.ppermute(value, axis, [(i, i ^ k) for i in range(lax.axis_size(axis))])  50.6 us
    pallas_call x1, Pallas kernels, tile_products(): pl.pallas_call(functools.partial(tile_kernel, slots, tile, group, shard_o...  10.8 us
    pallas_call x10, Pallas kernels, small_call(): pl.pallas_call(kernel, out_shape=out_shape, in_specs=[VMEM] * len(values)...  4.5 us
    dynamic_slice x1, local copies, waits for them, and re-layouts, local(): lax.dynamic_slice(weight, (col * width, (col ^ k) * width), (width, width))  2.7 us
  transfers between devices with their start and end apart: 40, of which 17 were waited for; matrix products, arithmetic and copies ran while one was open for 3% of the time, Pallas kernels for 2%

profile of v6, /device:TPU:0, one launch (start us, length us, event | category | flops | bytes accessed | tf_op | source)
XLA Modules:
  0.0 130.6 jit_solution(17265248528078713332)
XLA Ops:
  0.6 0.9 slice.9.refs_4_.refs_3_
  1.6 5.1 %collective-permute-start.12 = (bf16[288,256]{1,0:T(8,128)(2,1)S(1)}, bf16[288,256]{1,0:T(8,128)(2,1)S(1)}, u32[]{:S(2)}, u32[]{:S(2)}) collective-permute-start(bf16[288,256]{1,0:T(8,128)(2,1)S(1)} %slice.9.refs_4_.refs_3_), channel_id=1, source_target_pairs={{0,3},{1,2},{2,1},{3,0},{4,7},{5,6},{6,5},{7,4},{8,11},{9,10},{10,... | collective-permute-start | bytes 442376 | tf_op jit(solution)/shard_map/ppermute | solution.py:319
  6.7 0.6 collective-permute-start.10
  7.3 1.0 slice.8.refs_4_.refs_2_
  8.3 3.8 %collective-permute-start.2 = (bf16[288,384]{1,0:T(8,128)(2,1)S(1)}, bf16[288,384]{1,0:T(8,128)(2,1)S(1)}, u32[]{:S(2)}, u32[]{:S(2)}) collective-permute-start(bf16[288,384]{1,0:T(8,128)(2,1)S(1)} %slice.8.refs_4_.refs_2_), channel_id=1, source_target_pairs={{0,3},{1,2},{2,1},{3,0},{4,7},{5,6},{6,5},{7,4},{8,11},{9,10},{10,... | collective-permute-start | bytes 663560 | tf_op jit(solution)/shard_map/ppermute | solution.py:319
  12.1 6.3 %collective-permute-start = (bf16[288,384]{1,0:T(8,128)(2,1)S(1)}, bf16[288,384]{1,0:T(8,128)(2,1)S(1)}, u32[]{:S(2)}, u32[]{:S(2)}) collective-permute-start(bf16[288,384]{1,0:T(8,128)(2,1)S(1)} %slice.8.refs_4_.refs_2_), channel_id=1, source_target_pairs={{0,1},{1,0},{2,3},{3,2},{4,5},{5,4},{6,7},{7,6},{8,9},{9,8},{10,11... | collective-permute-start | bytes 663560 | tf_op jit(solution)/shard_map/ppermute | solution.py:319
  18.4 2.7 %fusion = (bf16[288,288]{1,0:T(8,128)(2,1)S(1)}, bf16[288,288]{1,0:T(8,128)(2,1)S(1)}, bf16[288,288]{1,0:T(8,128)(2,1)S(1)}, bf16[288,288]{1,0:T(8,128)(2,1)S(1)...) fusion(bf16[1152,1152]{1,0:T(8,128)(2,1)} %param.8, s32[]{:T(128)S(6)} %select_n.8, ...), kind=kLoop, calls=%fused_computation | loop fusion | bytes 2322448 | tf_op jit(solution)/shard_map/dynamic_slice | solution.py:347
  21.1 8.5 %collective-permute-done.11.refs_6_.refs_7_ = bf16[288,256]{1,0:T(8,128)(2,1)S(1)} collective-permute-done((bf16[288,256]{1,0:T(8,128)(2,1)S(1)}, bf16[288,256]{1,0:T(8,128)(2,1)S(1)}, u32[]{:S(2)}, u32[]{:S(2)}) %collective-permute-start.11) | collective-permute-done | bytes 147488 | tf_op jit(solution)/shard_map/ppermute | solution.py:319
  29.6 0.5 shard_map.95.rest_8_
  30.2 2.5 %collective-permute-start.15 = (bf16[288,256]{1,0:T(8,128)(2,1)S(1)}, bf16[288,256]{1,0:T(8,128)(2,1)S(1)}, u32[]{:S(2)}, u32[]{:S(2)}) collective-permute-start(bf16[288,256]{1,0:T(8,128)(2,1)S(1)} %shard_map.95.rest_8_), channel_id=1, source_target_pairs={{0,24},{4,28},{8,16},{12,20},{16,8},{20,12},{24,0},{28,4},{1,25},{... | collective-permute-start | bytes 442376 | tf_op jit(solution)/shard_map/ppermute | solution.py:319
  32.7 0.5 collective-permute-start.14
  33.2 4.9 %collective-permute-done.1.refs_6_ = bf16[288,384]{1,0:T(8,128)(2,1)S(1)} collective-permute-done((bf16[288,384]{1,0:T(8,128)(2,1)S(1)}, bf16[288,384]{1,0:T(8,128)(2,1)S(1)}, u32[]{:S(2)}, u32[]{:S(2)}) %collective-permute-start.1) | collective-permute-done | bytes 221216 | tf_op jit(solution)/shard_map/ppermute | solution.py:319
  38.1 1.5 %collective-permute-start.13 = (bf16[288,256]{1,0:T(8,128)(2,1)S(1)}, bf16[288,256]{1,0:T(8,128)(2,1)}, u32[]{:S(2)}, u32[]{:S(2)}) collective-permute-start(bf16[288,256]{1,0:T(8,128)(2,1)S(1)} %shard_map.95.rest_8_), channel_id=1, source_target_pairs={{0,8},{4,12},{8,0},{12,4},{16,24},{20,28},{24,16},{28,20},{1,9},{5... | collective-permute-start | bytes 442376 | tf_op jit(solution)/shard_map/ppermute | solution.py:319
  39.6 0.7 shard_map.94.rest_0_
  40.4 1.6 %collective-permute-start.5 = (bf16[288,384]{1,0:T(8,128)(2,1)S(1)}, bf16[288,384]{1,0:T(8,128)(2,1)S(1)}, u32[]{:S(2)}, u32[]{:S(2)}) collective-permute-start(bf16[288,384]{1,0:T(8,128)(2,1)S(1)} %shard_map.94.rest_0_), channel_id=1, source_target_pairs={{0,24},{4,28},{8,16},{12,20},{16,8},{20,12},{24,0},{28,4},{1,25},{... | collective-permute-start | bytes 663560 | tf_op jit(solution)/shard_map/ppermute | solution.py:319
  42.4 1.5 %collective-permute-start.3 = (bf16[288,384]{1,0:T(8,128)(2,1)S(1)}, bf16[288,384]{1,0:T(8,128)(2,1)}, u32[]{:S(2)}, u32[]{:S(2)}) collective-permute-start(bf16[288,384]{1,0:T(8,128)(2,1)S(1)} %shard_map.94.rest_0_), channel_id=1, source_target_pairs={{0,8},{4,12},{8,0},{12,4},{16,24},{20,28},{24,16},{28,20},{1,9},{5... | collective-permute-start | bytes 663560 | tf_op jit(solution)/shard_map/ppermute | solution.py:319
  44.5 0.9 collective-permute-done.19.rest_15_
  45.5 5.0 %collective-permute-done.5.rest_3_ = bf16[288,384]{1,0:T(8,128)(2,1)S(1)} collective-permute-done((bf16[288,384]{1,0:T(8,128)(2,1)S(1)}, bf16[288,384]{1,0:T(8,128)(2,1)S(1)}, u32[]{:S(2)}, u32[]{:S(2)}) %collective-permute-start.5) | collective-permute-done | bytes 221216 | tf_op jit(solution)/shard_map/ppermute | solution.py:319
  50.4 2.0 %collective-permute-done.4.rest_2_ = bf16[288,384]{1,0:T(8,128)(2,1)S(1)} collective-permute-done((bf16[288,384]{1,0:T(8,128)(2,1)S(1)}, bf16[288,384]{1,0:T(8,128)(2,1)S(1)}, u32[]{:S(2)}, u32[]{:S(2)}) %collective-permute-start.4) | collective-permute-done | bytes 221216 | tf_op jit(solution)/shard_map/ppermute | solution.py:319
  53.0 0.6 copy-done.13
  54.3 1.2 collective-permute-done.17.rest_13_
  55.5 10.8 %shard_map.96 = (bf16[288,640]{1,0:T(8,128)(2,1)}, bf16[288,256]{1,0:T(8,128)(2,1)S(1)}, bf16[3,288,256]{2,1,0:T(8,128)(2,1)S(1)}, bf16[288,256]{1,0:T(8,128)(2,...) custom-call(s32[240]{0:T(256)S(1)} %reshape.16.coords_ref, ...), custom_call_target="tpu_custom_call" | custom-call | flops 4529848320 | bytes 7864320 | tf_op jit(solution)/shard_map/pallas_call | solution.py:155
  66.4 5.3 %collective-permute-start.21 = (bf16[3,288,384]{2,1,0:T(8,128)(2,1)S(1)}, bf16[3,288,384]{2,1,0:T(8,128)(2,1)S(1)}, u32[]{:S(2)}, u32[]{:S(2)}) collective-permute-start(bf16[3,288,384]{2,1,0:T(8,128)(2,1)S(1)} %get-tuple-element.27), channel_id=1, source_target_pairs={{0,4},{4,0},{8,12},{12,8},{16,20},{20,16},{24,28},{28,24},{1,5},{5... | collective-permute-start | bytes 1990664 | tf_op jit(solution)/shard_map/ppermute | solution.py:319
  71.7 2.3 %collective-permute-done.22.got_ref = bf16[3,288,256]{2,1,0:T(8,128)(2,1)S(1)} collective-permute-done((bf16[3,288,256]{2,1,0:T(8,128)(2,1)S(1)}, bf16[3,288,256]{2,1,0:T(8,128)(2,1)S(1)}, u32[]{:S(2)}, u32[]{:S(2)}) %collective-permute-start.22) | collective-permute-done | bytes 442400 | tf_op jit(solution)/shard_map/ppermute | solution.py:319
  74.2 3.9 %collective-permute-start.24 = (bf16[288,256]{1,0:T(8,128)(2,1)S(1)}, bf16[288,256]{1,0:T(8,128)(2,1)S(1)}, u32[]{:S(2)}, u32[]{:S(2)}) collective-permute-start(bf16[288,256]{1,0:T(8,128)(2,1)S(1)} %get-tuple-element.31), channel_id=1, source_target_pairs={{0,16},{4,20},{8,24},{12,28},{16,0},{20,4},{24,8},{28,12},{1,17},{... | collective-permute-start | bytes 442376 | tf_op jit(solution)/shard_map/ppermute | solution.py:319
  78.1 1.4 %collective-permute-start.25 = (bf16[288,256]{1,0:T(8,128)(2,1)S(1)}, bf16[288,256]{1,0:T(8,128)(2,1)S(1)}, u32[]{:S(2)}, u32[]{:S(2)}) collective-permute-start(bf16[288,256]{1,0:T(8,128)(2,1)S(1)} %get-tuple-element.32), channel_id=1, source_target_pairs={{0,24},{4,28},{8,16},{12,20},{16,8},{20,12},{24,0},{28,4},{1,25},{... | collective-permute-start | bytes 442376 | tf_op jit(solution)/shard_map/ppermute | solution.py:319
  79.5 0.8 collective-permute-done.23.refs_0_.refs_2_
  80.3 4.6 %collective-permute-done.24.refs_1_.refs_3_ = bf16[288,256]{1,0:T(8,128)(2,1)S(1)} collective-permute-done((bf16[288,256]{1,0:T(8,128)(2,1)S(1)}, bf16[288,256]{1,0:T(8,128)(2,1)S(1)}, u32[]{:S(2)}, u32[]{:S(2)}) %collective-permute-start.24) | collective-permute-done | bytes 147488 | tf_op jit(solution)/shard_map/ppermute | solution.py:319
  84.9 1.8 %collective-permute-done.25.refs_2_.refs_4_ = bf16[288,256]{1,0:T(8,128)(2,1)S(1)} collective-permute-done((bf16[288,256]{1,0:T(8,128)(2,1)S(1)}, bf16[288,256]{1,0:T(8,128)(2,1)S(1)}, u32[]{:S(2)}, u32[]{:S(2)}) %collective-permute-start.25) | collective-permute-done | bytes 147488 | tf_op jit(solution)/shard_map/ppermute | solution.py:319
  86.9 0.6 collective-permute-start.26
  87.5 1.7 %collective-permute-start.27 = (bf16[288,384]{1,0:T(8,128)(2,1)S(1)}, bf16[288,384]{1,0:T(8,128)(2,1)S(1)}, u32[]{:S(2)}, u32[]{:S(2)}) collective-permute-start(bf16[288,384]{1,0:T(8,128)(2,1)S(1)} %get-tuple-element.34), channel_id=1, source_target_pairs={{0,16},{4,20},{8,24},{12,28},{16,0},{20,4},{24,8},{28,12},{1,17},{... | collective-permute-start | bytes 663560 | tf_op jit(solution)/shard_map/ppermute | solution.py:319
  89.3 1.2 collective-permute-start.28
  90.6 2.5 %collective-permute-start.35 = (bf16[288,256]{1,0:T(8,128)(2,1)S(1)}, bf16[288,256]{1,0:T(8,128)(2,1)S(1)}, u32[]{:S(2)}, u32[]{:S(2)}) collective-permute-start(bf16[288,256]{1,0:T(8,128)(2,1)S(1)} %shard_map.100.refs_4_.refs_0_), channel_id=1, source_target_pairs={{0,3},{1,2},{2,1},{3,0},{4,7},{5,6},{6,5},{7,4},{8,11},{9,10},{10,... | collective-permute-start | bytes 442376 | tf_op jit(solution)/shard_map/ppermute | solution.py:319
  93.1 2.2 %collective-permute-done.26.refs_2_ = bf16[288,384]{1,0:T(8,128)(2,1)S(1)} collective-permute-done((bf16[288,384]{1,0:T(8,128)(2,1)S(1)}, bf16[288,384]{1,0:T(8,128)(2,1)S(1)}, u32[]{:S(2)}, u32[]{:S(2)}) %collective-permute-start.26) | collective-permute-done | bytes 221216 | tf_op jit(solution)/shard_map/ppermute | solution.py:319
  95.3 4.8 %collective-permute-done.27.refs_3_ = bf16[288,384]{1,0:T(8,128)(2,1)S(1)} collective-permute-done((bf16[288,384]{1,0:T(8,128)(2,1)S(1)}, bf16[288,384]{1,0:T(8,128)(2,1)S(1)}, u32[]{:S(2)}, u32[]{:S(2)}) %collective-permute-start.27) | collective-permute-done | bytes 221216 | tf_op jit(solution)/shard_map/ppermute | solution.py:319
  100.3 4.6 %collective-permute-done.34.refs_6_.refs_11_ = bf16[288,256]{1,0:T(8,128)(2,1)S(1)} collective-permute-done((bf16[288,256]{1,0:T(8,128)(2,1)S(1)}, bf16[288,256]{1,0:T(8,128)(2,1)S(1)}, u32[]{:S(2)}, u32[]{:S(2)}) %collective-permute-start.34) | collective-permute-done | bytes 147488 | tf_op jit(solution)/shard_map/ppermute | solution.py:319
  104.9 1.4 %shard_map.102 = (f32[4,144,288]{2,1,0:T(8,128)S(1)}, bf16[4,144,288]{2,1,0:T(8,128)(2,1)S(1)}) custom-call(s32[1]{0:T(128)} %bitcast.4.col_ref, s32[1]{0:T(128)} %bitcast.me_ref, bf16[288,256]{1,0:T(8,128)(2,1)S(1)} %shard_map.100.refs_4_.refs_0_, bf16[288,384]{1,0:T(8,128)(2,1)S(1)} %shard_map.99.refs_1_.refs_4_, ...), custom_call_target="tpu_custom_call" | custom-call | tf_op jit(solution)/shard_map/pallas_call | solution.py:299
  106.4 2.1 %collective-permute-start.31 = (bf16[288,384]{1,0:T(8,128)(2,1)S(1)}, bf16[288,384]{1,0:T(8,128)(2,1)S(1)}, u32[]{:S(2)}, u32[]{:S(2)}) collective-permute-start(bf16[288,384]{1,0:T(8,128)(2,1)S(1)} %shard_map.99.refs_1_.refs_4_), channel_id=1, source_target_pairs={{0,3},{1,2},{2,1},{3,0},{4,7},{5,6},{6,5},{7,4},{8,11},{9,10},{10,... | collective-permute-start | bytes 663560 | tf_op jit(solution)/shard_map/ppermute | solution.py:319
  108.5 2.3 %collective-permute-start.29 = (bf16[288,384]{1,0:T(8,128)(2,1)S(1)}, bf16[288,384]{1,0:T(8,128)(2,1)S(1)}, u32[]{:S(2)}, u32[]{:S(2)}) collective-permute-start(bf16[288,384]{1,0:T(8,128)(2,1)S(1)} %shard_map.99.refs_1_.refs_4_), channel_id=1, source_target_pairs={{0,1},{1,0},{2,3},{3,2},{4,5},{5,4},{6,7},{7,6},{8,9},{9,8},{10,11... | collective-permute-start | bytes 663560 | tf_op jit(solution)/shard_map/ppermute | solution.py:319
  111.0 0.6 collective-permute-start.37
  111.6 1.7 %collective-permute-start.38 = (bf16[144,288]{1,0:T(8,128)(2,1)S(1)}, bf16[144,288]{1,0:T(8,128)(2,1)S(1)}, u32[]{:S(2)}, u32[]{:S(2)}) collective-permute-start(bf16[144,288]{1,0:T(8,128)(2,1)S(1)} %get-tuple-element.41), channel_id=1, source_target_pairs={{0,16},{4,20},{8,24},{12,28},{16,0},{20,4},{24,8},{28,12},{1,17},{... | collective-permute-start | bytes 248840 | tf_op jit(solution)/shard_map/ppermute | solution.py:319
  113.3 2.4 %collective-permute-done.37.refs_2_ = bf16[144,288]{1,0:T(8,128)(2,1)S(1)} collective-permute-done((bf16[144,288]{1,0:T(8,128)(2,1)S(1)}, bf16[144,288]{1,0:T(8,128)(2,1)S(1)}, u32[]{:S(2)}, u32[]{:S(2)}) %collective-permute-start.37) | collective-permute-done | bytes 82976 | tf_op jit(solution)/shard_map/ppermute | solution.py:319
  115.8 1.8 %collective-permute-start.39 = (bf16[144,288]{1,0:T(8,128)(2,1)S(1)}, bf16[144,288]{1,0:T(8,128)(2,1)S(1)}, u32[]{:S(2)}, u32[]{:S(2)}) collective-permute-start(bf16[144,288]{1,0:T(8,128)(2,1)S(1)} %get-tuple-element.42), channel_id=1, source_target_pairs={{0,24},{4,28},{8,16},{12,20},{16,8},{20,12},{24,0},{28,4},{1,25},{... | collective-permute-start | bytes 248840 | tf_op jit(solution)/shard_map/ppermute | solution.py:319
  118.0 3.4 %collective-permute-done.39.refs_4_ = bf16[144,288]{1,0:T(8,128)(2,1)S(1)} collective-permute-done((bf16[144,288]{1,0:T(8,128)(2,1)S(1)}, bf16[144,288]{1,0:T(8,128)(2,1)S(1)}, u32[]{:S(2)}, u32[]{:S(2)}) %collective-permute-start.39) | collective-permute-done | bytes 82976 | tf_op jit(solution)/shard_map/ppermute | solution.py:319
  121.4 0.8 shard_map.104.refs_9_
  122.2 6.0 %collective-permute-done.30.refs_6_ = bf16[288,384]{1,0:T(8,128)(2,1)S(1)} collective-permute-done((bf16[288,384]{1,0:T(8,128)(2,1)S(1)}, bf16[288,384]{1,0:T(8,128)(2,1)S(1)}, u32[]{:S(2)}, u32[]{:S(2)}) %collective-permute-start.30) | collective-permute-done | bytes 221216 | tf_op jit(solution)/shard_map/ppermute | solution.py:319
  128.2 0.9 copy-done
  129.2 1.4 %shard_map.105 = bf16[288,640]{1,0:T(8,128)(2,1)} custom-call(bf16[288,288]{1,0:T(8,128)(2,1)S(1)} %get-tuple-element.48.refs_0_, bf16[288,288]{1,0:T(8,128)(2,1)S(1)} %get-tuple-element.44.refs_1_, bf16[288,288]{1,0:T(8,128)(2,1)S(1)} %get-tuple-element.49.refs_2_, bf16[288,288]{1,0:T(8,128)(2,1)S(1)} %get-tuple-element.43.refs_3_, ...), custom_call_target="tpu_custom_call" | custom-call | tf_op jit(solution)/shard_map/pallas_call | solution.py:196
  (77 shorter events, 3.8 us)
Async XLA Ops:
  1.6 10.5 %collective-permute-start.12 = (bf16[288,256]{1,0:T(8,128)(2,1)S(1)}, bf16[288,256]{1,0:T(8,128)(2,1)S(1)}, u32[]{:S(2)}, u32[]{:S(2)}) collective-permute-start(bf16[288,256]{1,0:T(8,128)(2,1)S(1)} %slice.9.refs_4_.refs_3_), channel_id=1, source_target_pairs={{0,3},{1,2},{2,1},{3,0},{4,7},{5,6},{6,5},{7,4},{8,11},{9,10},{10,... | collective-permute-start | bytes 442376 | tf_op jit(solution)/shard_map/ppermute | solution.py:319
  6.7 22.9 %collective-permute-start.11 = (bf16[288,256]{1,0:T(8,128)(2,1)S(1)}, bf16[288,256]{1,0:T(8,128)(2,1)S(1)}, u32[]{:S(2)}, u32[]{:S(2)}) collective-permute-start(bf16[288,256]{1,0:T(8,128)(2,1)S(1)} %slice.9.refs_4_.refs_3_), channel_id=1, source_target_pairs={{0,2},{1,3},{2,0},{3,1},{4,6},{5,7},{6,4},{7,5},{8,10},{9,11},{10,... | collective-permute-start | bytes 442376 | tf_op jit(solution)/shard_map/ppermute | solution.py:319
  6.7 22.9 %collective-permute-start.10 = (bf16[288,256]{1,0:T(8,128)(2,1)S(1)}, bf16[288,256]{1,0:T(8,128)(2,1)S(1)}, u32[]{:S(2)}, u32[]{:S(2)}) collective-permute-start(bf16[288,256]{1,0:T(8,128)(2,1)S(1)} %slice.9.refs_4_.refs_3_), channel_id=1, source_target_pairs={{0,1},{1,0},{2,3},{3,2},{4,5},{5,4},{6,7},{7,6},{8,9},{9,8},{10,11... | collective-permute-start | bytes 442376 | tf_op jit(solution)/shard_map/ppermute | solution.py:319
  8.3 24.5 %collective-permute-start.2 = (bf16[288,384]{1,0:T(8,128)(2,1)S(1)}, bf16[288,384]{1,0:T(8,128)(2,1)S(1)}, u32[]{:S(2)}, u32[]{:S(2)}) collective-permute-start(bf16[288,384]{1,0:T(8,128)(2,1)S(1)} %slice.8.refs_4_.refs_2_), channel_id=1, source_target_pairs={{0,3},{1,2},{2,1},{3,0},{4,7},{5,6},{6,5},{7,4},{8,11},{9,10},{10,... | collective-permute-start | bytes 663560 | tf_op jit(solution)/shard_map/ppermute | solution.py:319
  12.1 26.0 %collective-permute-start.1 = (bf16[288,384]{1,0:T(8,128)(2,1)S(1)}, bf16[288,384]{1,0:T(8,128)(2,1)S(1)}, u32[]{:S(2)}, u32[]{:S(2)}) collective-permute-start(bf16[288,384]{1,0:T(8,128)(2,1)S(1)} %slice.8.refs_4_.refs_2_), channel_id=1, source_target_pairs={{0,2},{1,3},{2,0},{3,1},{4,6},{5,7},{6,4},{7,5},{8,10},{9,11},{10,... | collective-permute-start | bytes 663560 | tf_op jit(solution)/shard_map/ppermute | solution.py:319
  12.1 42.0 %copy-start.5 = (s32[5,48]{1,0:T(8,128)S(1)}, s32[5,48]{1,0:T(8,128)}, u32[]{:S(2)}) copy-start(s32[5,48]{1,0:T(8,128)} %param.11) | copy-start | bytes 2884
  12.1 42.1 %copy-start.6 = (f32[288]{0:T(512)S(1)}, f32[288]{0:T(512)}, u32[]{:S(2)}) copy-start(f32[288]{0:T(512)} %param.9) | copy-start | bytes 3460
  12.1 27.5 %collective-permute-start = (bf16[288,384]{1,0:T(8,128)(2,1)S(1)}, bf16[288,384]{1,0:T(8,128)(2,1)S(1)}, u32[]{:S(2)}, u32[]{:S(2)}) collective-permute-start(bf16[288,384]{1,0:T(8,128)(2,1)S(1)} %slice.8.refs_4_.refs_2_), channel_id=1, source_target_pairs={{0,1},{1,0},{2,3},{3,2},{4,5},{5,4},{6,7},{7,6},{8,9},{9,8},{10,11... | collective-permute-start | bytes 663560 | tf_op jit(solution)/shard_map/ppermute | solution.py:319
  21.1 34.4 %copy-start.3 = (bf16[640,288]{0,1:T(8,128)(2,1)S(1)}, bf16[640,288]{0,1:T(8,128)(2,1)}, u32[]{:S(2)}) copy-start(bf16[640,288]{0,1:T(8,128)(2,1)} %param.13) | copy-start | bytes 1105924
  21.1 34.4 %copy-start.4 = (s32[5]{0:T(128)S(1)}, s32[5]{0:T(128)}, u32[]{:S(2)}) copy-start(s32[5]{0:T(128)} %counts_ref.1) | copy-start | bytes 64
  30.1 25.3 %copy-start.2 = (bf16[288,256]{1,0:T(8,128)(2,1)}, bf16[288,256]{1,0:T(8,128)(2,1)S(1)}, u32[]{:S(2)}) copy-start(bf16[288,256]{1,0:T(8,128)(2,1)S(1)} %shard_map.95.rest_8_) | copy-start | bytes 442372
  30.1 11.8 %collective-permute-start.16 = (bf16[288,256]{1,0:T(8,128)(2,1)S(1)}, bf16[288,256]{1,0:T(8,128)(2,1)S(1)}, u32[]{:S(2)}, u32[]{:S(2)}) collective-permute-start(bf16[288,256]{1,0:T(8,128)(2,1)S(1)} %shard_map.95.rest_8_), channel_id=1, source_target_pairs={{0,4},{4,0},{8,12},{12,8},{16,20},{20,16},{24,28},{28,24},{1,5},{5... | collective-permute-start | bytes 442376 | tf_op jit(solution)/shard_map/ppermute | solution.py:319
  30.2 12.2 %collective-permute-start.15 = (bf16[288,256]{1,0:T(8,128)(2,1)S(1)}, bf16[288,256]{1,0:T(8,128)(2,1)S(1)}, u32[]{:S(2)}, u32[]{:S(2)}) collective-permute-start(bf16[288,256]{1,0:T(8,128)(2,1)S(1)} %shard_map.95.rest_8_), channel_id=1, source_target_pairs={{0,24},{4,28},{8,16},{12,20},{16,8},{20,12},{24,0},{28,4},{1,25},{... | collective-permute-start | bytes 442376 | tf_op jit(solution)/shard_map/ppermute | solution.py:319
  32.7 11.2 %collective-permute-start.14 = (bf16[288,256]{1,0:T(8,128)(2,1)S(1)}, bf16[288,256]{1,0:T(8,128)(2,1)S(1)}, u32[]{:S(2)}, u32[]{:S(2)}) collective-permute-start(bf16[288,256]{1,0:T(8,128)(2,1)S(1)} %shard_map.95.rest_8_), channel_id=1, source_target_pairs={{0,16},{4,20},{8,24},{12,28},{16,0},{20,4},{24,8},{28,12},{1,17},{... | collective-permute-start | bytes 442376 | tf_op jit(solution)/shard_map/ppermute | solution.py:319
  38.1 5.8 %collective-permute-start.13 = (bf16[288,256]{1,0:T(8,128)(2,1)S(1)}, bf16[288,256]{1,0:T(8,128)(2,1)}, u32[]{:S(2)}, u32[]{:S(2)}) collective-permute-start(bf16[288,256]{1,0:T(8,128)(2,1)S(1)} %shard_map.95.rest_8_), channel_id=1, source_target_pairs={{0,8},{4,12},{8,0},{12,4},{16,24},{20,28},{24,16},{28,20},{1,9},{5... | collective-permute-start | bytes 442376 | tf_op jit(solution)/shard_map/ppermute | solution.py:319
  40.4 15.1 %copy-start.1 = (bf16[288,384]{1,0:T(8,128)(2,1)}, bf16[288,384]{1,0:T(8,128)(2,1)S(1)}, u32[]{:S(2)}) copy-start(bf16[288,384]{1,0:T(8,128)(2,1)S(1)} %shard_map.94.rest_0_) | copy-start | bytes 663556
  40.4 10.0 %collective-permute-start.5 = (bf16[288,384]{1,0:T(8,128)(2,1)S(1)}, bf16[288,384]{1,0:T(8,128)(2,1)S(1)}, u32[]{:S(2)}, u32[]{:S(2)}) collective-permute-start(bf16[288,384]{1,0:T(8,128)(2,1)S(1)} %shard_map.94.rest_0_), channel_id=1, source_target_pairs={{0,24},{4,28},{8,16},{12,20},{16,8},{20,12},{24,0},{28,4},{1,25},{... | collective-permute-start | bytes 663560 | tf_op jit(solution)/shard_map/ppermute | solution.py:319
  41.9 11.0 %copy-start.9 = (bf16[288,256]{1,0:T(8,128)(2,1)}, bf16[288,256]{1,0:T(8,128)(2,1)S(1)}, u32[]{:S(2)}) copy-start(bf16[288,256]{1,0:T(8,128)(2,1)S(1)} %collective-permute-done.16.rest_12_) | copy-start | bytes 442372
  41.9 10.5 %collective-permute-start.4 = (bf16[288,384]{1,0:T(8,128)(2,1)S(1)}, bf16[288,384]{1,0:T(8,128)(2,1)S(1)}, u32[]{:S(2)}, u32[]{:S(2)}) collective-permute-start(bf16[288,384]{1,0:T(8,128)(2,1)S(1)} %shard_map.94.rest_0_), channel_id=1, source_target_pairs={{0,16},{4,20},{8,24},{12,28},{16,0},{20,4},{24,8},{28,12},{1,17},{... | collective-permute-start | bytes 663560 | tf_op jit(solution)/shard_map/ppermute | solution.py:319
  42.4 10.5 %copy-start.10 = (bf16[288,256]{1,0:T(8,128)(2,1)}, bf16[288,256]{1,0:T(8,128)(2,1)S(1)}, u32[]{:S(2)}) copy-start(bf16[288,256]{1,0:T(8,128)(2,1)S(1)} %collective-permute-done.15.rest_11_) | copy-start | bytes 442372
  42.4 10.4 %collective-permute-start.3 = (bf16[288,384]{1,0:T(8,128)(2,1)S(1)}, bf16[288,384]{1,0:T(8,128)(2,1)}, u32[]{:S(2)}, u32[]{:S(2)}) collective-permute-start(bf16[288,384]{1,0:T(8,128)(2,1)S(1)} %shard_map.94.rest_0_), channel_id=1, source_target_pairs={{0,8},{4,12},{8,0},{12,4},{16,24},{20,28},{24,16},{28,20},{1,9},{5... | collective-permute-start | bytes 663560 | tf_op jit(solution)/shard_map/ppermute | solution.py:319
  43.9 1.4 %collective-permute-start.19 = (bf16[288,256]{1,0:T(8,128)(2,1)S(1)}, bf16[288,256]{1,0:T(8,128)(2,1)S(1)}, u32[]{:S(2)}, u32[]{:S(2)}) collective-permute-start(bf16[288,256]{1,0:T(8,128)(2,1)S(1)} %collective-permute-done.15.rest_11_), channel_id=1, source_target_pairs={{0,4},{4,0},{8,12},{12,8},{16,20},{20,16},{24,28},{28,24},{1,5},{5... | collective-permute-start | bytes 442376 | tf_op jit(solution)/shard_map/ppermute | solution.py:319
  44.0 9.0 %collective-permute-start.18 = (bf16[288,256]{1,0:T(8,128)(2,1)S(1)}, bf16[288,256]{1,0:T(8,128)(2,1)S(1)}, u32[]{:S(2)}, u32[]{:S(2)}) collective-permute-start(bf16[288,256]{1,0:T(8,128)(2,1)S(1)} %collective-permute-done.14.rest_10_), channel_id=1, source_target_pairs={{0,4},{4,0},{8,12},{12,8},{16,20},{20,16},{24,28},{28,24},{1,5},{5... | collective-permute-start | bytes 442376 | tf_op jit(solution)/shard_map/ppermute | solution.py:319
  45.3 10.1 %collective-permute-start.6 = (bf16[288,384]{1,0:T(8,128)(2,1)S(1)}, bf16[288,384]{1,0:T(8,128)(2,1)}, u32[]{:S(2)}, u32[]{:S(2)}) collective-permute-start(bf16[288,384]{1,0:T(8,128)(2,1)S(1)} %shard_map.94.rest_0_), channel_id=1, source_target_pairs={{0,4},{4,0},{8,12},{12,8},{16,20},{20,16},{24,28},{28,24},{1,5},{5... | collective-permute-start | bytes 663560 | tf_op jit(solution)/shard_map/ppermute | solution.py:319
  50.4 5.0 %collective-permute-start.9 = (bf16[288,384]{1,0:T(8,128)(2,1)S(1)}, bf16[288,384]{1,0:T(8,128)(2,1)}, u32[]{:S(2)}, u32[]{:S(2)}) collective-permute-start(bf16[288,384]{1,0:T(8,128)(2,1)S(1)} %collective-permute-done.5.rest_3_), channel_id=1, source_target_pairs={{0,4},{4,0},{8,12},{12,8},{16,20},{20,16},{24,28},{28,24},{1,5},{5... | collective-permute-start | bytes 663560 | tf_op jit(solution)/shard_map/ppermute | solution.py:319
  52.4 3.0 %collective-permute-start.8 = (bf16[288,384]{1,0:T(8,128)(2,1)S(1)}, bf16[288,384]{1,0:T(8,128)(2,1)}, u32[]{:S(2)}, u32[]{:S(2)}) collective-permute-start(bf16[288,384]{1,0:T(8,128)(2,1)S(1)} %collective-permute-done.4.rest_2_), channel_id=1, source_target_pairs={{0,4},{4,0},{8,12},{12,8},{16,20},{20,16},{24,28},{28,24},{1,5},{5... | collective-permute-start | bytes 663560 | tf_op jit(solution)/shard_map/ppermute | solution.py:319
  52.9 2.5 %collective-permute-start.7 = (bf16[288,384]{1,0:T(8,128)(2,1)}, bf16[288,384]{1,0:T(8,128)(2,1)}, u32[]{:S(2)}, u32[]{:S(2)}) collective-permute-start(bf16[288,384]{1,0:T(8,128)(2,1)} %collective-permute-done.3.rest_1_), channel_id=1, source_target_pairs={{0,4},{4,0},{8,12},{12,8},{16,20},{20,16},{24,28},{28,24},{1,5},{5... | collective-permute-start | bytes 663560 | tf_op jit(solution)/shard_map/ppermute | solution.py:319
  53.6 1.8 %collective-permute-start.17 = (bf16[288,256]{1,0:T(8,128)(2,1)}, bf16[288,256]{1,0:T(8,128)(2,1)}, u32[]{:S(2)}, u32[]{:S(2)}) collective-permute-start(bf16[288,256]{1,0:T(8,128)(2,1)} %collective-permute-done.13.rest_9_), channel_id=1, source_target_pairs={{0,4},{4,0},{8,12},{12,8},{16,20},{20,16},{24,28},{28,24},{1,5},{5... | collective-permute-start | bytes 442376 | tf_op jit(solution)/shard_map/ppermute | solution.py:319
  66.4 20.4 %collective-permute-start.21 = (bf16[3,288,384]{2,1,0:T(8,128)(2,1)S(1)}, bf16[3,288,384]{2,1,0:T(8,128)(2,1)S(1)}, u32[]{:S(2)}, u32[]{:S(2)}) collective-permute-start(bf16[3,288,384]{2,1,0:T(8,128)(2,1)S(1)} %get-tuple-element.27), channel_id=1, source_target_pairs={{0,4},{4,0},{8,12},{12,8},{16,20},{20,16},{24,28},{28,24},{1,5},{5... | collective-permute-start | bytes 1990664 | tf_op jit(solution)/shard_map/ppermute | solution.py:319
  71.6 2.4 %collective-permute-start.22 = (bf16[3,288,256]{2,1,0:T(8,128)(2,1)S(1)}, bf16[3,288,256]{2,1,0:T(8,128)(2,1)S(1)}, u32[]{:S(2)}, u32[]{:S(2)}) collective-permute-start(bf16[3,288,256]{2,1,0:T(8,128)(2,1)S(1)} %get-tuple-element.29), channel_id=1, source_target_pairs={{0,4},{4,0},{8,12},{12,8},{16,20},{20,16},{24,28},{28,24},{1,5},{5... | collective-permute-start | bytes 1327112 | tf_op jit(solution)/shard_map/ppermute | solution.py:319
  74.1 6.2 %collective-permute-start.23 = (bf16[288,256]{1,0:T(8,128)(2,1)S(1)}, bf16[288,256]{1,0:T(8,128)(2,1)S(1)}, u32[]{:S(2)}, u32[]{:S(2)}) collective-permute-start(bf16[288,256]{1,0:T(8,128)(2,1)S(1)} %get-tuple-element.30), channel_id=1, source_target_pairs={{0,8},{4,12},{8,0},{12,4},{16,24},{20,28},{24,16},{28,20},{1,9},{5... | collective-permute-start | bytes 442376 | tf_op jit(solution)/shard_map/ppermute | solution.py:319
  74.2 10.7 %collective-permute-start.24 = (bf16[288,256]{1,0:T(8,128)(2,1)S(1)}, bf16[288,256]{1,0:T(8,128)(2,1)S(1)}, u32[]{:S(2)}, u32[]{:S(2)}) collective-permute-start(bf16[288,256]{1,0:T(8,128)(2,1)S(1)} %get-tuple-element.31), channel_id=1, source_target_pairs={{0,16},{4,20},{8,24},{12,28},{16,0},{20,4},{24,8},{28,12},{1,17},{... | collective-permute-start | bytes 442376 | tf_op jit(solution)/shard_map/ppermute | solution.py:319
  78.1 8.6 %collective-permute-start.25 = (bf16[288,256]{1,0:T(8,128)(2,1)S(1)}, bf16[288,256]{1,0:T(8,128)(2,1)S(1)}, u32[]{:S(2)}, u32[]{:S(2)}) collective-permute-start(bf16[288,256]{1,0:T(8,128)(2,1)S(1)} %get-tuple-element.32), channel_id=1, source_target_pairs={{0,24},{4,28},{8,16},{12,20},{16,8},{20,12},{24,0},{28,4},{1,25},{... | collective-permute-start | bytes 442376 | tf_op jit(solution)/shard_map/ppermute | solution.py:319
  79.5 13.6 %collective-permute-start.20 = (bf16[288,384]{1,0:T(8,128)(2,1)S(1)}, bf16[288,384]{1,0:T(8,128)(2,1)S(1)}, u32[]{:S(2)}, u32[]{:S(2)}) collective-permute-start(bf16[288,384]{1,0:T(8,128)(2,1)S(1)} %get-tuple-element.25), channel_id=1, source_target_pairs={{0,4},{4,0},{8,12},{12,8},{16,20},{20,16},{24,28},{28,24},{1,5},{5... | collective-permute-start | bytes 663560 | tf_op jit(solution)/shard_map/ppermute | solution.py:319
  86.9 8.4 %collective-permute-start.26 = (bf16[288,384]{1,0:T(8,128)(2,1)S(1)}, bf16[288,384]{1,0:T(8,128)(2,1)S(1)}, u32[]{:S(2)}, u32[]{:S(2)}) collective-permute-start(bf16[288,384]{1,0:T(8,128)(2,1)S(1)} %get-tuple-element.33), channel_id=1, source_target_pairs={{0,8},{4,12},{8,0},{12,4},{16,24},{20,28},{24,16},{28,20},{1,9},{5... | collective-permute-start | bytes 663560 | tf_op jit(solution)/shard_map/ppermute | solution.py:319
  87.5 2.9 %collective-permute-start.32 = (bf16[288,256]{1,0:T(8,128)(2,1)S(1)}, bf16[288,256]{1,0:T(8,128)(2,1)S(1)}, u32[]{:S(2)}, u32[]{:S(2)}) collective-permute-start(bf16[288,256]{1,0:T(8,128)(2,1)S(1)} %get-tuple-element.37), channel_id=1, source_target_pairs={{0,4},{4,0},{8,12},{12,8},{16,20},{20,16},{24,28},{28,24},{1,5},{5... | collective-permute-start | bytes 442376 | tf_op jit(solution)/shard_map/ppermute | solution.py:319
  87.5 12.6 %collective-permute-start.27 = (bf16[288,384]{1,0:T(8,128)(2,1)S(1)}, bf16[288,384]{1,0:T(8,128)(2,1)S(1)}, u32[]{:S(2)}, u32[]{:S(2)}) collective-permute-start(bf16[288,384]{1,0:T(8,128)(2,1)S(1)} %get-tuple-element.34), channel_id=1, source_target_pairs={{0,16},{4,20},{8,24},{12,28},{16,0},{20,4},{24,8},{28,12},{1,17},{... | collective-permute-start | bytes 663560 | tf_op jit(solution)/shard_map/ppermute | solution.py:319
  89.3 10.8 %collective-permute-start.28 = (bf16[288,384]{1,0:T(8,128)(2,1)S(1)}, bf16[288,384]{1,0:T(8,128)(2,1)S(1)}, u32[]{:S(2)}, u32[]{:S(2)}) collective-permute-start(bf16[288,384]{1,0:T(8,128)(2,1)S(1)} %get-tuple-element.35), channel_id=1, source_target_pairs={{0,24},{4,28},{8,16},{12,20},{16,8},{20,12},{24,0},{28,4},{1,25},{... | collective-permute-start | bytes 663560 | tf_op jit(solution)/shard_map/ppermute | solution.py:319
  90.6 9.7 %collective-permute-start.35 = (bf16[288,256]{1,0:T(8,128)(2,1)S(1)}, bf16[288,256]{1,0:T(8,128)(2,1)S(1)}, u32[]{:S(2)}, u32[]{:S(2)}) collective-permute-start(bf16[288,256]{1,0:T(8,128)(2,1)S(1)} %shard_map.100.refs_4_.refs_0_), channel_id=1, source_target_pairs={{0,3},{1,2},{2,1},{3,0},{4,7},{5,6},{6,5},{7,4},{8,11},{9,10},{10,... | collective-permute-start | bytes 442376 | tf_op jit(solution)/shard_map/ppermute | solution.py:319
  93.1 11.8 %collective-permute-start.34 = (bf16[288,256]{1,0:T(8,128)(2,1)S(1)}, bf16[288,256]{1,0:T(8,128)(2,1)S(1)}, u32[]{:S(2)}, u32[]{:S(2)}) collective-permute-start(bf16[288,256]{1,0:T(8,128)(2,1)S(1)} %shard_map.100.refs_4_.refs_0_), channel_id=1, source_target_pairs={{0,2},{1,3},{2,0},{3,1},{4,6},{5,7},{6,4},{7,5},{8,10},{9,11},{10,... | collective-permute-start | bytes 442376 | tf_op jit(solution)/shard_map/ppermute | solution.py:319
  95.3 9.6 %collective-permute-start.33 = (bf16[288,256]{1,0:T(8,128)(2,1)S(1)}, bf16[288,256]{1,0:T(8,128)(2,1)S(1)}, u32[]{:S(2)}, u32[]{:S(2)}) collective-permute-start(bf16[288,256]{1,0:T(8,128)(2,1)S(1)} %shard_map.100.refs_4_.refs_0_), channel_id=1, source_target_pairs={{0,1},{1,0},{2,3},{3,2},{4,5},{5,4},{6,7},{7,6},{8,9},{9,8},{10,11... | collective-permute-start | bytes 442376 | tf_op jit(solution)/shard_map/ppermute | solution.py:319
  106.3 4.5 %collective-permute-start.36 = (bf16[4,144,288]{2,1,0:T(8,128)(2,1)S(1)}, bf16[4,144,288]{2,1,0:T(8,128)(2,1)S(1)}, u32[]{:S(2)}, u32[]{:S(2)}) collective-permute-start(bf16[4,144,288]{2,1,0:T(8,128)(2,1)S(1)} %get-tuple-element.39), channel_id=1, source_target_pairs={{0,4},{4,0},{8,12},{12,8},{16,20},{20,16},{24,28},{28,24},{1,5},{5... | collective-permute-start | bytes 995336 | tf_op jit(solution)/shard_map/ppermute | solution.py:319
  106.4 15.8 %collective-permute-start.31 = (bf16[288,384]{1,0:T(8,128)(2,1)S(1)}, bf16[288,384]{1,0:T(8,128)(2,1)S(1)}, u32[]{:S(2)}, u32[]{:S(2)}) collective-permute-start(bf16[288,384]{1,0:T(8,128)(2,1)S(1)} %shard_map.99.refs_1_.refs_4_), channel_id=1, source_target_pairs={{0,3},{1,2},{2,1},{3,0},{4,7},{5,6},{6,5},{7,4},{8,11},{9,10},{10,... | collective-permute-start | bytes 663560 | tf_op jit(solution)/shard_map/ppermute | solution.py:319
  108.5 19.7 %collective-permute-start.30 = (bf16[288,384]{1,0:T(8,128)(2,1)S(1)}, bf16[288,384]{1,0:T(8,128)(2,1)S(1)}, u32[]{:S(2)}, u32[]{:S(2)}) collective-permute-start(bf16[288,384]{1,0:T(8,128)(2,1)S(1)} %shard_map.99.refs_1_.refs_4_), channel_id=1, source_target_pairs={{0,2},{1,3},{2,0},{3,1},{4,6},{5,7},{6,4},{7,5},{8,10},{9,11},{10,... | collective-permute-start | bytes 663560 | tf_op jit(solution)/shard_map/ppermute | solution.py:319
  108.5 19.7 %collective-permute-start.29 = (bf16[288,384]{1,0:T(8,128)(2,1)S(1)}, bf16[288,384]{1,0:T(8,128)(2,1)S(1)}, u32[]{:S(2)}, u32[]{:S(2)}) collective-permute-start(bf16[288,384]{1,0:T(8,128)(2,1)S(1)} %shard_map.99.refs_1_.refs_4_), channel_id=1, source_target_pairs={{0,1},{1,0},{2,3},{3,2},{4,5},{5,4},{6,7},{7,6},{8,9},{9,8},{10,11... | collective-permute-start | bytes 663560 | tf_op jit(solution)/shard_map/ppermute | solution.py:319
  111.0 4.8 %collective-permute-start.37 = (bf16[144,288]{1,0:T(8,128)(2,1)S(1)}, bf16[144,288]{1,0:T(8,128)(2,1)S(1)}, u32[]{:S(2)}, u32[]{:S(2)}) collective-permute-start(bf16[144,288]{1,0:T(8,128)(2,1)S(1)} %get-tuple-element.40), channel_id=1, source_target_pairs={{0,8},{4,12},{8,0},{12,4},{16,24},{20,28},{24,16},{28,20},{1,9},{5... | collective-permute-start | bytes 248840 | tf_op jit(solution)/shard_map/ppermute | solution.py:319
  111.6 6.4 %collective-permute-start.38 = (bf16[144,288]{1,0:T(8,128)(2,1)S(1)}, bf16[144,288]{1,0:T(8,128)(2,1)S(1)}, u32[]{:S(2)}, u32[]{:S(2)}) collective-permute-start(bf16[144,288]{1,0:T(8,128)(2,1)S(1)} %get-tuple-element.41), channel_id=1, source_target_pairs={{0,16},{4,20},{8,24},{12,28},{16,0},{20,4},{24,8},{28,12},{1,17},{... | collective-permute-start | bytes 248840 | tf_op jit(solution)/shard_map/ppermute | solution.py:319
  115.8 5.6 %collective-permute-start.39 = (bf16[144,288]{1,0:T(8,128)(2,1)S(1)}, bf16[144,288]{1,0:T(8,128)(2,1)S(1)}, u32[]{:S(2)}, u32[]{:S(2)}) collective-permute-start(bf16[144,288]{1,0:T(8,128)(2,1)S(1)} %get-tuple-element.42), channel_id=1, source_target_pairs={{0,24},{4,28},{8,16},{12,20},{16,8},{20,12},{24,0},{28,4},{1,25},{... | collective-permute-start | bytes 248840 | tf_op jit(solution)/shard_map/ppermute | solution.py:319
  (6 other events, 26.4 us)
